TPU v7x, 32 devices: a whole 2x2x4 slice. The times are simulated.
32 devices in a mesh: grp: 4 (over x, core), blk: 8 (over z, y).
Axes of the slice: x: 2, y: 2, z: 4, core: 2. Of those that a mesh axis runs over, the one named last changes fastest.
Arguments:
- amplitudes: bfloat16 [64, 8, 256, 256], P('grp', None, 'blk'), may hold values from -6 to 6
- chol_vv: bfloat16 [4, 8, 256, 256], P('grp'), may hold values from -0.375 to 0.375
- chol_irrep: int32 [4], replicated, may hold values from 0 to 7
- pair_occ: int32 [64, 2], replicated, may hold values from 0 to 239
- occ_irrep: int32 [240], replicated, may hold values from 0 to 7
- vir_count: int32 [8], replicated, may hold values from 128 to 256, as said below
- ov_left: bfloat16 [4096, 8, 256], P(('grp', 'blk')), may hold values from -1.5 to 1.5
- ov_right: bfloat16 [4096, 8, 256], P(('grp', 'blk')), may hold values from -1.5 to 1.5
Outputs:
- residual: bfloat16 [64, 8, 256, 256], P('grp', None, 'blk')
Inputs may be any that keep to these rules, and one draw needn't show every extreme that they name: `vir_count`: one irrep block is full in every draw; slots of a block beyond its count are padding.
All inputs are finite; a program needn't handle non-finite values.
Results may differ from a plain program's by a relative error of at most 0.0049.
Values may be sent and summed in bfloat16 or wider, within the bound.
No kernel may reach another device: no remote copies, remote signals or barrier semaphores. Data moves between devices by JAX's collectives and lax.ppermute only.
A program may use at most 192 MiB of HBM per device.

v0:
```python
import math

import jax
import jax.numpy as jnp
from jax import lax
from jax.sharding import PartitionSpec as P

IRREPS = 8


def slab_terms(masked, col_index, slot_mask, slab_tile, slab_irrep):
    irrep_ids = jnp.arange(IRREPS, dtype=jnp.int32)
    block_perm = jnp.bitwise_xor(irrep_ids, slab_irrep)
    left_tile = slab_tile * (slot_mask[:, :, None] * slot_mask[block_perm][:, None, :]).astype(
        jnp.bfloat16
    )
    shifted = masked[:, block_perm]
    half_product = jnp.einsum(
        "hac,phcd->phad", left_tile, shifted, preferred_element_type=jnp.float32
    ).astype(jnp.bfloat16)
    right_tile = left_tile[col_index]
    return jnp.einsum(
        "phad,phbd->phab", half_product, right_tile, preferred_element_type=jnp.float32
    )


def per_device(amplitudes, chol_vv, chol_irrep, pair_occ, occ_irrep, vir_count, ov_left, ov_right):
    blk_count = lax.axis_size("blk")
    grp_count = lax.axis_size("grp")
    slot_total = amplitudes.shape[3]
    irrep_ids = jnp.arange(IRREPS, dtype=jnp.int32)
    slot_mask = (
        lax.broadcasted_iota(jnp.int32, (IRREPS, slot_total), 1) < vir_count[:, None]
    ).astype(jnp.float32)
    local_sum = jnp.einsum("rhs,rht->hst", ov_left, ov_right, preferred_element_type=jnp.float32)
    scale_factor = 1.0 / math.sqrt(ov_left.shape[0] * grp_count * blk_count)
    coupling = lax.psum(local_sum, ("grp", "blk"))
    coupling_bf = (coupling * scale_factor).astype(jnp.bfloat16)
    pair_tiles = lax.all_to_all(amplitudes, "blk", split_axis=0, concat_axis=2, tiled=True)
    per_dev = pair_tiles.shape[0]
    pair_start = (lax.axis_index("grp") * blk_count + lax.axis_index("blk")) * per_dev
    own_pairs = lax.dynamic_slice_in_dim(pair_occ, pair_start, per_dev, 0)
    occ_ids = jnp.arange(occ_irrep.shape[0], dtype=jnp.int32)
    one_hot = own_pairs[:, :, None] == occ_ids[None, None, :]
    pair_labels = jnp.sum(jnp.where(one_hot, occ_irrep[None, None, :], 0), axis=2)
    pair_irrep = jnp.bitwise_xor(pair_labels[:, 0], pair_labels[:, 1])
    col_index = jnp.bitwise_xor(irrep_ids[None, :], pair_irrep[:, None])
    col_mask = slot_mask[col_index]
    masked = pair_tiles * (slot_mask[None, :, :, None] * col_mask[:, :, None, :]).astype(
        jnp.bfloat16
    )
    empty = jnp.zeros(pair_tiles.shape, jnp.float32)
    gathered = lax.all_gather(chol_vv, "grp", axis=0, tiled=True)

    def add_vector(q, running):
        return running + slab_terms(masked, col_index, slot_mask, gathered[q], chol_irrep[q])

    ladder = lax.fori_loop(0, gathered.shape[0], add_vector, empty)
    dress_one = jnp.einsum(
        "phac,phcb->phab", masked, coupling_bf[col_index], preferred_element_type=jnp.float32
    )
    dress_two = jnp.einsum(
        "hac,phcb->phab", coupling_bf, masked, preferred_element_type=jnp.float32
    )
    out_mask = slot_mask[None, :, :, None] * col_mask[:, :, None, :]
    result = (out_mask * (ladder + dress_one + dress_two)).astype(jnp.bfloat16)
    return lax.all_to_all(result, "blk", split_axis=2, concat_axis=0, tiled=True)


def solution(mesh):
    return jax.shard_map(
        per_device,
        mesh=mesh,
        in_specs=(
            P("grp", None, "blk", None),
            P("grp", None, None, None),
            P(),
            P(),
            P(),
            P(),
            P(("grp", "blk"), None, None),
            P(("grp", "blk"), None, None),
        ),
        out_specs=P("grp", None, "blk", None),
        check_vma=False,
    )
```

profile of v0, /device:TPU:0, one launch (start us, length us, event | category | flops | bytes accessed | tf_op | source)
XLA Modules:
  0.0 320.8 jit_solution(5942828362039518568)
XLA Ops:
  8.4 2.8 fusion.20
  11.9 7.4 %all-to-all-start = ((bf16[16,8,32,256]{3,2,1,0:T(8,128)(2,1)}), bf16[16,8,32,256]{3,2,1,0:T(8,128)(2,1)}, u32[]{:S(2)}, u32[]{:S(2)}) async-start(bf16[16,8,32,256]{3,2,1,0:T(8,128)(2,1)} %param.10), calls=%async_computation | async-start | bytes 4194304 | tf_op jit(solution)/shard_map/all_to_all | solution.py:39
  20.7 160.2 %all-reduce.2.cloned.1.call-done = f32[8,256,256]{2,1,0:T(8,128)} async-done(((f32[8,256,256]{2,1,0:T(8,128)}), f32[8,256,256]{2,1,0:T(8,128)}) %all-reduce.2.cloned.1.call-update) | async-done | bytes 2097168 | tf_op jit(solution)/shard_map/psum | solution.py:37
  181.0 1.8 multiply_convert_fusion.2
  182.7 2.0 gather_fusion.4
  184.8 1.8 copy.37
  188.6 2.7 fusion.25
  191.4 63.0 %while.14 = (s32[]{:T(128)}, f32[2,8,256,256]{3,2,1,0:T(8,128)}, s32[4]{0:T(128)S(1)}, bf16[2,8,256,256]{3,2,1,0:T(8,128)(2,1)}, bf16[4,8,256,256]{3,2,1,0:T(8,1...) while((s32[]{:T(128)}, f32[2,8,256,256]{3,2,1,0:T(8,128)}, ...), condition=%wide.region_2.3_spmd.clone, body=%wide.region_1.2_spmd.clone.sunk | while | flops 1078466688 | bytes 24167020 | solution.py:58
  193.3 1.6 fusion.46
  195.0 2.0 gather_fusion.1
  197.0 3.6 %gather_fusion.2 = bf16[8,2,256,256]{3,2,1,0:T(8,128)(2,1)} fusion(bf16[2,8,256,256]{3,2,1,0:T(8,128)(2,1)} %get-tuple-element.238, s32[1024]{0:T(1024)S(1)} %pad_clamp_fusion.5), kind=kCustom, calls=%fused_computation.clone.clone.1 | custom fusion | bytes 4194336 | tf_op jit(solution)/shard_map/while/body/eval_jaxpr/gather | solution.py:17
  200.6 5.6 %select_add_fusion.2 = f32[2,8,256,256]{3,2,1,0:T(8,128)} fusion(f32[2,8,256,256]{3,2,1,0:T(8,128)} %get-tuple-element.227, bf16[2,8,256,256]{3,2,1,0:T(8,128)(2,1)} %bitcast.64, pred[]{:T(512)S(6)} %compare.3, bf16[8,256,256]{2,1,0:T(8,128)(2,1)S(1)} %fusion.46, bf16[8,2,256,256]{3,2,1,0:T(8,128)(2,1)} %gather_fusion.2), kind=kOutput, calls=%fused_computation.7.clone.1 | convolution fusion | flops 1076887552 | bytes 13631489 | tf_op jit(solution)/shard_map/while/body/eval_jaxpr/phad,phbd->phab/dot_general | solution.py:22
  209.8 2.0 gather_fusion.1
  211.8 3.6 %gather_fusion.2 = bf16[8,2,256,256]{3,2,1,0:T(8,128)(2,1)} fusion(bf16[2,8,256,256]{3,2,1,0:T(8,128)(2,1)} %get-tuple-element.238, s32[1024]{0:T(1024)S(1)} %pad_clamp_fusion.5), kind=kCustom, calls=%fused_computation.clone.clone.1 | custom fusion | bytes 4194336 | tf_op jit(solution)/shard_map/while/body/eval_jaxpr/gather | solution.py:17
  215.4 6.8 %select_add_fusion.2 = f32[2,8,256,256]{3,2,1,0:T(8,128)} fusion(f32[2,8,256,256]{3,2,1,0:T(8,128)} %get-tuple-element.227, bf16[2,8,256,256]{3,2,1,0:T(8,128)(2,1)} %bitcast.64, pred[]{:T(512)S(6)} %compare.3, bf16[8,256,256]{2,1,0:T(8,128)(2,1)S(1)} %fusion.46, bf16[8,2,256,256]{3,2,1,0:T(8,128)(2,1)} %gather_fusion.2), kind=kOutput, calls=%fused_computation.7.clone.1 | convolution fusion | flops 1076887552 | bytes 13631489 | tf_op jit(solution)/shard_map/while/body/eval_jaxpr/phad,phbd->phab/dot_general | solution.py:22
  225.9 2.0 gather_fusion.1
  227.9 3.6 %gather_fusion.2 = bf16[8,2,256,256]{3,2,1,0:T(8,128)(2,1)} fusion(bf16[2,8,256,256]{3,2,1,0:T(8,128)(2,1)} %get-tuple-element.238, s32[1024]{0:T(1024)S(1)} %pad_clamp_fusion.5), kind=kCustom, calls=%fused_computation.clone.clone.1 | custom fusion | bytes 4194336 | tf_op jit(solution)/shard_map/while/body/eval_jaxpr/gather | solution.py:17
  231.5 6.8 %select_add_fusion.2 = f32[2,8,256,256]{3,2,1,0:T(8,128)} fusion(f32[2,8,256,256]{3,2,1,0:T(8,128)} %get-tuple-element.227, bf16[2,8,256,256]{3,2,1,0:T(8,128)(2,1)} %bitcast.64, pred[]{:T(512)S(6)} %compare.3, bf16[8,256,256]{2,1,0:T(8,128)(2,1)S(1)} %fusion.46, bf16[8,2,256,256]{3,2,1,0:T(8,128)(2,1)} %gather_fusion.2), kind=kOutput, calls=%fused_computation.7.clone.1 | convolution fusion | flops 1076887552 | bytes 13631489 | tf_op jit(solution)/shard_map/while/body/eval_jaxpr/phad,phbd->phab/dot_general | solution.py:22
  242.0 2.0 gather_fusion.1
  244.0 3.6 %gather_fusion.2 = bf16[8,2,256,256]{3,2,1,0:T(8,128)(2,1)} fusion(bf16[2,8,256,256]{3,2,1,0:T(8,128)(2,1)} %get-tuple-element.238, s32[1024]{0:T(1024)S(1)} %pad_clamp_fusion.5), kind=kCustom, calls=%fused_computation.clone.clone.1 | custom fusion | bytes 4194336 | tf_op jit(solution)/shard_map/while/body/eval_jaxpr/gather | solution.py:17
  247.6 6.8 %select_add_fusion.2 = f32[2,8,256,256]{3,2,1,0:T(8,128)} fusion(f32[2,8,256,256]{3,2,1,0:T(8,128)} %get-tuple-element.227, bf16[2,8,256,256]{3,2,1,0:T(8,128)(2,1)} %bitcast.64, pred[]{:T(512)S(6)} %compare.3, bf16[8,256,256]{2,1,0:T(8,128)(2,1)S(1)} %fusion.46, bf16[8,2,256,256]{3,2,1,0:T(8,128)(2,1)} %gather_fusion.2), kind=kOutput, calls=%fused_computation.7.clone.1 | convolution fusion | flops 1076887552 | bytes 13631489 | tf_op jit(solution)/shard_map/while/body/eval_jaxpr/phad,phbd->phab/dot_general | solution.py:22
  254.4 5.0 %fusion.17 = bf16[2,8,256,256]{3,2,1,0:T(8,128)(2,1)S(1)} fusion(f32[2,8,256,256]{3,2,1,0:T(8,128)} %get-tuple-element.129, f32[2,8,256,256]{3,2,1,0:T(8,128)} %fusion.25, bf16[2,8,256,256]{3,2,1,0:T(8,128)(2,1)} %get-tuple-element.246, f32[2,8,256]{2,1,0:T(8,128)S(1)} %bitcast.68, f32[8,256]{1,0:T(8,128)S(1)} %fusion.23, ...), kind=kOutput, calls=%fused_computation.24 | convolution fusion | flops 542113792 | bytes 13656064 | tf_op jit(solution)/shard_map/hac,phcb->phab/dot_general | solution.py:62
  260.6 50.6 %all_to_all.36 = bf16[2,8,256,256]{3,1,0,2:T(8,128)(2,1)S(1)} all-to-all(bf16[2,8,256,256]{3,1,0,2:T(8,128)(2,1)S(1)} %copy.42), channel_id=1, replica_groups=mesh['grp'=4,'blk'=8] {'blk'}, dimensions={2} | all-to-all | bytes 4194304 | tf_op jit(solution)/shard_map/all_to_all | solution.py:67
  311.3 2.1 copy.43
  (67 shorter events, 19.1 us)
Async XLA Ops:
  7.4 1.0 copy-start
  7.4 173.6 %all-reduce.2.cloned.1.call-start = ((), (), s32[]{:S(2)}) async-start(), calls=%async_computation.3 | async-start | bytes 4194304 | tf_op jit(solution)/shard_map/psum | solution.py:37
  11.3 180.1 %all-gather.2.cloned.1.call-start = ((), (), s32[]{:S(2)}) async-start(), calls=%async_computation.2 | async-start | bytes 5242880 | tf_op jit(solution)/shard_map/all_gather | solution.py:53
  11.9 7.5 %copy-start.5 = (s32[64,2]{0,1:T(2,128)S(1)}, s32[64,2]{0,1:T(2,128)}, u32[]{:S(2)}) copy-start(s32[64,2]{0,1:T(2,128)} %param.13) | copy-start | bytes 1540
  11.9 7.6 %copy-start.4 = (s32[240]{0:T(256)S(1)}, s32[240]{0:T(256)}, u32[]{:S(2)}) copy-start(s32[240]{0:T(256)} %param.14) | copy-start | bytes 2884
  11.9 8.2 %copy-start.3 = (s32[8]{0:T(128)S(1)}, s32[8]{0:T(128)}, u32[]{:S(2)}) copy-start(s32[8]{0:T(128)} %param.15) | copy-start | bytes 100
  11.9 172.9 %all-to-all-start = ((bf16[16,8,32,256]{3,2,1,0:T(8,128)(2,1)}), bf16[16,8,32,256]{3,2,1,0:T(8,128)(2,1)}, u32[]{:S(2)}, u32[]{:S(2)}) async-start(bf16[16,8,32,256]{3,2,1,0:T(8,128)(2,1)} %param.10), calls=%async_computation | async-start | bytes 4194304 | tf_op jit(solution)/shard_map/all_to_all | solution.py:39
  186.6 2.0 copy-start.2
  187.3 1.3 copy-start.1
  188.6 2.7 copy-start.6
Sparse Core Ops, SparseCore 0:
  13.5 167.3 all-reduce.1
Sparse Core Ops, SparseCore 1:
  13.3 37.3 all-gather.1
where the time goes:
time: 322 us; the launch traced here: 321 us
  waiting for transfers between devices  161 us (50%)
  blocking collectives  50.6 us (16%)
  local copies, waits for them, and re-layouts  37.7 us (12%)
  matrix products  36.7 us (11%)
  between operations  14.9 us (5%)
  other arithmetic  12.5 us (4%)
  starting transfers between devices  7.47 us (2%)
    psum x1, waiting for transfers between devices, per_device(): coupling = lax.psum(local_sum, ('grp', 'blk'))  160 us
    all_to_all x1, blocking collectives, per_device(): lax.all_to_all(result, 'blk', split_axis=2, concat_axis=0, tiled=True)  50.6 us
    dot_general x4, matrix products, slab_terms(): jnp.einsum('phad,phbd->phab', half_product, right_tile, preferred_element...  26.1 us
    gather x4, local copies, waits for them, and re-layouts, slab_terms(): shifted = masked[:, block_perm]  14.3 us
    gather x4, local copies, waits for them, and re-layouts, slab_terms(): right_tile = left_tile[col_index]  8.02 us
    all_to_all x1, starting transfers between devices, per_device(): lax.all_to_all(amplitudes, 'blk', split_axis=0, concat_axis=2, tiled=True)  7.42 us
  transfers between devices with their start and end apart: 3, of which 1 were waited for; matrix products, arithmetic and copies ran while one was open for 3% of the time, Pallas kernels for 0%

commit v1 on v0

v1 whole, which is shorter than its diff:
```python
import functools
import math

import jax
import jax.numpy as jnp
from jax import lax
from jax.experimental import pallas as pl
from jax.experimental.pallas import tpu as pltpu
from jax.sharding import PartitionSpec as P

IRREPS = 8


def xor_permute(value, axis, count, bits):
    return lax.ppermute(value, axis, [(i, i ^ bits) for i in range(count)])


def pair_kernel(
    blk_count, slab_count, scalars, *refs
):
    piece_refs = refs[:blk_count]
    slab_refs = refs[blk_count : blk_count + slab_count]
    coupling_ref = refs[blk_count + slab_count]
    out_refs = refs[blk_count + slab_count + 1 : 2 * blk_count + slab_count + 1]
    assembled, masked, total = refs[2 * blk_count + slab_count + 1 :]
    rows = piece_refs[0].shape[1]
    slots = piece_refs[0].shape[2]
    sym = scalars[IRREPS]
    me = scalars[IRREPS + 1]

    def assemble(h, carry):
        for s in range(blk_count):
            start = pl.multiple_of((me ^ s) * rows, rows)
            assembled[pl.ds(start, rows), :] = piece_refs[s][h].astype(jnp.float32)
        row_ids = lax.broadcasted_iota(jnp.int32, (slots, slots), 0)
        col_ids = lax.broadcasted_iota(jnp.int32, (slots, slots), 1)
        keep = (row_ids < scalars[h]) & (col_ids < scalars[h ^ sym])
        masked[h] = jnp.where(keep, assembled[...], 0.0).astype(jnp.bfloat16)
        return carry

    lax.fori_loop(0, IRREPS, assemble, 0)

    def one_block(h, carry):
        col = h ^ sym
        acc = jnp.dot(masked[h], coupling_ref[col], preferred_element_type=jnp.float32)
        acc += jnp.dot(coupling_ref[h], masked[h], preferred_element_type=jnp.float32)
        for q in range(slab_count):
            half = jnp.dot(
                slab_refs[q][h], masked[h ^ scalars[IRREPS + 2 + q]], preferred_element_type=jnp.float32
            ).astype(jnp.bfloat16)
            acc += lax.dot_general(
                half, slab_refs[q][col], (((1,), (1,)), ((), ())), preferred_element_type=jnp.float32
            )
        row_ids = lax.broadcasted_iota(jnp.int32, (slots, slots), 0)
        col_ids = lax.broadcasted_iota(jnp.int32, (slots, slots), 1)
        keep = (row_ids < scalars[h]) & (col_ids < scalars[col])
        total[...] = jnp.where(keep, acc, 0.0)
        for s in range(blk_count):
            start = pl.multiple_of((me ^ s) * rows, rows)
            out_refs[s][h] = total[pl.ds(start, rows), :].astype(jnp.bfloat16)
        return carry

    lax.fori_loop(0, IRREPS, one_block, 0)


def pair_call(scalars, pieces, slabs, coupling):
    blk_count, slab_count = len(pieces), len(slabs)
    rows, slots = pieces[0].shape[1:]
    vmem = pl.BlockSpec(memory_space=pltpu.VMEM)
    flops = IRREPS * (2 * slab_count + 2) * 2 * slots**3
    return pl.pallas_call(
        functools.partial(pair_kernel, blk_count, slab_count),
        out_shape=[jax.ShapeDtypeStruct((IRREPS, rows, slots), jnp.bfloat16)] * blk_count,
        in_specs=[pl.BlockSpec(memory_space=pltpu.SMEM)] + [vmem] * (blk_count + slab_count + 1),
        out_specs=[vmem] * blk_count,
        scratch_shapes=[
            pltpu.VMEM((slots, slots), jnp.float32),
            pltpu.VMEM((IRREPS, slots, slots), jnp.bfloat16),
            pltpu.VMEM((slots, slots), jnp.float32),
        ],
        compiler_params=pltpu.CompilerParams(vmem_limit_bytes=40 * 1024 * 1024),
        cost_estimate=pl.CostEstimate(flops=flops, bytes_accessed=16 * slots**2 * 10, transcendentals=0),
    )(scalars, *pieces, *slabs, coupling)


def coupling_blocks(ov_left, ov_right, grp_count, blk_count):
    rows, _, slots = ov_left.shape
    per_grp = IRREPS // grp_count
    grp, blk = lax.axis_index("grp"), lax.axis_index("blk")
    factors = jnp.stack([ov_left, ov_right]).transpose(2, 0, 1, 3)
    parts = [
        lax.dynamic_slice_in_dim(factors, (grp ^ s) * per_grp, per_grp, 0) for s in range(grp_count)
    ]
    parts = [parts[0]] + [xor_permute(parts[s], "grp", grp_count, s) for s in range(1, grp_count)]
    gathered = jnp.concatenate(parts, axis=2)
    local = jnp.einsum(
        "hrs,hrt->hst", gathered[:, 0], gathered[:, 1], preferred_element_type=jnp.float32
    )
    scale = 1.0 / math.sqrt(rows * grp_count * blk_count)
    flat = local.reshape(per_grp * slots, slots)
    half_rows = per_grp * slots // 2
    low, high = blk % 2, blk // 2
    away = lax.dynamic_slice_in_dim(flat, (1 - low) * half_rows, half_rows, 0)
    kept = lax.dynamic_slice_in_dim(flat, low * half_rows, half_rows, 0)
    kept = kept + xor_permute(away, "blk", blk_count, 1)
    highs = blk_count // 2
    piece = half_rows // highs
    own = lax.dynamic_slice_in_dim(kept, high * piece, piece, 0)
    for s in range(1, highs):
        away = lax.dynamic_slice_in_dim(kept, (high ^ s) * piece, piece, 0)
        own = own + xor_permute(away, "blk", blk_count, 2 * s)
    own = (own * scale).astype(jnp.bfloat16)
    half = jnp.zeros((half_rows, slots), jnp.bfloat16)
    half = lax.dynamic_update_slice_in_dim(half, own, high * piece, 0)
    for s in range(1, highs):
        came = xor_permute(own, "blk", blk_count, 2 * s)
        half = lax.dynamic_update_slice_in_dim(half, came, (high ^ s) * piece, 0)
    same_core = jnp.zeros((grp_count // 2, 2, half_rows, slots), jnp.bfloat16)
    for dx in range(grp_count // 2):
        for dy in range(2):
            came = half
            if dx or dy:
                flat_ids = [(g, b) for g in range(grp_count) for b in range(blk_count)]
                perm = [
                    (g * blk_count + b, (g ^ (2 * dx)) * blk_count + (b ^ dy)) for g, b in flat_ids
                ]
                came = lax.ppermute(half, ("grp", "blk"), perm)
            same_core = lax.dynamic_update_slice(
                same_core, came[None, None], ((grp // 2) ^ dx, low ^ dy, 0, 0)
            )
    other_core = xor_permute(same_core, "grp", grp_count, 1)
    core = grp % 2
    first = jnp.where(core == 0, same_core, other_core)
    second = jnp.where(core == 0, other_core, same_core)
    return jnp.stack([first, second], axis=1).reshape(IRREPS, slots, slots), gathered


def per_device(amplitudes, chol_vv, chol_irrep, pair_occ, occ_irrep, vir_count, ov_left, ov_right):
    blk_count = lax.axis_size("blk")
    grp_count = lax.axis_size("grp")
    pair_total, _, rows, slots = amplitudes.shape
    per_dev = pair_total // blk_count
    grp, blk = lax.axis_index("grp"), lax.axis_index("blk")

    pieces = [None] * blk_count
    for s in reversed(range(blk_count)):
        block = lax.dynamic_slice_in_dim(amplitudes, (blk ^ s) * per_dev, per_dev, 0)
        pieces[s] = xor_permute(block, "blk", blk_count, s) if s else block

    coupling, after = coupling_blocks(ov_left, ov_right, grp_count, blk_count)

    per_slab = chol_vv.shape[0]
    chol_vv, _ = lax.optimization_barrier((chol_vv, after))
    same = [chol_vv] + [
        xor_permute(chol_vv, "grp", grp_count, 2 * s) for s in range(1, grp_count // 2)
    ]
    other = [xor_permute(slab, "grp", grp_count, 1) for slab in same]
    slabs, owners = [], []
    for s in range(grp_count // 2):
        for c, group in enumerate((same, other)):
            for k in range(per_slab):
                slabs.append(group[s][k])
                owners.append((grp ^ (2 * s + c)) * per_slab + k)
    slab_irreps = chol_irrep[jnp.stack(owners)]

    pair_start = (grp * blk_count + blk) * per_dev
    own_pairs = lax.dynamic_slice_in_dim(pair_occ, pair_start, per_dev, 0)
    occ_ids = jnp.arange(occ_irrep.shape[0], dtype=jnp.int32)
    one_hot = own_pairs[:, :, None] == occ_ids[None, None, :]
    labels = jnp.sum(jnp.where(one_hot, occ_irrep[None, None, :], 0), axis=2)
    pair_irrep = jnp.bitwise_xor(labels[:, 0], labels[:, 1])

    result = jnp.zeros(amplitudes.shape, jnp.bfloat16)
    for j in range(per_dev):
        scalars = jnp.concatenate(
            [vir_count, pair_irrep[j : j + 1], blk[None].astype(jnp.int32), slab_irreps]
        )
        outs = pair_call(scalars, [piece[j] for piece in pieces], slabs, coupling)
        for s in reversed(range(blk_count)):
            came = xor_permute(outs[s], "blk", blk_count, s) if s else outs[s]
            result = lax.dynamic_update_slice(
                result, came[None], ((blk ^ s) * per_dev + j, 0, 0, 0)
            )
    return result


def solution(mesh):
    return jax.shard_map(
        per_device,
        mesh=mesh,
        in_specs=(
            P("grp", None, "blk", None),
            P("grp", None, None, None),
            P(),
            P(),
            P(),
            P(),
            P(("grp", "blk"), None, None),
            P(("grp", "blk"), None, None),
        ),
        out_specs=P("grp", None, "blk", None),
        check_vma=False,
    )
```

time: 322 us -> 183 us (0.57)
  waiting for transfers between devices: 161 us -> 103 us
  blocking collectives: 50.6 us -> 0 us
  starting transfers between devices: 7.47 us -> 55.4 us
  matrix products: 36.7 us -> 0.34 us
  local copies, waits for them, and re-layouts: 37.7 us -> 7.99 us
  between operations: 14.9 us -> 0.6 us
  Pallas kernels: 0 us -> 12.2 us
  other arithmetic: 12.5 us -> 3.27 us
    psum x1 -> x0, waiting for transfers between devices: 160 us -> none  [per_device(): coupling = lax.psum(local_sum, ('grp', 'blk'))]
    ppermute x0 -> x38, waiting for transfers between devices: none -> 103 us  [the longest x35 88.4 us: xor_permute(): return lax.ppermute(value, axis, [(i, i ^ bits) for i in range(count)])]
    ppermute x0 -> x38, starting transfers between devices: none -> 55.4 us  [the longest x35 54.4 us: xor_permute(): return lax.ppermute(value, axis, [(i, i ^ bits) for i in range(count)])]
    all_to_all x1 -> x0, blocking collectives: 50.6 us -> none  [per_device(): lax.all_to_all(result, 'blk', split_axis=2, concat_axis=0, tiled=True)]
    dot_general x7 -> x1, matrix products: 36.7 us -> 0.34 us  [coupling_blocks(): jnp.einsum('hrs,hrt->hst', gathered[:, 0], gathered[:, 1], preferred_elem...]
    gather x14 -> x1, local copies, waits for them, and re-layouts: 27.2 us -> 0.64 us  [per_device(): slab_irreps = chol_irrep[jnp.stack(owners)]]
    pallas_call x0 -> x2, Pallas kernels: none -> 12.2 us  [pair_call(): pl.pallas_call(functools.partial(pair_kernel, blk_count, slab_count), out...]
    all_to_all x1 -> x0, starting transfers between devices: 7.42 us -> none  [per_device(): lax.all_to_all(amplitudes, 'blk', split_axis=0, concat_axis=2, tiled=True)]
  transfers between devices with their start and end apart: 3 -> 38, of which waited for: 1 -> 22; matrix products, arithmetic and copies ran while one was open for 3% -> 4% of each run, Pallas kernels for 0% -> 3%
where the time goes in v1:
time: 183 us
  waiting for transfers between devices  103 us (56%)
  starting transfers between devices  55.4 us (30%)
  Pallas kernels  12.2 us (7%)
  local copies, waits for them, and re-layouts  7.99 us (4%)
  other arithmetic  3.27 us (2%)
    ppermute x35, waiting for transfers between devices, xor_permute(): return lax.ppermute(value, axis, [(i, i ^ bits) for i in range(count)])  88.4 us
    ppermute x35, starting transfers between devices, xor_permute(): return lax.ppermute(value, axis, [(i, i ^ bits) for i in range(count)])  54.4 us
    ppermute x3, waiting for transfers between devices, coupling_blocks(): came = lax.ppermute(half, ('grp', 'blk'), perm)  14.7 us
    pallas_call x2, Pallas kernels, pair_call(): pl.pallas_call(functools.partial(pair_kernel, blk_count, slab_count), out...  12.2 us
  transfers between devices with their start and end apart: 38, of which 22 were waited for; matrix products, arithmetic and copies ran while one was open for 4% of the time, Pallas kernels for 3%

profile of v1, /device:TPU:0, one launch (start us, length us, event | category | flops | bytes accessed | tf_op | source)
XLA Modules:
  0.0 182.9 jit_solution(6009659076917997893)
XLA Ops:
  2.2 2.6 %collective-permute-start.8 = (bf16[2,2,128,256]{3,2,0,1:T(8,128)(2,1)S(1)}, bf16[2,2,128,256]{3,2,0,1:T(8,128)(2,1)}, u32[]{:S(2)}, u32[]{:S(2)}) collective-permute-start(bf16[2,2,128,256]{3,2,0,1:T(8,128)(2,1)S(1)} %get-tuple-element.54), channel_id=1, source_target_pairs={{0,16},{8,24},{16,0},{24,8},{1,17},{9,25},{17,1},{25,9},{2,18},{10... | collective-permute-start | bytes 786440 | tf_op jit(solution)/shard_map/ppermute | solution.py:15
  6.1 4.8 %collective-permute-start.6 = (bf16[2,8,32,256]{3,2,1,0:T(8,128)(2,1)}, bf16[2,8,32,256]{3,2,1,0:T(8,128)(2,1)}, u32[]{:S(2)}, u32[]{:S(2)}) collective-permute-start(bf16[2,8,32,256]{3,2,1,0:T(8,128)(2,1)} %get-tuple-element.43), channel_id=1, source_target_pairs={{0,7},{1,6},{2,5},{3,4},{4,3},{5,2},{6,1},{7,0},{8,15},{9,14},{10,... | collective-permute-start | bytes 786440 | tf_op jit(solution)/shard_map/ppermute | solution.py:15
  14.3 2.9 %collective-permute-start.3 = (bf16[2,8,32,256]{3,2,1,0:T(8,128)(2,1)}, bf16[2,8,32,256]{3,2,1,0:T(8,128)(2,1)S(1)}, u32[]{:S(2)}, u32[]{:S(2)}) collective-permute-start(bf16[2,8,32,256]{3,2,1,0:T(8,128)(2,1)} %get-tuple-element.45), channel_id=1, source_target_pairs={{0,4},{1,5},{2,6},{3,7},{4,0},{5,1},{6,2},{7,3},{8,12},{9,13},{10,... | collective-permute-start | bytes 786440 | tf_op jit(solution)/shard_map/ppermute | solution.py:15
  17.7 2.5 %collective-permute-start.1 = (bf16[2,8,32,256]{3,2,1,0:T(8,128)(2,1)}, bf16[2,8,32,256]{3,2,1,0:T(8,128)(2,1)S(1)}, u32[]{:S(2)}, u32[]{:S(2)}) collective-permute-start(bf16[2,8,32,256]{3,2,1,0:T(8,128)(2,1)} %get-tuple-element.47), channel_id=1, source_target_pairs={{0,2},{1,3},{2,0},{3,1},{4,6},{5,7},{6,4},{7,5},{8,10},{9,11},{10,... | collective-permute-start | bytes 786440 | tf_op jit(solution)/shard_map/ppermute | solution.py:15
  23.4 18.9 %collective-permute-done.4 = bf16[2,8,32,256]{3,2,1,0:T(8,128)(2,1)S(1)} collective-permute-done((bf16[2,8,32,256]{3,2,1,0:T(8,128)(2,1)}, bf16[2,8,32,256]{3,2,1,0:T(8,128)(2,1)S(1)}, u32[]{:S(2)}, u32[]{:S(2)}) %collective-permute-start.4) | collective-permute-done | bytes 262176 | tf_op jit(solution)/shard_map/ppermute | solution.py:15
  42.4 3.5 %collective-permute-start.14 = (f32[64,256]{1,0:T(8,128)S(1)}, f32[64,256]{1,0:T(8,128)S(1)}, u32[]{:S(2)}, u32[]{:S(2)}) collective-permute-start(f32[64,256]{1,0:T(8,128)S(1)} %get-tuple-element.70), channel_id=1, source_target_pairs={{0,2},{1,3},{2,0},{3,1},{4,6},{5,7},{6,4},{7,5},{8,10},{9,11},{10,... | collective-permute-start | bytes 196616 | tf_op jit(solution)/shard_map/ppermute | solution.py:15
  53.5 6.7 %collective-permute-done.15 = f32[64,256]{1,0:T(8,128)S(1)} collective-permute-done((f32[64,256]{1,0:T(8,128)S(1)}, f32[64,256]{1,0:T(8,128)S(1)}, u32[]{:S(2)}, u32[]{:S(2)}) %collective-permute-start.15) | collective-permute-done | bytes 65568 | tf_op jit(solution)/shard_map/ppermute | solution.py:15
  61.9 3.9 %collective-permute-done.17 = bf16[64,256]{1,0:T(8,128)(2,1)S(1)} collective-permute-done((bf16[64,256]{1,0:T(8,128)(2,1)S(1)}, bf16[64,256]{1,0:T(8,128)(2,1)S(1)}, u32[]{:S(2)}, u32[]{:S(2)}) %collective-permute-start.17) | collective-permute-done | bytes 32800 | tf_op jit(solution)/shard_map/ppermute | solution.py:15
  66.7 3.9 %collective-permute-done.18 = bf16[64,256]{1,0:T(8,128)(2,1)S(1)} collective-permute-done((bf16[64,256]{1,0:T(8,128)(2,1)S(1)}, bf16[64,256]{1,0:T(8,128)(2,1)S(1)}, u32[]{:S(2)}, u32[]{:S(2)}) %collective-permute-start.18) | collective-permute-done | bytes 32800 | tf_op jit(solution)/shard_map/ppermute | solution.py:15
  72.9 3.4 %collective-permute-done.19 = bf16[64,256]{1,0:T(8,128)(2,1)S(1)} collective-permute-done((bf16[64,256]{1,0:T(8,128)(2,1)S(1)}, bf16[64,256]{1,0:T(8,128)(2,1)S(1)}, u32[]{:S(2)}, u32[]{:S(2)}) %collective-permute-start.19) | collective-permute-done | bytes 32800 | tf_op jit(solution)/shard_map/ppermute | solution.py:15
  76.4 4.9 %collective-permute-done.20 = bf16[256,256]{1,0:T(8,128)(2,1)S(1)} collective-permute-done((bf16[256,256]{1,0:T(8,128)(2,1)S(1)}, bf16[256,256]{1,0:T(8,128)(2,1)S(1)}, u32[]{:S(2)}, u32[]{:S(2)}) %collective-permute-start.20) | collective-permute-done | bytes 131104 | tf_op jit(solution)/shard_map/ppermute | solution.py:127
  82.1 4.2 %collective-permute-done.21 = bf16[256,256]{1,0:T(8,128)(2,1)S(1)} collective-permute-done((bf16[256,256]{1,0:T(8,128)(2,1)S(1)}, bf16[256,256]{1,0:T(8,128)(2,1)S(1)}, u32[]{:S(2)}, u32[]{:S(2)}) %collective-permute-start.21) | collective-permute-done | bytes 131104 | tf_op jit(solution)/shard_map/ppermute | solution.py:127
  86.5 5.6 %collective-permute-done.22 = bf16[256,256]{1,0:T(8,128)(2,1)S(1)} collective-permute-done((bf16[256,256]{1,0:T(8,128)(2,1)S(1)}, bf16[256,256]{1,0:T(8,128)(2,1)S(1)}, u32[]{:S(2)}, u32[]{:S(2)}) %collective-permute-start.22) | collective-permute-done | bytes 131104 | tf_op jit(solution)/shard_map/ppermute | solution.py:127
  92.9 2.6 %collective-permute-done.23 = bf16[2,2,256,256]{3,2,1,0:T(8,128)(2,1)S(1)} collective-permute-done((bf16[2,2,256,256]{3,2,1,0:T(8,128)(2,1)S(1)}, bf16[2,2,256,256]{3,2,1,0:T(8,128)(2,1)S(1)}, u32[]{:S(2)}, u32[]{:S(2)}) %collective-permute-start.23) | collective-permute-done | bytes 524320 | tf_op jit(solution)/shard_map/ppermute | solution.py:15
  97.0 6.1 %shard_map.82 = (bf16[8,32,256]{2,1,0:T(8,128)(2,1)S(1)}, bf16[8,32,256]{2,1,0:T(8,128)(2,1)S(1)}, bf16[8,32,256]{2,1,0:T(8,128)(2,1)S(1)}, bf16[8,32,256]{2,1,0...) custom-call(s32[14]{0:T(128)S(1)} %get-tuple-element.74.scalars, ...), custom_call_target="tpu_custom_call" | custom-call | flops 2684354560 | bytes 10485760 | tf_op jit(solution)/shard_map/pallas_call | solution.py:71
  105.0 6.1 %shard_map.83 = (bf16[8,32,256]{2,1,0:T(8,128)(2,1)S(1)}, bf16[8,32,256]{2,1,0:T(8,128)(2,1)S(1)}, bf16[8,32,256]{2,1,0:T(8,128)(2,1)S(1)}, bf16[8,32,256]{2,1,0...) custom-call(s32[14]{0:T(128)S(1)} %get-tuple-element.73.scalars, ...), custom_call_target="tpu_custom_call" | custom-call | flops 2684354560 | bytes 10485760 | tf_op jit(solution)/shard_map/pallas_call | solution.py:71
  111.1 3.0 %collective-permute-start.31 = (bf16[8,32,256]{2,1,0:T(8,128)(2,1)S(1)}, bf16[8,32,256]{2,1,0:T(8,128)(2,1)S(1)}, u32[]{:S(2)}, u32[]{:S(2)}) collective-permute-start(bf16[8,32,256]{2,1,0:T(8,128)(2,1)S(1)} %get-tuple-element.31), channel_id=1, source_target_pairs={{0,7},{1,6},{2,5},{3,4},{4,3},{5,2},{6,1},{7,0},{8,15},{9,14},{10,... | collective-permute-start | bytes 393224 | tf_op jit(solution)/shard_map/ppermute | solution.py:15
  120.6 10.4 %collective-permute-done.25 = bf16[8,32,256]{2,1,0:T(8,128)(2,1)S(1)} collective-permute-done((bf16[8,32,256]{2,1,0:T(8,128)(2,1)S(1)}, bf16[8,32,256]{2,1,0:T(8,128)(2,1)S(1)}, u32[]{:S(2)}, u32[]{:S(2)}) %collective-permute-start.25) | collective-permute-done | bytes 131104 | tf_op jit(solution)/shard_map/ppermute | solution.py:15
  131.0 10.0 %collective-permute-start.26 = (bf16[8,32,256]{2,1,0:T(8,128)(2,1)S(1)}, bf16[8,32,256]{2,1,0:T(8,128)(2,1)S(1)}, u32[]{:S(2)}, u32[]{:S(2)}) collective-permute-start(bf16[8,32,256]{2,1,0:T(8,128)(2,1)S(1)} %get-tuple-element.25), channel_id=1, source_target_pairs={{0,5},{1,4},{2,7},{3,6},{4,1},{5,0},{6,3},{7,2},{8,13},{9,12},{10,... | collective-permute-start | bytes 393224 | tf_op jit(solution)/shard_map/ppermute | solution.py:15
  141.0 6.5 %collective-permute-done.26 = bf16[8,32,256]{2,1,0:T(8,128)(2,1)S(1)} collective-permute-done((bf16[8,32,256]{2,1,0:T(8,128)(2,1)S(1)}, bf16[8,32,256]{2,1,0:T(8,128)(2,1)S(1)}, u32[]{:S(2)}, u32[]{:S(2)}) %collective-permute-start.26) | collective-permute-done | bytes 131104 | tf_op jit(solution)/shard_map/ppermute | solution.py:15
  147.5 6.6 %collective-permute-done.27 = bf16[8,32,256]{2,1,0:T(8,128)(2,1)S(1)} collective-permute-done((bf16[8,32,256]{2,1,0:T(8,128)(2,1)S(1)}, bf16[8,32,256]{2,1,0:T(8,128)(2,1)S(1)}, u32[]{:S(2)}, u32[]{:S(2)}) %collective-permute-start.27) | collective-permute-done | bytes 131104 | tf_op jit(solution)/shard_map/ppermute | solution.py:15
  154.2 5.8 %collective-permute-done.28 = bf16[8,32,256]{2,1,0:T(8,128)(2,1)S(1)} collective-permute-done((bf16[8,32,256]{2,1,0:T(8,128)(2,1)S(1)}, bf16[8,32,256]{2,1,0:T(8,128)(2,1)S(1)}, u32[]{:S(2)}, u32[]{:S(2)}) %collective-permute-start.28) | collective-permute-done | bytes 131104 | tf_op jit(solution)/shard_map/ppermute | solution.py:15
  160.4 4.6 %collective-permute-done.29 = bf16[8,32,256]{2,1,0:T(8,128)(2,1)S(1)} collective-permute-done((bf16[8,32,256]{2,1,0:T(8,128)(2,1)S(1)}, bf16[8,32,256]{2,1,0:T(8,128)(2,1)S(1)}, u32[]{:S(2)}, u32[]{:S(2)}) %collective-permute-start.29) | collective-permute-done | bytes 131104 | tf_op jit(solution)/shard_map/ppermute | solution.py:15
  167.3 4.6 %collective-permute-done.30 = bf16[8,32,256]{2,1,0:T(8,128)(2,1)S(1)} collective-permute-done((bf16[8,32,256]{2,1,0:T(8,128)(2,1)S(1)}, bf16[8,32,256]{2,1,0:T(8,128)(2,1)S(1)}, u32[]{:S(2)}, u32[]{:S(2)}) %collective-permute-start.30) | collective-permute-done | bytes 131104 | tf_op jit(solution)/shard_map/ppermute | solution.py:15
  (126 shorter events, 48.3 us)
Async XLA Ops:
  1.7 12.6 %collective-permute-start.7 = (bf16[2,2,128,256]{3,2,0,1:T(8,128)(2,1)S(1)}, bf16[2,2,128,256]{3,2,0,1:T(8,128)(2,1)}, u32[]{:S(2)}, u32[]{:S(2)}) collective-permute-start(bf16[2,2,128,256]{3,2,0,1:T(8,128)(2,1)S(1)} %get-tuple-element.53), channel_id=1, source_target_pairs={{0,8},{8,0},{16,24},{24,16},{1,9},{9,1},{17,25},{25,17},{2,10},{10... | collective-permute-start | bytes 786440 | tf_op jit(solution)/shard_map/ppermute | solution.py:15
  2.2 15.0 %collective-permute-start.8 = (bf16[2,2,128,256]{3,2,0,1:T(8,128)(2,1)S(1)}, bf16[2,2,128,256]{3,2,0,1:T(8,128)(2,1)}, u32[]{:S(2)}, u32[]{:S(2)}) collective-permute-start(bf16[2,2,128,256]{3,2,0,1:T(8,128)(2,1)S(1)} %get-tuple-element.54), channel_id=1, source_target_pairs={{0,16},{8,24},{16,0},{24,8},{1,17},{9,25},{17,1},{25,9},{2,18},{10... | collective-permute-start | bytes 786440 | tf_op jit(solution)/shard_map/ppermute | solution.py:15
  4.8 12.9 %collective-permute-start.9 = (bf16[2,2,128,256]{3,2,0,1:T(8,128)(2,1)S(1)}, bf16[2,2,128,256]{3,2,0,1:T(8,128)(2,1)}, u32[]{:S(2)}, u32[]{:S(2)}) collective-permute-start(bf16[2,2,128,256]{3,2,0,1:T(8,128)(2,1)S(1)} %get-tuple-element.55), channel_id=1, source_target_pairs={{0,24},{8,16},{16,8},{24,0},{1,25},{9,17},{17,9},{25,1},{2,26},{10... | collective-permute-start | bytes 786440 | tf_op jit(solution)/shard_map/ppermute | solution.py:15
  6.1 15.7 %collective-permute-start.6 = (bf16[2,8,32,256]{3,2,1,0:T(8,128)(2,1)}, bf16[2,8,32,256]{3,2,1,0:T(8,128)(2,1)}, u32[]{:S(2)}, u32[]{:S(2)}) collective-permute-start(bf16[2,8,32,256]{3,2,1,0:T(8,128)(2,1)} %get-tuple-element.43), channel_id=1, source_target_pairs={{0,7},{1,6},{2,5},{3,4},{4,3},{5,2},{6,1},{7,0},{8,15},{9,14},{10,... | collective-permute-start | bytes 786440 | tf_op jit(solution)/shard_map/ppermute | solution.py:15
  10.9 31.4 %collective-permute-start.4 = (bf16[2,8,32,256]{3,2,1,0:T(8,128)(2,1)}, bf16[2,8,32,256]{3,2,1,0:T(8,128)(2,1)S(1)}, u32[]{:S(2)}, u32[]{:S(2)}) collective-permute-start(bf16[2,8,32,256]{3,2,1,0:T(8,128)(2,1)} %get-tuple-element.44), channel_id=1, source_target_pairs={{0,5},{1,4},{2,7},{3,6},{4,1},{5,0},{6,3},{7,2},{8,13},{9,12},{10,... | collective-permute-start | bytes 786440 | tf_op jit(solution)/shard_map/ppermute | solution.py:15
  14.3 33.7 %collective-permute-start.3 = (bf16[2,8,32,256]{3,2,1,0:T(8,128)(2,1)}, bf16[2,8,32,256]{3,2,1,0:T(8,128)(2,1)S(1)}, u32[]{:S(2)}, u32[]{:S(2)}) collective-permute-start(bf16[2,8,32,256]{3,2,1,0:T(8,128)(2,1)} %get-tuple-element.45), channel_id=1, source_target_pairs={{0,4},{1,5},{2,6},{3,7},{4,0},{5,1},{6,2},{7,3},{8,12},{9,13},{10,... | collective-permute-start | bytes 786440 | tf_op jit(solution)/shard_map/ppermute | solution.py:15
  17.2 44.6 %collective-permute-start.2 = (bf16[2,8,32,256]{3,2,1,0:T(8,128)(2,1)}, bf16[2,8,32,256]{3,2,1,0:T(8,128)(2,1)S(1)}, u32[]{:S(2)}, u32[]{:S(2)}) collective-permute-start(bf16[2,8,32,256]{3,2,1,0:T(8,128)(2,1)} %get-tuple-element.46), channel_id=1, source_target_pairs={{0,3},{1,2},{2,1},{3,0},{4,7},{5,6},{6,5},{7,4},{8,11},{9,10},{10,... | collective-permute-start | bytes 786440 | tf_op jit(solution)/shard_map/ppermute | solution.py:15
  17.7 74.4 %collective-permute-start.1 = (bf16[2,8,32,256]{3,2,1,0:T(8,128)(2,1)}, bf16[2,8,32,256]{3,2,1,0:T(8,128)(2,1)S(1)}, u32[]{:S(2)}, u32[]{:S(2)}) collective-permute-start(bf16[2,8,32,256]{3,2,1,0:T(8,128)(2,1)} %get-tuple-element.47), channel_id=1, source_target_pairs={{0,2},{1,3},{2,0},{3,1},{4,6},{5,7},{6,4},{7,5},{8,10},{9,11},{10,... | collective-permute-start | bytes 786440 | tf_op jit(solution)/shard_map/ppermute | solution.py:15
  21.8 20.5 %collective-permute-start.13 = (f32[256,256]{1,0:T(8,128)S(1)}, f32[256,256]{1,0:T(8,128)S(1)}, u32[]{:S(2)}, u32[]{:S(2)}) collective-permute-start(f32[256,256]{1,0:T(8,128)S(1)} %constant_dynamic-slice_fusion.3), channel_id=1, source_target_pairs={{0,1},{1,0},{2,3},{3,2},{4,5},{5,4},{6,7},{7,6},{8,9},{9,8},{10,11... | collective-permute-start | bytes 786440 | tf_op jit(solution)/shard_map/ppermute | solution.py:15
  42.4 7.1 %collective-permute-start.14 = (f32[64,256]{1,0:T(8,128)S(1)}, f32[64,256]{1,0:T(8,128)S(1)}, u32[]{:S(2)}, u32[]{:S(2)}) collective-permute-start(f32[64,256]{1,0:T(8,128)S(1)} %get-tuple-element.70), channel_id=1, source_target_pairs={{0,2},{1,3},{2,0},{3,1},{4,6},{5,7},{6,4},{7,5},{8,10},{9,11},{10,... | collective-permute-start | bytes 196616 | tf_op jit(solution)/shard_map/ppermute | solution.py:15
  48.0 12.3 %collective-permute-start.15 = (f32[64,256]{1,0:T(8,128)S(1)}, f32[64,256]{1,0:T(8,128)S(1)}, u32[]{:S(2)}, u32[]{:S(2)}) collective-permute-start(f32[64,256]{1,0:T(8,128)S(1)} %get-tuple-element.72), channel_id=1, source_target_pairs={{0,4},{1,5},{2,6},{3,7},{4,0},{5,1},{6,2},{7,3},{8,12},{9,13},{10,... | collective-permute-start | bytes 196616 | tf_op jit(solution)/shard_map/ppermute | solution.py:15
  49.5 43.3 %collective-permute-start = (bf16[2,8,32,256]{3,2,1,0:T(8,128)(2,1)S(1)}, bf16[2,8,32,256]{3,2,1,0:T(8,128)(2,1)S(1)}, u32[]{:S(2)}, u32[]{:S(2)}) collective-permute-start(bf16[2,8,32,256]{3,2,1,0:T(8,128)(2,1)S(1)} %copy-done.6), channel_id=1, source_target_pairs={{0,1},{1,0},{2,3},{3,2},{4,5},{5,4},{6,7},{7,6},{8,9},{9,8},{10,11... | collective-permute-start | bytes 786440 | tf_op jit(solution)/shard_map/ppermute | solution.py:15
  51.9 40.9 %collective-permute-start.5 = (bf16[2,8,32,256]{3,2,1,0:T(8,128)(2,1)S(1)}, bf16[2,8,32,256]{3,2,1,0:T(8,128)(2,1)S(1)}, u32[]{:S(2)}, u32[]{:S(2)}) collective-permute-start(bf16[2,8,32,256]{3,2,1,0:T(8,128)(2,1)S(1)} %copy-done.5), channel_id=1, source_target_pairs={{0,6},{1,7},{2,4},{3,5},{4,2},{5,3},{6,0},{7,1},{8,14},{9,15},{10,... | collective-permute-start | bytes 786440 | tf_op jit(solution)/shard_map/ppermute | solution.py:15
  60.2 32.5 %collective-permute-start.11 = (bf16[1,8,256,256]{3,2,1,0:T(8,128)(2,1)S(1)}, bf16[1,8,256,256]{3,2,1,0:T(8,128)(2,1)S(1)}, u32[]{:S(2)}, u32[]{:S(2)}) collective-permute-start(bf16[1,8,256,256]{3,2,1,0:T(8,128)(2,1)S(1)} %copy-done.1), channel_id=1, source_target_pairs={{0,16},{8,24},{16,0},{24,8},{1,17},{9,25},{17,1},{25,9},{2,18},{10... | collective-permute-start | bytes 3145736 | tf_op jit(solution)/shard_map/ppermute | solution.py:15
  103.1 15.7 %collective-permute-start.24 = (bf16[8,32,256]{2,1,0:T(8,128)(2,1)S(1)}, bf16[8,32,256]{2,1,0:T(8,128)(2,1)S(1)}, u32[]{:S(2)}, u32[]{:S(2)}) collective-permute-start(bf16[8,32,256]{2,1,0:T(8,128)(2,1)S(1)} %get-tuple-element.23), channel_id=1, source_target_pairs={{0,7},{1,6},{2,5},{3,4},{4,3},{5,2},{6,1},{7,0},{8,15},{9,14},{10,... | collective-permute-start | bytes 393224 | tf_op jit(solution)/shard_map/ppermute | solution.py:15
  111.1 62.7 %collective-permute-start.31 = (bf16[8,32,256]{2,1,0:T(8,128)(2,1)S(1)}, bf16[8,32,256]{2,1,0:T(8,128)(2,1)S(1)}, u32[]{:S(2)}, u32[]{:S(2)}) collective-permute-start(bf16[8,32,256]{2,1,0:T(8,128)(2,1)S(1)} %get-tuple-element.31), channel_id=1, source_target_pairs={{0,7},{1,6},{2,5},{3,4},{4,3},{5,2},{6,1},{7,0},{8,15},{9,14},{10,... | collective-permute-start | bytes 393224 | tf_op jit(solution)/shard_map/ppermute | solution.py:15
  114.1 61.8 %collective-permute-start.32 = (bf16[8,32,256]{2,1,0:T(8,128)(2,1)S(1)}, bf16[8,32,256]{2,1,0:T(8,128)(2,1)S(1)}, u32[]{:S(2)}, u32[]{:S(2)}) collective-permute-start(bf16[8,32,256]{2,1,0:T(8,128)(2,1)S(1)} %get-tuple-element.32), channel_id=1, source_target_pairs={{0,6},{1,7},{2,4},{3,5},{4,2},{5,3},{6,0},{7,1},{8,14},{9,15},{10,... | collective-permute-start | bytes 393224 | tf_op jit(solution)/shard_map/ppermute | solution.py:15
  116.4 59.6 %collective-permute-start.33 = (bf16[8,32,256]{2,1,0:T(8,128)(2,1)S(1)}, bf16[8,32,256]{2,1,0:T(8,128)(2,1)S(1)}, u32[]{:S(2)}, u32[]{:S(2)}) collective-permute-start(bf16[8,32,256]{2,1,0:T(8,128)(2,1)S(1)} %get-tuple-element.33), channel_id=1, source_target_pairs={{0,5},{1,4},{2,7},{3,6},{4,1},{5,0},{6,3},{7,2},{8,13},{9,12},{10,... | collective-permute-start | bytes 393224 | tf_op jit(solution)/shard_map/ppermute | solution.py:15
  116.4 59.6 %collective-permute-start.34 = (bf16[8,32,256]{2,1,0:T(8,128)(2,1)S(1)}, bf16[8,32,256]{2,1,0:T(8,128)(2,1)S(1)}, u32[]{:S(2)}, u32[]{:S(2)}) collective-permute-start(bf16[8,32,256]{2,1,0:T(8,128)(2,1)S(1)} %get-tuple-element.34), channel_id=1, source_target_pairs={{0,4},{1,5},{2,6},{3,7},{4,0},{5,1},{6,2},{7,3},{8,12},{9,13},{10,... | collective-permute-start | bytes 393224 | tf_op jit(solution)/shard_map/ppermute | solution.py:15
  118.8 12.2 %collective-permute-start.25 = (bf16[8,32,256]{2,1,0:T(8,128)(2,1)S(1)}, bf16[8,32,256]{2,1,0:T(8,128)(2,1)S(1)}, u32[]{:S(2)}, u32[]{:S(2)}) collective-permute-start(bf16[8,32,256]{2,1,0:T(8,128)(2,1)S(1)} %get-tuple-element.24), channel_id=1, source_target_pairs={{0,6},{1,7},{2,4},{3,5},{4,2},{5,3},{6,0},{7,1},{8,14},{9,15},{10,... | collective-permute-start | bytes 393224 | tf_op jit(solution)/shard_map/ppermute | solution.py:15
  131.0 16.5 %collective-permute-start.26 = (bf16[8,32,256]{2,1,0:T(8,128)(2,1)S(1)}, bf16[8,32,256]{2,1,0:T(8,128)(2,1)S(1)}, u32[]{:S(2)}, u32[]{:S(2)}) collective-permute-start(bf16[8,32,256]{2,1,0:T(8,128)(2,1)S(1)} %get-tuple-element.25), channel_id=1, source_target_pairs={{0,5},{1,4},{2,7},{3,6},{4,1},{5,0},{6,3},{7,2},{8,13},{9,12},{10,... | collective-permute-start | bytes 393224 | tf_op jit(solution)/shard_map/ppermute | solution.py:15
  147.5 6.7 %collective-permute-start.27 = (bf16[8,32,256]{2,1,0:T(8,128)(2,1)S(1)}, bf16[8,32,256]{2,1,0:T(8,128)(2,1)S(1)}, u32[]{:S(2)}, u32[]{:S(2)}) collective-permute-start(bf16[8,32,256]{2,1,0:T(8,128)(2,1)S(1)} %get-tuple-element.26), channel_id=1, source_target_pairs={{0,4},{1,5},{2,6},{3,7},{4,0},{5,1},{6,2},{7,3},{8,12},{9,13},{10,... | collective-permute-start | bytes 393224 | tf_op jit(solution)/shard_map/ppermute | solution.py:15
  165.0 6.9 %collective-permute-start.30 = (bf16[8,32,256]{2,1,0:T(8,128)(2,1)S(1)}, bf16[8,32,256]{2,1,0:T(8,128)(2,1)S(1)}, u32[]{:S(2)}, u32[]{:S(2)}) collective-permute-start(bf16[8,32,256]{2,1,0:T(8,128)(2,1)S(1)} %get-tuple-element.29), channel_id=1, source_target_pairs={{0,1},{1,0},{2,3},{3,2},{4,5},{5,4},{6,7},{7,6},{8,9},{9,8},{10,11... | collective-permute-start | bytes 393224 | tf_op jit(solution)/shard_map/ppermute | solution.py:15
  173.8 6.3 %collective-permute-start.36 = (bf16[8,32,256]{2,1,0:T(8,128)(2,1)S(1)}, bf16[8,32,256]{2,1,0:T(8,128)(2,1)S(1)}, u32[]{:S(2)}, u32[]{:S(2)}) collective-permute-start(bf16[8,32,256]{2,1,0:T(8,128)(2,1)S(1)} %get-tuple-element.36), channel_id=1, source_target_pairs={{0,2},{1,3},{2,0},{3,1},{4,6},{5,7},{6,4},{7,5},{8,10},{9,11},{10,... | collective-permute-start | bytes 393224 | tf_op jit(solution)/shard_map/ppermute | solution.py:15
  (23 other events, 211.9 us)

commit v2 on v0

v2 whole, which is shorter than its diff:
```python
import functools
import math

import jax
import jax.numpy as jnp
from jax import lax
from jax.experimental import pallas as pl
from jax.experimental.pallas import tpu as pltpu
from jax.sharding import PartitionSpec as P

IRREPS = 8


def xor_permute(value, axis, count, bits):
    return lax.ppermute(value, axis, [(i, i ^ bits) for i in range(count)])


def ladder_kernel(which, slab_at, part_counts, scalars, piece_ref, *refs):
    part_refs, (ladder_ref, masked_ref, assembled, joined) = refs[:-4], refs[-4:]
    slab_refs, at, room = [], 0, 0
    for parts in part_counts:
        if parts == 1:
            slab_refs.append(part_refs[at])
        else:
            size = IRREPS // parts
            for k in range(parts):
                joined[room, k * size : (k + 1) * size] = part_refs[at + k][...]
            slab_refs.append(joined.at[room])
            room += 1
        at += parts
    blk_count, _, _, rows, slots = piece_ref.shape
    sym = scalars[IRREPS + which]
    whole_tiles = rows % 16 == 0
    row_ids = lax.broadcasted_iota(jnp.int32, (rows, slots), 0)
    col_ids = lax.broadcasted_iota(jnp.int32, (rows, slots), 1)

    def mask(h, carry):
        in_cols = col_ids < scalars[h ^ sym]
        for owner in range(blk_count):
            keep = in_cols & (row_ids < scalars[h] - owner * rows)
            block = jnp.where(keep, piece_ref[owner, which, h].astype(jnp.float32), 0.0)
            at = slice(owner * rows, (owner + 1) * rows)
            if whole_tiles:
                masked_ref[h, at, :] = block.astype(jnp.bfloat16)
            else:
                assembled[at, :] = block
        if not whole_tiles:
            masked_ref[h] = assembled[...].astype(jnp.bfloat16)
        return carry

    lax.fori_loop(0, IRREPS, mask, 0, unroll=2)

    def one_block(h, carry):
        acc = None
        for q, slab in enumerate(slab_refs):
            shift = scalars[slab_at + q]
            half = jnp.dot(
                slab[h], masked_ref[h ^ shift], preferred_element_type=jnp.float32
            ).astype(jnp.bfloat16)
            term = lax.dot_general(
                half, slab[h ^ sym], (((1,), (1,)), ((), ())), preferred_element_type=jnp.float32
            )
            acc = term if acc is None else acc + term
        ladder_ref[h] = acc
        return carry

    lax.fori_loop(0, IRREPS, one_block, 0, unroll=max(1, 32 // len(slab_refs)))


def ladder_call(scalars, which, slab_at, pieces, slabs):
    slots = pieces.shape[-1]
    vmem = pl.BlockSpec(memory_space=pltpu.VMEM)
    flops = IRREPS * 2 * len(slabs) * 2 * slots**3
    parts = [part for slab in slabs for part in slab]
    part_counts = [len(slab) for slab in slabs]
    rooms = max(1, sum(count > 1 for count in part_counts))
    return pl.pallas_call(
        functools.partial(ladder_kernel, which, slab_at, part_counts),
        out_shape=[
            jax.ShapeDtypeStruct((IRREPS, slots, slots), jnp.float32),
            jax.ShapeDtypeStruct((IRREPS, slots, slots), jnp.bfloat16),
        ],
        in_specs=[pl.BlockSpec(memory_space=pltpu.SMEM)] + [vmem] * (1 + len(parts)),
        out_specs=[vmem] * 2,
        scratch_shapes=[
            pltpu.VMEM((slots, slots), jnp.float32),
            pltpu.VMEM((rooms, IRREPS, slots, slots), jnp.bfloat16),
        ],
        compiler_params=pltpu.CompilerParams(vmem_limit_bytes=20 * 1024 * 1024),
        cost_estimate=pl.CostEstimate(
            flops=flops, bytes_accessed=10 * 1024 * 1024, transcendentals=0
        ),
    )(scalars, pieces, *parts)


def dress_kernel(per_dev, core_at, scalars, same_ref, other_ref, *refs):
    ladder_refs, masked_refs = refs[: 2 * per_dev : 2], refs[1 : 2 * per_dev : 2]
    out_ref, coupling = refs[2 * per_dev :]
    blk_count, _, _, rows, slots = out_ref.shape
    core = scalars[core_at]
    half = same_ref.shape[0]
    for k in range(half):
        coupling[core * half + k] = same_ref[k]
        coupling[(1 - core) * half + k] = other_ref[k]
    row_ids = lax.broadcasted_iota(jnp.int32, (slots, slots), 0)
    col_ids = lax.broadcasted_iota(jnp.int32, (slots, slots), 1)

    def one_block(h, carry):
        for j in range(per_dev):
            col = h ^ scalars[IRREPS + j]
            block = masked_refs[j][h]
            acc = ladder_refs[j][h]
            acc += jnp.dot(block, coupling[col], preferred_element_type=jnp.float32)
            acc += jnp.dot(coupling[h], block, preferred_element_type=jnp.float32)
            keep = (row_ids < scalars[h]) & (col_ids < scalars[col])
            acc = jnp.where(keep, acc, 0.0)
            for owner in range(blk_count):
                part = acc[owner * rows : (owner + 1) * rows, :]
                out_ref[owner, j, h] = part.astype(jnp.bfloat16)
        return carry

    lax.fori_loop(0, IRREPS, one_block, 0, unroll=2)


def dress_call(scalars, core_at, blk_count, ladders, same_core, other_core):
    per_dev, slots = len(ladders), same_core.shape[-1]
    vmem = pl.BlockSpec(memory_space=pltpu.VMEM)
    return pl.pallas_call(
        functools.partial(dress_kernel, per_dev, core_at),
        out_shape=jax.ShapeDtypeStruct(
            (blk_count, per_dev, IRREPS, slots // blk_count, slots), jnp.bfloat16
        ),
        in_specs=[pl.BlockSpec(memory_space=pltpu.SMEM)] + [vmem] * (2 + 2 * per_dev),
        out_specs=vmem,
        scratch_shapes=[pltpu.VMEM((IRREPS, slots, slots), jnp.bfloat16)],
        compiler_params=pltpu.CompilerParams(vmem_limit_bytes=20 * 1024 * 1024),
        cost_estimate=pl.CostEstimate(
            flops=per_dev * IRREPS * 4 * slots**3, bytes_accessed=8 * 1024 * 1024, transcendentals=0
        ),
    )(scalars, same_core, other_core, *[one for pair in ladders for one in pair])


def after(value, *others):
    return lax.optimization_barrier((value, *others))[0]


def factor_kernel(kept, came, out_ref):
    dims = (((0,), (0,)), ((), ()))
    for h in range(out_ref.shape[0]):
        total = lax.dot_general(kept[h, 0], kept[h, 1], dims, preferred_element_type=jnp.float32)
        total += lax.dot_general(came[h, 0], came[h, 1], dims, preferred_element_type=jnp.float32)
        out_ref[h] = total.astype(out_ref.dtype)


def plane_permute(value, grp_count, blk_count, dx, dy):
    perm = [
        (g * blk_count + b, (g ^ (2 * dx)) * blk_count + (b ^ dy))
        for g in range(grp_count)
        for b in range(blk_count)
    ]
    return lax.ppermute(value, ("grp", "blk"), perm)


def per_device(amplitudes, chol_vv, chol_irrep, pair_occ, occ_irrep, vir_count, ov_left, ov_right):
    blk_count = lax.axis_size("blk")
    grp_count = lax.axis_size("grp")
    pair_total, _, rows, slots = amplitudes.shape
    per_dev = pair_total // blk_count
    grp, blk = lax.axis_index("grp"), lax.axis_index("blk")

    by_dest = amplitudes.reshape(blk_count, per_dev, IRREPS, rows, slots)
    all_rows = lax.all_to_all(by_dest, "blk", split_axis=0, concat_axis=0, tiled=True)

    ov_rows = ov_left.shape[0]
    low_count = IRREPS // grp_count
    core, x, low = grp % 2, grp // 2, blk % low_count
    planes = [(dx, dy) for dx in range(grp_count // 2) for dy in range(low_count)]
    half = len(planes)
    factors = jnp.stack([ov_left, ov_right]).transpose(2, 0, 1, 3)
    kept = lax.dynamic_slice_in_dim(factors, core * half, half, 0)
    away = lax.dynamic_slice_in_dim(factors, (1 - core) * half, half, 0)
    came = xor_permute(away, "grp", grp_count, 1)
    vmem = pl.BlockSpec(memory_space=pltpu.VMEM)
    local = pl.pallas_call(
        factor_kernel,
        out_shape=jax.ShapeDtypeStruct((half, slots, slots), jnp.bfloat16),
        in_specs=[vmem] * 2,
        out_specs=vmem,
    )(kept, came)
    per_slab = chol_vv.shape[0]
    cut = IRREPS // 2

    def along_x(part):
        return [xor_permute(part, "grp", grp_count, 2 * s) for s in range(1, grp_count // 2)]

    def other_core_of(parts):
        return [xor_permute(part, "grp", grp_count, 1) for part in parts]

    first_half = along_x(chol_vv[:, :cut])

    parts = []
    for dx, dy in planes:
        at = (x ^ dx) * low_count + (low ^ dy)
        part = lax.dynamic_index_in_dim(local, at, 0, keepdims=False)
        if dx or dy:
            part = plane_permute(part, grp_count, blk_count, dx, dy)
        parts.append(part.astype(jnp.float32))
    total = sum(parts).astype(jnp.bfloat16)
    total = after(total, *first_half)
    second_half = along_x(after(chol_vv[:, cut:], total))
    same = [(chol_vv,)] + list(zip(first_half, second_half))
    own_other = other_core_of([chol_vv])
    other = [(own_other[0],)] + list(zip(other_core_of(first_half), other_core_of(second_half)))

    bit = low_count
    while bit < blk_count:
        came = xor_permute(total, "blk", blk_count, bit)
        summed = total.astype(jnp.float32) + came.astype(jnp.float32)
        bit *= 2
        total = summed.astype(jnp.bfloat16)
    scale = 1.0 / math.sqrt(ov_rows * grp_count * blk_count)
    block = (summed * scale).astype(jnp.bfloat16)
    slabs, owners = [], []
    for s in range(grp_count // 2):
        for c, group in enumerate((same, other)):
            for k in range(per_slab):
                slabs.append([part[k] for part in group[s]])
                owners.append((grp ^ (2 * s + c)) * per_slab + k)
    slab_irreps = chol_irrep[jnp.stack(owners)]

    pair_start = (grp * blk_count + blk) * per_dev
    own_pairs = lax.dynamic_slice_in_dim(pair_occ, pair_start, per_dev, 0)
    occ_ids = jnp.arange(occ_irrep.shape[0], dtype=jnp.int32)
    one_hot = own_pairs[:, :, None] == occ_ids[None, None, :]
    labels = jnp.sum(jnp.where(one_hot, occ_irrep[None, None, :], 0), axis=2)
    pair_irrep = jnp.bitwise_xor(labels[:, 0], labels[:, 1])

    scalars = jnp.concatenate([vir_count, pair_irrep, slab_irreps, core[None].astype(jnp.int32)])
    slab_at = IRREPS + per_dev
    ladders = [ladder_call(scalars, j, slab_at, all_rows, slabs) for j in range(per_dev)]

    got = [
        plane_permute(block, grp_count, blk_count, dx, dy) if dx or dy else block
        for dx, dy in planes
    ]
    got, ladders[0] = lax.optimization_barrier((tuple(got), ladders[0]))
    same_core = jnp.zeros((half, slots, slots), jnp.bfloat16)
    for (dx, dy), one in zip(planes, got):
        at = (x ^ dx) * low_count + (low ^ dy)
        same_core = lax.dynamic_update_slice(same_core, one[None], (at, 0, 0))
    other_core = xor_permute(same_core, "grp", grp_count, 1)
    if per_dev > 1:
        other_core, ladders[1:] = lax.optimization_barrier((other_core, ladders[1:]))
    core_at = slab_at + len(slabs)
    sent = dress_call(scalars, core_at, blk_count, ladders, same_core, other_core)
    result = lax.all_to_all(sent, "blk", split_axis=0, concat_axis=0, tiled=True)
    return result.reshape(amplitudes.shape)


def solution(mesh):
    return jax.shard_map(
        per_device,
        mesh=mesh,
        in_specs=(
            P("grp", None, "blk", None),
            P("grp", None, None, None),
            P(),
            P(),
            P(),
            P(),
            P(("grp", "blk"), None, None),
            P(("grp", "blk"), None, None),
        ),
        out_specs=P("grp", None, "blk", None),
        check_vma=False,
    )
```

time: 322 us -> 139 us (0.43)
  waiting for transfers between devices: 161 us -> 30.9 us
  matrix products: 36.7 us -> 0 us
  local copies, waits for them, and re-layouts: 37.7 us -> 7.46 us
  starting transfers between devices: 7.47 us -> 28.4 us
  between operations: 14.9 us -> 0.16 us
  Pallas kernels: 0 us -> 14.6 us
  other arithmetic: 12.5 us -> 2.74 us
  blocking collectives: 50.6 us -> 54 us
    psum x1 -> x0, waiting for transfers between devices: 160 us -> none  [per_device(): coupling = lax.psum(local_sum, ('grp', 'blk'))]
    dot_general x7 -> x0, matrix products: 36.7 us -> none  [the longest x4 26.1 us: slab_terms(): jnp.einsum('phad,phbd->phab', half_product, right_tile, preferred_element...]
    ppermute x0 -> x15, waiting for transfers between devices: none -> 30.9 us  [the longest x9 15.6 us: xor_permute(): return lax.ppermute(value, axis, [(i, i ^ bits) for i in range(count)])]
    gather x14 -> x1, local copies, waits for them, and re-layouts: 27.2 us -> 0.64 us  [per_device(): slab_irreps = chol_irrep[jnp.stack(owners)]]
    ppermute x0 -> x15, starting transfers between devices: none -> 21 us  [the longest x9 14 us: xor_permute(): return lax.ppermute(value, axis, [(i, i ^ bits) for i in range(count)])]
    pallas_call x0 -> x4, Pallas kernels: none -> 14.6 us  [the longest x2 9.76 us: ladder_call(): pl.pallas_call(functools.partial(ladder_kernel, which, slab_at, part_coun...]
    mul x5 -> x0, other arithmetic: 6.96 us -> none  [the longest x4 6.27 us: slab_terms(): slab_tile * (slot_mask[:, :, None] * slot_mask[block_perm][:, None, :]).a...]
    all_to_all x2 -> x0, local copies, waits for them, and re-layouts: 3.9 us -> none  [the longest x1 2.1 us: per_device(): lax.all_to_all(result, 'blk', split_axis=2, concat_axis=0, tiled=True)]
  transfers between devices with their start and end apart: 3 -> 16, of which waited for: 1 -> 5; matrix products, arithmetic and copies ran while one was open for 3% -> 6% of each run, Pallas kernels for 0% -> 9%
where the time goes in v2:
time: 139 us; the launch traced here: 138 us
  blocking collectives  54 us (39%)
  waiting for transfers between devices  30.9 us (22%)
  starting transfers between devices  28.4 us (20%)
  Pallas kernels  14.6 us (11%)
  local copies, waits for them, and re-layouts  7.46 us (5%)
  other arithmetic  2.74 us (2%)
    all_to_all x1, blocking collectives, per_device(): lax.all_to_all(sent, 'blk', split_axis=0, concat_axis=0, tiled=True)  54 us
    ppermute x9, waiting for transfers between devices, xor_permute(): return lax.ppermute(value, axis, [(i, i ^ bits) for i in range(count)])  15.6 us
    ppermute x6, waiting for transfers between devices, plane_permute(): return lax.ppermute(value, ('grp', 'blk'), perm)  15.3 us
    ppermute x9, starting transfers between devices, xor_permute(): return lax.ppermute(value, axis, [(i, i ^ bits) for i in range(count)])  14 us
    pallas_call x2, Pallas kernels, ladder_call(): pl.pallas_call(functools.partial(ladder_kernel, which, slab_at, part_coun...  9.76 us
    all_to_all x1, starting transfers between devices, per_device(): lax.all_to_all(by_dest, 'blk', split_axis=0, concat_axis=0, tiled=True)  7.41 us
    ppermute x6, starting transfers between devices, plane_permute(): return lax.ppermute(value, ('grp', 'blk'), perm)  7.03 us
  transfers between devices with their start and end apart: 16, of which 5 were waited for; matrix products, arithmetic and copies ran while one was open for 6% of the time, Pallas kernels for 9%

profile of v2, /device:TPU:0, one launch (start us, length us, event | category | flops | bytes accessed | tf_op | source)
XLA Modules:
  0.0 138.3 jit_solution(8119369465041546904)
XLA Ops:
  0.0 7.4 %all-to-all-start = ((bf16[8,2,8,32,256]{4,3,2,1,0:T(8,128)(2,1)}), bf16[8,2,8,32,256]{4,3,2,1,0:T(8,128)(2,1)S(1)}, u32[]{:S(2)}, u32[]{:S(2)}) async-start(bf16[8,2,8,32,256]{4,3,2,1,0:T(8,128)(2,1)} %bitcast.43), calls=%async_computation | async-start | bytes 4194304 | tf_op jit(solution)/shard_map/all_to_all | solution.py:172
  7.4 1.5 %copy_bitcast_fusion = (bf16[1,128,8,256]{3,1,0,2:T(8,128)(2,1)S(1)}, bf16[1,128,8,256]{3,1,0,2:T(8,128)(2,1)S(1)}) fusion(bf16[128,8,256]{2,1,0:T(8,128)(2,1)} %param.15, bf16[128,8,256]{2,1,0:T(8,128)(2,1)} %param.14), kind=kLoop, calls=%fused_computation.9 | loop fusion | bytes 2097152 | tf_op jit(solution)/shard_map/stack | solution.py:179
  8.9 1.1 fusion.1
  10.0 1.0 fusion.9
  11.1 1.5 %collective-permute-start.4 = (bf16[1,4,256,256]{3,2,1,0:T(8,128)(2,1)}, bf16[1,4,256,256]{3,2,1,0:T(8,128)(2,1)}, u32[]{:S(2)}, u32[]{:S(2)}) collective-permute-start(bf16[1,4,256,256]{3,2,1,0:T(8,128)(2,1)} %get-tuple-element.36), channel_id=1, source_target_pairs={{0,16},{8,24},{16,0},{24,8},{1,17},{9,25},{17,1},{25,9},{2,18},{10... | collective-permute-start | bytes 1572872 | tf_op jit(solution)/shard_map/ppermute | solution.py:15
  12.6 2.5 %shard_map.82 = bf16[4,256,256]{2,1,0:T(8,128)(2,1)} custom-call(bf16[4,2,128,256]{3,2,1,0:T(8,128)(2,1)} %get-tuple-element.38.kept, bf16[4,2,128,256]{3,2,1,0:T(8,128)(2,1)} %collective-permute-done.came), custom_call_target="tpu_custom_call" | custom-call | tf_op jit(solution)/shard_map/pallas_call | solution.py:184
  15.0 1.8 %dynamic-slice_bitcast_fusion.2 = (bf16[256,256]{1,0:T(8,128)(2,1)}, bf16[256,256]{1,0:T(8,128)(2,1)S(1)}, bf16[256,256]{1,0:T(8,128)(2,1)}) fusion(bf16[4,256,256]{2,1,0:T(8,128)(2,1)} %shard_map.82, s32[]{:T(128)S(6)} %select_n.64, s32[]{:T(128)S(6)} %select_n.66, s32[]{:T(128)S(6)} %select_n.65), kind=kLoop, calls=%fused_computation.23 | loop fusion | bytes 786444 | tf_op jit(solution)/shard_map/jit(dynamic_index_in_dim)/squeeze | solution.py:204
  16.8 2.0 %collective-permute-start.1 = (bf16[256,256]{1,0:T(8,128)(2,1)}, bf16[256,256]{1,0:T(8,128)(2,1)S(1)}, u32[]{:S(2)}, u32[]{:S(2)}) collective-permute-start(bf16[256,256]{1,0:T(8,128)(2,1)} %get-tuple-element.39), channel_id=1, source_target_pairs={{0,1},{1,0},{2,3},{3,2},{4,5},{5,4},{6,7},{7,6},{8,9},{9,8},{10,11... | collective-permute-start | bytes 393224 | tf_op jit(solution)/shard_map/ppermute | solution.py:161
  18.8 1.2 collective-permute-start.2
  20.3 11.1 %collective-permute-done.1 = bf16[256,256]{1,0:T(8,128)(2,1)S(1)} collective-permute-done((bf16[256,256]{1,0:T(8,128)(2,1)}, bf16[256,256]{1,0:T(8,128)(2,1)S(1)}, u32[]{:S(2)}, u32[]{:S(2)}) %collective-permute-start.1) | collective-permute-done | bytes 131104 | tf_op jit(solution)/shard_map/ppermute | solution.py:161
  31.4 3.6 %collective-permute-done.3 = bf16[256,256]{1,0:T(8,128)(2,1)} collective-permute-done((bf16[256,256]{1,0:T(8,128)(2,1)S(1)}, bf16[256,256]{1,0:T(8,128)(2,1)}, u32[]{:S(2)}, u32[]{:S(2)}) %collective-permute-start.3) | collective-permute-done | bytes 131104 | tf_op jit(solution)/shard_map/ppermute | solution.py:161
  35.0 1.0 fusion.6
  36.0 1.6 %collective-permute-start.11 = (bf16[1,4,256,256]{3,2,1,0:T(8,128)(2,1)}, bf16[1,4,256,256]{3,2,1,0:T(8,128)(2,1)}, u32[]{:S(2)}, u32[]{:S(2)}) collective-permute-start(bf16[1,4,256,256]{3,2,1,0:T(8,128)(2,1)} %get-tuple-element.21), channel_id=1, source_target_pairs={{0,16},{8,24},{16,0},{24,8},{1,17},{9,25},{17,1},{25,9},{2,18},{10... | collective-permute-start | bytes 1572872 | tf_op jit(solution)/shard_map/ppermute | solution.py:15
  39.4 9.8 %collective-permute-done.11 = bf16[1,4,256,256]{3,2,1,0:T(8,128)(2,1)} collective-permute-done((bf16[1,4,256,256]{3,2,1,0:T(8,128)(2,1)}, bf16[1,4,256,256]{3,2,1,0:T(8,128)(2,1)}, u32[]{:S(2)}, u32[]{:S(2)}) %collective-permute-start.11) | collective-permute-done | bytes 524320 | tf_op jit(solution)/shard_map/ppermute | solution.py:15
  49.3 9.7 %collective-permute-start.6 = (bf16[256,256]{1,0:T(8,128)(2,1)S(1)}, bf16[256,256]{1,0:T(8,128)(2,1)S(1)}, u32[]{:S(2)}, u32[]{:S(2)}) collective-permute-start(bf16[256,256]{1,0:T(8,128)(2,1)S(1)} %add_convert_fusion), channel_id=1, source_target_pairs={{0,4},{1,5},{2,6},{3,7},{4,0},{5,1},{6,2},{7,3},{8,12},{9,13},{10,... | collective-permute-start | bytes 393224 | tf_op jit(solution)/shard_map/ppermute | solution.py:15
  59.7 5.8 %collective-permute-done.6 = bf16[256,256]{1,0:T(8,128)(2,1)S(1)} collective-permute-done((bf16[256,256]{1,0:T(8,128)(2,1)S(1)}, bf16[256,256]{1,0:T(8,128)(2,1)S(1)}, u32[]{:S(2)}, u32[]{:S(2)}) %collective-permute-start.6) | collective-permute-done | bytes 131104 | tf_op jit(solution)/shard_map/ppermute | solution.py:15
  65.6 1.6 %collective-permute-start.8 = (bf16[256,256]{1,0:T(8,128)(2,1)S(1)}, bf16[256,256]{1,0:T(8,128)(2,1)S(1)}, u32[]{:S(2)}, u32[]{:S(2)}) collective-permute-start(bf16[256,256]{1,0:T(8,128)(2,1)S(1)} %multiply_convert_fusion), channel_id=1, source_target_pairs={{0,16},{1,17},{2,18},{3,19},{4,20},{5,21},{6,22},{7,23},{8,24},{9,... | collective-permute-start | bytes 393224 | tf_op jit(solution)/shard_map/ppermute | solution.py:161
  67.2 1.9 %collective-permute-start.9 = (bf16[256,256]{1,0:T(8,128)(2,1)S(1)}, bf16[256,256]{1,0:T(8,128)(2,1)}, u32[]{:S(2)}, u32[]{:S(2)}) collective-permute-start(bf16[256,256]{1,0:T(8,128)(2,1)S(1)} %multiply_convert_fusion), channel_id=1, source_target_pairs={{0,17},{1,16},{2,19},{3,18},{4,21},{5,20},{6,23},{7,22},{8,25},{9,... | collective-permute-start | bytes 393224 | tf_op jit(solution)/shard_map/ppermute | solution.py:161
  69.1 4.9 %shard_map.83 = (f32[8,256,256]{2,1,0:T(8,128)S(1)}, bf16[8,256,256]{2,1,0:T(8,128)(2,1)S(1)}) custom-call(s32[15]{0:T(128)S(1)} %pad_add_fusion.scalars, bf16[8,2,8,32,256]{4,3,2,1,0:T(8,128)(2,1)S(1)} %all-to-all-done.piece_ref, bf16[8,256,256]{2,1,0:T(8,128)(2,1)S(1)} %bitcast.40, bf16[8,256,256]{2,1,0:T(8,128)(2,1)} %bitcast.16.refs_1_, ...), custom_call_target="tpu_custom_call" | custom-call | flops 2147483648 | bytes 10485760 | tf_op jit(solution)/shard_map/pallas_call | solution.py:77
  74.7 0.9 bitcast_dynamic-update-slice_fusion.same_ref
  75.7 4.9 %shard_map.84 = (f32[8,256,256]{2,1,0:T(8,128)S(1)}, bf16[8,256,256]{2,1,0:T(8,128)(2,1)S(1)}) custom-call(s32[15]{0:T(128)S(1)} %pad_add_fusion.scalars, bf16[8,2,8,32,256]{4,3,2,1,0:T(8,128)(2,1)S(1)} %all-to-all-done.piece_ref, bf16[8,256,256]{2,1,0:T(8,128)(2,1)S(1)} %bitcast.41, bf16[8,256,256]{2,1,0:T(8,128)(2,1)} %bitcast.16.refs_1_, ...), custom_call_target="tpu_custom_call" | custom-call | flops 2147483648 | bytes 10485760 | tf_op jit(solution)/shard_map/pallas_call | solution.py:77
  80.6 2.4 %shard_map.85 = bf16[8,2,8,32,256]{4,3,2,1,0:T(8,128)(2,1)S(1)} custom-call(s32[15]{0:T(128)S(1)} %pad_add_fusion.scalars, bf16[4,256,256]{2,1,0:T(8,128)(2,1)S(1)} %bitcast_dynamic-update-slice_fusion.same_ref, bf16[4,256,256]{2,1,0:T(8,128)(2,1)S(1)} %collective-permute-done.14.other_ref, f32[8,256,256]{2,1,0:T(8,128)S(1)} %get-tuple-element.31.refs_0_, ...), custom_call_target="tpu_custom_call" | custom-call | flops 1073741824 | bytes 8388608 | tf_op jit(solution)/shard_map/pallas_call | solution.py:128
  83.0 54.0 %all_to_all.10 = bf16[8,2,8,32,256]{4,3,2,1,0:T(8,128)(2,1)S(1)} all-to-all(bf16[8,2,8,32,256]{4,3,2,1,0:T(8,128)(2,1)S(1)} %shard_map.85), channel_id=1, replica_groups=mesh['grp'=4,'blk'=8] {'blk'}, dimensions={0} | all-to-all | bytes 4194304 | tf_op jit(solution)/shard_map/all_to_all | solution.py:256
  137.0 1.3 copy.28
  (44 shorter events, 3.8 us)
Async XLA Ops:
  0.0 37.6 %copy-start = (s32[64,2]{0,1:T(2,128)S(1)}, s32[64,2]{0,1:T(2,128)}, u32[]{:S(2)}) copy-start(s32[64,2]{0,1:T(2,128)} %param.11) | copy-start | bytes 1540
  0.0 69.1 %all-to-all-start = ((bf16[8,2,8,32,256]{4,3,2,1,0:T(8,128)(2,1)}), bf16[8,2,8,32,256]{4,3,2,1,0:T(8,128)(2,1)S(1)}, u32[]{:S(2)}, u32[]{:S(2)}) async-start(bf16[8,2,8,32,256]{4,3,2,1,0:T(8,128)(2,1)} %bitcast.43), calls=%async_computation | async-start | bytes 4194304 | tf_op jit(solution)/shard_map/all_to_all | solution.py:172
  7.4 2.6 %copy-start.1 = (bf16[1,8,256,256]{3,2,1,0:T(8,128)(2,1)S(1)}, bf16[1,8,256,256]{3,2,1,0:T(8,128)(2,1)}, u32[]{:S(2)}) copy-start(bf16[1,8,256,256]{3,2,1,0:T(8,128)(2,1)} %param.9) | copy-start | bytes 3145732
  10.0 27.7 %copy-start.3 = (s32[240]{0:T(256)S(1)}, s32[240]{0:T(256)}, u32[]{:S(2)}) copy-start(s32[240]{0:T(256)} %param.12) | copy-start | bytes 2884
  10.0 2.6 %collective-permute-start = (bf16[4,2,128,256]{3,2,1,0:T(8,128)(2,1)}, bf16[4,2,128,256]{3,2,1,0:T(8,128)(2,1)}, u32[]{:S(2)}, u32[]{:S(2)}) collective-permute-start(bf16[4,2,128,256]{3,2,1,0:T(8,128)(2,1)} %get-tuple-element.37), channel_id=1, source_target_pairs={{0,8},{8,0},{16,24},{24,16},{1,9},{9,1},{17,25},{25,17},{2,10},{10... | collective-permute-start | bytes 1572872 | tf_op jit(solution)/shard_map/ppermute | solution.py:15
  11.1 47.9 %copy-start.2 = (s32[4]{0:T(128)S(1)}, s32[4]{0:T(128)}, u32[]{:S(2)}) copy-start(s32[4]{0:T(128)} %param.10) | copy-start | bytes 52
  11.1 48.5 %copy-start.4 = (s32[8]{0:T(128)S(1)}, s32[8]{0:T(128)}, u32[]{:S(2)}) copy-start(s32[8]{0:T(128)} %param.13) | copy-start | bytes 100
  11.1 24.9 %collective-permute-start.4 = (bf16[1,4,256,256]{3,2,1,0:T(8,128)(2,1)}, bf16[1,4,256,256]{3,2,1,0:T(8,128)(2,1)}, u32[]{:S(2)}, u32[]{:S(2)}) collective-permute-start(bf16[1,4,256,256]{3,2,1,0:T(8,128)(2,1)} %get-tuple-element.36), channel_id=1, source_target_pairs={{0,16},{8,24},{16,0},{24,8},{1,17},{9,25},{17,1},{25,9},{2,18},{10... | collective-permute-start | bytes 1572872 | tf_op jit(solution)/shard_map/ppermute | solution.py:15
  16.8 14.6 %collective-permute-start.1 = (bf16[256,256]{1,0:T(8,128)(2,1)}, bf16[256,256]{1,0:T(8,128)(2,1)S(1)}, u32[]{:S(2)}, u32[]{:S(2)}) collective-permute-start(bf16[256,256]{1,0:T(8,128)(2,1)} %get-tuple-element.39), channel_id=1, source_target_pairs={{0,1},{1,0},{2,3},{3,2},{4,5},{5,4},{6,7},{7,6},{8,9},{9,8},{10,11... | collective-permute-start | bytes 393224 | tf_op jit(solution)/shard_map/ppermute | solution.py:161
  18.8 12.6 %collective-permute-start.2 = (bf16[256,256]{1,0:T(8,128)(2,1)}, bf16[256,256]{1,0:T(8,128)(2,1)S(1)}, u32[]{:S(2)}, u32[]{:S(2)}) collective-permute-start(bf16[256,256]{1,0:T(8,128)(2,1)} %get-tuple-element.41), channel_id=1, source_target_pairs={{0,16},{1,17},{2,18},{3,19},{4,20},{5,21},{6,22},{7,23},{8,24},{9,... | collective-permute-start | bytes 393224 | tf_op jit(solution)/shard_map/ppermute | solution.py:161
  20.0 15.0 %collective-permute-start.3 = (bf16[256,256]{1,0:T(8,128)(2,1)S(1)}, bf16[256,256]{1,0:T(8,128)(2,1)}, u32[]{:S(2)}, u32[]{:S(2)}) collective-permute-start(bf16[256,256]{1,0:T(8,128)(2,1)S(1)} %get-tuple-element.40), channel_id=1, source_target_pairs={{0,17},{1,16},{2,19},{3,18},{4,21},{5,20},{6,23},{7,22},{8,25},{9,... | collective-permute-start | bytes 393224 | tf_op jit(solution)/shard_map/ppermute | solution.py:161
  36.0 13.2 %collective-permute-start.11 = (bf16[1,4,256,256]{3,2,1,0:T(8,128)(2,1)}, bf16[1,4,256,256]{3,2,1,0:T(8,128)(2,1)}, u32[]{:S(2)}, u32[]{:S(2)}) collective-permute-start(bf16[1,4,256,256]{3,2,1,0:T(8,128)(2,1)} %get-tuple-element.21), channel_id=1, source_target_pairs={{0,16},{8,24},{16,0},{24,8},{1,17},{9,25},{17,1},{25,9},{2,18},{10... | collective-permute-start | bytes 1572872 | tf_op jit(solution)/shard_map/ppermute | solution.py:15
  37.6 31.5 %collective-permute-start.10 = (bf16[1,8,256,256]{3,2,1,0:T(8,128)(2,1)S(1)}, bf16[1,8,256,256]{3,2,1,0:T(8,128)(2,1)}, u32[]{:S(2)}, u32[]{:S(2)}) collective-permute-start(bf16[1,8,256,256]{3,2,1,0:T(8,128)(2,1)S(1)} %copy-done.1), channel_id=1, source_target_pairs={{0,8},{8,0},{16,24},{24,16},{1,9},{9,1},{17,25},{25,17},{2,10},{10... | collective-permute-start | bytes 3145736 | tf_op jit(solution)/shard_map/ppermute | solution.py:15
  38.0 11.3 %collective-permute-start.5 = (bf16[256,256]{1,0:T(8,128)(2,1)S(1)}, bf16[256,256]{1,0:T(8,128)(2,1)S(1)}, u32[]{:S(2)}, u32[]{:S(2)}) collective-permute-start(bf16[256,256]{1,0:T(8,128)(2,1)S(1)} %fusion.6), channel_id=1, source_target_pairs={{0,2},{1,3},{2,0},{3,1},{4,6},{5,7},{6,4},{7,5},{8,10},{9,11},{10,... | collective-permute-start | bytes 393224 | tf_op jit(solution)/shard_map/ppermute | solution.py:15
  39.1 28.0 %collective-permute-start.12 = (bf16[1,4,256,256]{3,2,1,0:T(8,128)(2,1)}, bf16[1,4,256,256]{3,2,1,0:T(8,128)(2,1)}, u32[]{:S(2)}, u32[]{:S(2)}) collective-permute-start(bf16[1,4,256,256]{3,2,1,0:T(8,128)(2,1)} %collective-permute-done.4), channel_id=1, source_target_pairs={{0,8},{8,0},{16,24},{24,16},{1,9},{9,1},{17,25},{25,17},{2,10},{10... | collective-permute-start | bytes 1572872 | tf_op jit(solution)/shard_map/ppermute | solution.py:15
  49.2 19.9 %collective-permute-start.13 = (bf16[1,4,256,256]{3,2,1,0:T(8,128)(2,1)}, bf16[1,4,256,256]{3,2,1,0:T(8,128)(2,1)}, u32[]{:S(2)}, u32[]{:S(2)}) collective-permute-start(bf16[1,4,256,256]{3,2,1,0:T(8,128)(2,1)} %collective-permute-done.11), channel_id=1, source_target_pairs={{0,8},{8,0},{16,24},{24,16},{1,9},{9,1},{17,25},{25,17},{2,10},{10... | collective-permute-start | bytes 1572872 | tf_op jit(solution)/shard_map/ppermute | solution.py:15
  49.3 16.2 %collective-permute-start.6 = (bf16[256,256]{1,0:T(8,128)(2,1)S(1)}, bf16[256,256]{1,0:T(8,128)(2,1)S(1)}, u32[]{:S(2)}, u32[]{:S(2)}) collective-permute-start(bf16[256,256]{1,0:T(8,128)(2,1)S(1)} %add_convert_fusion), channel_id=1, source_target_pairs={{0,4},{1,5},{2,6},{3,7},{4,0},{5,1},{6,2},{7,3},{8,12},{9,13},{10,... | collective-permute-start | bytes 393224 | tf_op jit(solution)/shard_map/ppermute | solution.py:15
  65.5 8.5 %collective-permute-start.7 = (bf16[256,256]{1,0:T(8,128)(2,1)S(1)}, bf16[256,256]{1,0:T(8,128)(2,1)S(1)}, u32[]{:S(2)}, u32[]{:S(2)}) collective-permute-start(bf16[256,256]{1,0:T(8,128)(2,1)S(1)} %multiply_convert_fusion), channel_id=1, source_target_pairs={{0,1},{1,0},{2,3},{3,2},{4,5},{5,4},{6,7},{7,6},{8,9},{9,8},{10,11... | collective-permute-start | bytes 393224 | tf_op jit(solution)/shard_map/ppermute | solution.py:161
  65.6 8.4 %collective-permute-start.8 = (bf16[256,256]{1,0:T(8,128)(2,1)S(1)}, bf16[256,256]{1,0:T(8,128)(2,1)S(1)}, u32[]{:S(2)}, u32[]{:S(2)}) collective-permute-start(bf16[256,256]{1,0:T(8,128)(2,1)S(1)} %multiply_convert_fusion), channel_id=1, source_target_pairs={{0,16},{1,17},{2,18},{3,19},{4,20},{5,21},{6,22},{7,23},{8,24},{9,... | collective-permute-start | bytes 393224 | tf_op jit(solution)/shard_map/ppermute | solution.py:161
  67.2 7.4 %collective-permute-start.9 = (bf16[256,256]{1,0:T(8,128)(2,1)S(1)}, bf16[256,256]{1,0:T(8,128)(2,1)}, u32[]{:S(2)}, u32[]{:S(2)}) collective-permute-start(bf16[256,256]{1,0:T(8,128)(2,1)S(1)} %multiply_convert_fusion), channel_id=1, source_target_pairs={{0,17},{1,16},{2,19},{3,18},{4,21},{5,20},{6,23},{7,22},{8,25},{9,... | collective-permute-start | bytes 393224 | tf_op jit(solution)/shard_map/ppermute | solution.py:161
  75.6 5.0 %collective-permute-start.14 = (bf16[4,256,256]{2,1,0:T(8,128)(2,1)S(1)}, bf16[4,256,256]{2,1,0:T(8,128)(2,1)S(1)}, u32[]{:S(2)}, u32[]{:S(2)}) collective-permute-start(bf16[4,256,256]{2,1,0:T(8,128)(2,1)S(1)} %bitcast_dynamic-update-slice_fusion.same_ref), channel_id=1, source_target_pairs={{0,8},{8,0},{16,24},{24,16},{1,9},{9,1},{17,25},{25,17},{2,10},{10... | collective-permute-start | bytes 1572872 | tf_op jit(solution)/shard_map/ppermute | solution.py:15

commit v3 on v2

--- a/solution.py
+++ b/solution.py
@@ -22,9 +22,10 @@
         if parts == 1:
             slab_refs.append(part_refs[at])
         else:
-            size = IRREPS // parts
-            for k in range(parts):
-                joined[room, k * size : (k + 1) * size] = part_refs[at + k][...]
+            begin = 0
+            for part in part_refs[at : at + parts]:
+                joined[room, begin : begin + part.shape[0]] = part[...]
+                begin += part.shape[0]
             slab_refs.append(joined.at[room])
             room += 1
         at += parts
@@ -35,15 +36,16 @@
     col_ids = lax.broadcasted_iota(jnp.int32, (rows, slots), 1)
 
     def mask(h, carry):
-        in_cols = col_ids < scalars[h ^ sym]
+        ones = jnp.where(col_ids < scalars[h ^ sym], 1.0, 0.0)
         for owner in range(blk_count):
-            keep = in_cols & (row_ids < scalars[h] - owner * rows)
-            block = jnp.where(keep, piece_ref[owner, which, h].astype(jnp.float32), 0.0)
+            in_rows = row_ids < scalars[h] - owner * rows
+            keep = jnp.where(in_rows, ones, 0.0).astype(jnp.bfloat16)
+            block = piece_ref[owner, which, h] * keep
             at = slice(owner * rows, (owner + 1) * rows)
             if whole_tiles:
-                masked_ref[h, at, :] = block.astype(jnp.bfloat16)
+                masked_ref[h, at, :] = block
             else:
-                assembled[at, :] = block
+                assembled[at, :] = block.astype(jnp.float32)
         if not whole_tiles:
             masked_ref[h] = assembled[...].astype(jnp.bfloat16)
         return carry
@@ -86,22 +88,24 @@
             pltpu.VMEM((slots, slots), jnp.float32),
             pltpu.VMEM((rooms, IRREPS, slots, slots), jnp.bfloat16),
         ],
-        compiler_params=pltpu.CompilerParams(vmem_limit_bytes=20 * 1024 * 1024),
+        compiler_params=pltpu.CompilerParams(vmem_limit_bytes=16 * 1024 * 1024),
         cost_estimate=pl.CostEstimate(
             flops=flops, bytes_accessed=10 * 1024 * 1024, transcendentals=0
         ),
     )(scalars, pieces, *parts)
 
 
-def dress_kernel(per_dev, core_at, scalars, same_ref, other_ref, *refs):
+def dress_kernel(per_dev, planes, scalars, same_ref, other_ref, *refs):
     ladder_refs, masked_refs = refs[: 2 * per_dev : 2], refs[1 : 2 * per_dev : 2]
-    out_ref, coupling = refs[2 * per_dev :]
-    blk_count, _, _, rows, slots = out_ref.shape
-    core = scalars[core_at]
-    half = same_ref.shape[0]
-    for k in range(half):
-        coupling[core * half + k] = same_ref[k]
-        coupling[(1 - core) * half + k] = other_ref[k]
+    out_refs, (coupling, total) = refs[2 * per_dev : -2], refs[-2:]
+    blk_count = len(out_refs)
+    _, _, rows, slots = out_refs[0].shape
+    blk = lax.axis_index("blk")
+    core = lax.axis_index("grp") % 2
+    half = len(planes)
+    for k, place in enumerate(plane_places(planes, IRREPS // lax.axis_size("grp"))):
+        coupling[core * half + place] = same_ref[k]
+        coupling[(1 - core) * half + place] = other_ref[k]
     row_ids = lax.broadcasted_iota(jnp.int32, (slots, slots), 0)
     col_ids = lax.broadcasted_iota(jnp.int32, (slots, slots), 1)
 
@@ -113,27 +117,31 @@
             acc += jnp.dot(block, coupling[col], preferred_element_type=jnp.float32)
             acc += jnp.dot(coupling[h], block, preferred_element_type=jnp.float32)
             keep = (row_ids < scalars[h]) & (col_ids < scalars[col])
-            acc = jnp.where(keep, acc, 0.0)
-            for owner in range(blk_count):
-                part = acc[owner * rows : (owner + 1) * rows, :]
-                out_ref[owner, j, h] = part.astype(jnp.bfloat16)
+            total[j] = jnp.where(keep, acc, 0.0)
+            for s, out_ref in enumerate(out_refs):
+                at = pl.ds(pl.multiple_of((blk ^ s) * rows, rows), rows)
+                out_ref[j, h] = total[j, at, :].astype(jnp.bfloat16)
         return carry
 
     lax.fori_loop(0, IRREPS, one_block, 0, unroll=2)
 
 
-def dress_call(scalars, core_at, blk_count, ladders, same_core, other_core):
+def dress_call(scalars, planes, blk_count, ladders, same_core, other_core):
     per_dev, slots = len(ladders), same_core.shape[-1]
     vmem = pl.BlockSpec(memory_space=pltpu.VMEM)
     return pl.pallas_call(
-        functools.partial(dress_kernel, per_dev, core_at),
-        out_shape=jax.ShapeDtypeStruct(
-            (blk_count, per_dev, IRREPS, slots // blk_count, slots), jnp.bfloat16
-        ),
+        functools.partial(dress_kernel, per_dev, planes),
+        out_shape=[
+            jax.ShapeDtypeStruct((per_dev, IRREPS, slots // blk_count, slots), jnp.bfloat16)
+        ]
+        * blk_count,
         in_specs=[pl.BlockSpec(memory_space=pltpu.SMEM)] + [vmem] * (2 + 2 * per_dev),
-        out_specs=vmem,
-        scratch_shapes=[pltpu.VMEM((IRREPS, slots, slots), jnp.bfloat16)],
-        compiler_params=pltpu.CompilerParams(vmem_limit_bytes=20 * 1024 * 1024),
+        out_specs=[vmem] * blk_count,
+        scratch_shapes=[
+            pltpu.VMEM((IRREPS, slots, slots), jnp.bfloat16),
+            pltpu.VMEM((per_dev, slots, slots), jnp.float32),
+        ],
+        compiler_params=pltpu.CompilerParams(vmem_limit_bytes=16 * 1024 * 1024),
         cost_estimate=pl.CostEstimate(
             flops=per_dev * IRREPS * 4 * slots**3, bytes_accessed=8 * 1024 * 1024, transcendentals=0
         ),
@@ -144,12 +152,17 @@
     return lax.optimization_barrier((value, *others))[0]
 
 
-def factor_kernel(kept, came, out_ref):
+def plane_places(planes, low_count):
+    x, low = lax.axis_index("grp") // 2, lax.axis_index("blk") % low_count
+    return [(x ^ dx) * low_count + (low ^ dy) for dx, dy in planes]
+
+
+def factor_kernel(planes, low_count, kept, came, *out_refs):
     dims = (((0,), (0,)), ((), ()))
-    for h in range(out_ref.shape[0]):
+    for h, out_ref in zip(plane_places(planes, low_count), out_refs):
         total = lax.dot_general(kept[h, 0], kept[h, 1], dims, preferred_element_type=jnp.float32)
         total += lax.dot_general(came[h, 0], came[h, 1], dims, preferred_element_type=jnp.float32)
-        out_ref[h] = total.astype(out_ref.dtype)
+        out_ref[...] = total.astype(out_ref.dtype)
 
 
 def plane_permute(value, grp_count, blk_count, dx, dy):
@@ -182,10 +195,11 @@
     came = xor_permute(away, "grp", grp_count, 1)
     vmem = pl.BlockSpec(memory_space=pltpu.VMEM)
     local = pl.pallas_call(
-        factor_kernel,
-        out_shape=jax.ShapeDtypeStruct((half, slots, slots), jnp.bfloat16),
+        functools.partial(factor_kernel, planes, low_count),
+        out_shape=[jax.ShapeDtypeStruct((slots, slots), jnp.bfloat16)] * half,
         in_specs=[vmem] * 2,
-        out_specs=vmem,
+        out_specs=[vmem] * half,
+        compiler_params=pltpu.CompilerParams(vmem_limit_bytes=8 * 1024 * 1024),
     )(kept, came)
     per_slab = chol_vv.shape[0]
     cut = IRREPS // 2
@@ -199,27 +213,27 @@
     first_half = along_x(chol_vv[:, :cut])
 
     parts = []
-    for dx, dy in planes:
-        at = (x ^ dx) * low_count + (low ^ dy)
-        part = lax.dynamic_index_in_dim(local, at, 0, keepdims=False)
+    for (dx, dy), part in zip(planes, local):
         if dx or dy:
             part = plane_permute(part, grp_count, blk_count, dx, dy)
         parts.append(part.astype(jnp.float32))
-    total = sum(parts).astype(jnp.bfloat16)
+    total = sum(parts)
     total = after(total, *first_half)
     second_half = along_x(after(chol_vv[:, cut:], total))
     same = [(chol_vv,)] + list(zip(first_half, second_half))
     own_other = other_core_of([chol_vv])
-    other = [(own_other[0],)] + list(zip(other_core_of(first_half), other_core_of(second_half)))
+    other = [(own_other[0],)]
+    for one, two in zip(first_half, second_half):
+        mid = two.shape[1] // 2
+        other.append(tuple(other_core_of([one, two[:, :mid], two[:, mid:]])))
 
     bit = low_count
     while bit < blk_count:
-        came = xor_permute(total, "blk", blk_count, bit)
-        summed = total.astype(jnp.float32) + came.astype(jnp.float32)
+        came = xor_permute(total.astype(jnp.bfloat16), "blk", blk_count, bit)
+        total = total + came.astype(jnp.float32)
         bit *= 2
-        total = summed.astype(jnp.bfloat16)
     scale = 1.0 / math.sqrt(ov_rows * grp_count * blk_count)
-    block = (summed * scale).astype(jnp.bfloat16)
+    block = (total * scale).astype(jnp.bfloat16)
     slabs, owners = [], []
     for s in range(grp_count // 2):
         for c, group in enumerate((same, other)):
@@ -235,7 +249,7 @@
     labels = jnp.sum(jnp.where(one_hot, occ_irrep[None, None, :], 0), axis=2)
     pair_irrep = jnp.bitwise_xor(labels[:, 0], labels[:, 1])
 
-    scalars = jnp.concatenate([vir_count, pair_irrep, slab_irreps, core[None].astype(jnp.int32)])
+    scalars = jnp.concatenate([vir_count, pair_irrep, slab_irreps])
     slab_at = IRREPS + per_dev
     ladders = [ladder_call(scalars, j, slab_at, all_rows, slabs) for j in range(per_dev)]
 
@@ -244,17 +258,19 @@
         for dx, dy in planes
     ]
     got, ladders[0] = lax.optimization_barrier((tuple(got), ladders[0]))
-    same_core = jnp.zeros((half, slots, slots), jnp.bfloat16)
-    for (dx, dy), one in zip(planes, got):
-        at = (x ^ dx) * low_count + (low ^ dy)
-        same_core = lax.dynamic_update_slice(same_core, one[None], (at, 0, 0))
+    same_core = jnp.stack(got)
     other_core = xor_permute(same_core, "grp", grp_count, 1)
     if per_dev > 1:
         other_core, ladders[1:] = lax.optimization_barrier((other_core, ladders[1:]))
-    core_at = slab_at + len(slabs)
-    sent = dress_call(scalars, core_at, blk_count, ladders, same_core, other_core)
-    result = lax.all_to_all(sent, "blk", split_axis=0, concat_axis=0, tiled=True)
-    return result.reshape(amplitudes.shape)
+    sent = dress_call(scalars, planes, blk_count, ladders, same_core, other_core)
+    result = jnp.zeros(amplitudes.shape, jnp.bfloat16)
+    result = lax.dynamic_update_slice(result, sent[0], (blk * per_dev, 0, 0, 0))
+    top = blk_count // 2
+    far, near = list(range(blk_count - 1, top - 1, -1)), list(range(top - 1, 0, -1))
+    for s in [s for two in zip(far, near + [0]) for s in two if s]:
+        came = xor_permute(sent[s], "blk", blk_count, s)
+        result = lax.dynamic_update_slice(result, came, ((blk ^ s) * per_dev, 0, 0, 0))
+    return result
 
 
 def solution(mesh):

time: 139 us -> 130 us (0.935)
  blocking collectives: 54 us -> 0 us
  waiting for transfers between devices: 30.9 us -> 70.9 us
  starting transfers between devices: 28.4 us -> 34.1 us
  other arithmetic: 2.74 us -> 4.99 us
  Pallas kernels: 14.6 us -> 13 us
    all_to_all x1 -> x0, blocking collectives: 54 us -> none  [per_device(): lax.all_to_all(sent, 'blk', split_axis=0, concat_axis=0, tiled=True)]
    ppermute x9 -> x17, waiting for transfers between devices: 15.6 us -> 53.8 us  [xor_permute(): return lax.ppermute(value, axis, [(i, i ^ bits) for i in range(count)])]
    ppermute x9 -> x17, starting transfers between devices: 14 us -> 19.7 us  [xor_permute(): return lax.ppermute(value, axis, [(i, i ^ bits) for i in range(count)])]
    ppermute x6, waiting for transfers between devices: 15.3 us -> 17.2 us  [plane_permute(): return lax.ppermute(value, ('grp', 'blk'), perm)]
    squeeze x1 -> x0, local copies, waits for them, and re-layouts: 1.75 us -> none  [per_device(): part = lax.dynamic_index_in_dim(local, at, 0, keepdims=False)]
  transfers between devices with their start and end apart: 16 -> 24, of which waited for: 5 -> 10; matrix products, arithmetic and copies ran while one was open for 6% -> 6% of each run, Pallas kernels for 9% -> 8%
where the time goes in v3:
time: 130 us; the launch traced here: 129 us
  waiting for transfers between devices  70.9 us (55%)
  starting transfers between devices  34.1 us (26%)
  Pallas kernels  13 us (10%)
  local copies, waits for them, and re-layouts  6.17 us (5%)
  other arithmetic  4.99 us (4%)
    ppermute x17, waiting for transfers between devices, xor_permute(): return lax.ppermute(value, axis, [(i, i ^ bits) for i in range(count)])  53.8 us
    ppermute x17, starting transfers between devices, xor_permute(): return lax.ppermute(value, axis, [(i, i ^ bits) for i in range(count)])  19.7 us
    ppermute x6, waiting for transfers between devices, plane_permute(): return lax.ppermute(value, ('grp', 'blk'), perm)  17.2 us
    pallas_call x2, Pallas kernels, ladder_call(): pl.pallas_call(functools.partial(ladder_kernel, which, slab_at, part_coun...  9.29 us
    all_to_all x1, starting transfers between devices, per_device(): lax.all_to_all(by_dest, 'blk', split_axis=0, concat_axis=0, tiled=True)  7.43 us
    ppermute x6, starting transfers between devices, plane_permute(): return lax.ppermute(value, ('grp', 'blk'), perm)  6.98 us
    pallas_call x1, Pallas kernels, dress_call(): pl.pallas_call(functools.partial(dress_kernel, per_dev, planes), out_shap...  2.7 us
  transfers between devices with their start and end apart: 24, of which 10 were waited for; matrix products, arithmetic and copies ran while one was open for 6% of the time, Pallas kernels for 8%

profile of v3, /device:TPU:0, one launch (start us, length us, event | category | flops | bytes accessed | tf_op | source)
XLA Modules:
  0.0 129.5 jit_solution(9938184903494300829)
XLA Ops:
  0.0 7.4 %all-to-all-start = ((bf16[8,2,8,32,256]{4,3,2,1,0:T(8,128)(2,1)}), bf16[8,2,8,32,256]{4,3,2,1,0:T(8,128)(2,1)S(1)}, u32[]{:S(2)}, u32[]{:S(2)}) async-start(bf16[8,2,8,32,256]{4,3,2,1,0:T(8,128)(2,1)} %bitcast.34), calls=%async_computation | async-start | bytes 4194304 | tf_op jit(solution)/shard_map/all_to_all | solution.py:185
  8.6 2.3 %fusion.7 = (bf16[1,4,256,256]{3,2,1,0:T(8,128)(2,1)}, bf16[1,4,256,256]{3,2,1,0:T(8,128)(2,1)}) fusion(bf16[1,8,256,256]{3,2,1,0:T(8,128)(2,1)} %param.9), kind=kLoop, calls=%fused_computation.32 | loop fusion | bytes 2097152 | tf_op jit(solution)/shard_map/slice | solution.py:222
  13.6 2.0 %collective-permute-start.1 = (bf16[256,256]{1,0:T(8,128)(2,1)}, bf16[256,256]{1,0:T(8,128)(2,1)S(1)}, u32[]{:S(2)}, u32[]{:S(2)}) collective-permute-start(bf16[256,256]{1,0:T(8,128)(2,1)} %get-tuple-element.33), channel_id=1, source_target_pairs={{0,1},{1,0},{2,3},{3,2},{4,5},{5,4},{6,7},{7,6},{8,9},{9,8},{10,11... | collective-permute-start | bytes 393224 | tf_op jit(solution)/shard_map/ppermute | solution.py:174
  17.4 14.0 %collective-permute-done.1 = bf16[256,256]{1,0:T(8,128)(2,1)S(1)} collective-permute-done((bf16[256,256]{1,0:T(8,128)(2,1)}, bf16[256,256]{1,0:T(8,128)(2,1)S(1)}, u32[]{:S(2)}, u32[]{:S(2)}) %collective-permute-start.1) | collective-permute-done | bytes 131104 | tf_op jit(solution)/shard_map/ppermute | solution.py:174
  31.4 3.2 %collective-permute-done.3 = bf16[256,256]{1,0:T(8,128)(2,1)S(1)} collective-permute-done((bf16[256,256]{1,0:T(8,128)(2,1)S(1)}, bf16[256,256]{1,0:T(8,128)(2,1)S(1)}, u32[]{:S(2)}, u32[]{:S(2)}) %collective-permute-start.3) | collective-permute-done | bytes 131104 | tf_op jit(solution)/shard_map/ppermute | solution.py:174
  34.7 1.6 %collective-permute-start.11 = (bf16[1,4,256,256]{3,2,1,0:T(8,128)(2,1)}, bf16[1,4,256,256]{3,2,1,0:T(8,128)(2,1)S(1)}, u32[]{:S(2)}, u32[]{:S(2)}) collective-permute-start(bf16[1,4,256,256]{3,2,1,0:T(8,128)(2,1)} %get-tuple-element.37), channel_id=1, source_target_pairs={{0,16},{8,24},{16,0},{24,8},{1,17},{9,25},{17,1},{25,9},{2,18},{10... | collective-permute-start | bytes 1572872 | tf_op jit(solution)/shard_map/ppermute | solution.py:15
  38.4 6.9 %collective-permute-done.5 = bf16[256,256]{1,0:T(8,128)(2,1)S(1)} collective-permute-done((bf16[256,256]{1,0:T(8,128)(2,1)}, bf16[256,256]{1,0:T(8,128)(2,1)S(1)}, u32[]{:S(2)}, u32[]{:S(2)}) %collective-permute-start.5) | collective-permute-done | bytes 131104 | tf_op jit(solution)/shard_map/ppermute | solution.py:15
  45.4 3.6 %collective-permute-start.6 = (bf16[256,256]{1,0:T(8,128)(2,1)S(1)}, bf16[256,256]{1,0:T(8,128)(2,1)S(1)}, u32[]{:S(2)}, u32[]{:S(2)}) collective-permute-start(bf16[256,256]{1,0:T(8,128)(2,1)S(1)} %fusion.4), channel_id=1, source_target_pairs={{0,4},{1,5},{2,6},{3,7},{4,0},{5,1},{6,2},{7,3},{8,12},{9,13},{10,... | collective-permute-start | bytes 393224 | tf_op jit(solution)/shard_map/ppermute | solution.py:15
  49.6 11.7 %collective-permute-done.6 = bf16[256,256]{1,0:T(8,128)(2,1)S(1)} collective-permute-done((bf16[256,256]{1,0:T(8,128)(2,1)S(1)}, bf16[256,256]{1,0:T(8,128)(2,1)S(1)}, u32[]{:S(2)}, u32[]{:S(2)}) %collective-permute-start.6) | collective-permute-done | bytes 131104 | tf_op jit(solution)/shard_map/ppermute | solution.py:15
  61.3 1.7 %multiply_convert_fusion = bf16[256,256]{1,0:T(8,128)(2,1)} fusion(bf16[256,256]{1,0:T(8,128)(2,1)S(1)} %collective-permute-done.6, f32[256,256]{1,0:T(8,128)} %copy-done.5, bf16[256,256]{1,0:T(8,128)(2,1)S(1)} %collective-permute-done.5), kind=kLoop, calls=%fused_computation.12 | loop fusion | flops 393216 | bytes 655360 | tf_op jit(solution)/shard_map/convert_element_type | solution.py:236
  64.4 1.5 %collective-permute-start.8 = (bf16[256,256]{1,0:T(8,128)(2,1)}, bf16[256,256]{1,0:T(8,128)(2,1)}, u32[]{:S(2)}, u32[]{:S(2)}) collective-permute-start(bf16[256,256]{1,0:T(8,128)(2,1)} %multiply_convert_fusion), channel_id=1, source_target_pairs={{0,16},{1,17},{2,18},{3,19},{4,20},{5,21},{6,22},{7,23},{8,24},{9,... | collective-permute-start | bytes 393224 | tf_op jit(solution)/shard_map/ppermute | solution.py:174
  68.1 4.7 %shard_map.83 = (f32[8,256,256]{2,1,0:T(8,128)S(1)}, bf16[8,256,256]{2,1,0:T(8,128)(2,1)S(1)}) custom-call(s32[14]{0:T(128)S(1)} %pad_add_fusion.scalars, bf16[8,2,8,32,256]{4,3,2,1,0:T(8,128)(2,1)S(1)} %all-to-all-done.piece_ref, bf16[8,256,256]{2,1,0:T(8,128)(2,1)} %bitcast.10.refs_0_, bf16[8,256,256]{2,1,0:T(8,128)(2,1)} %bitcast.11.refs_1_, ...), custom_call_target="tpu_custom_call" | custom-call | flops 2147483648 | bytes 10485760 | tf_op jit(solution)/shard_map/pallas_call | solution.py:79
  74.0 4.6 %shard_map.84 = (f32[8,256,256]{2,1,0:T(8,128)S(1)}, bf16[8,256,256]{2,1,0:T(8,128)(2,1)S(1)}) custom-call(s32[14]{0:T(128)S(1)} %pad_add_fusion.scalars, bf16[8,2,8,32,256]{4,3,2,1,0:T(8,128)(2,1)S(1)} %all-to-all-done.piece_ref, bf16[8,256,256]{2,1,0:T(8,128)(2,1)} %bitcast.10.refs_0_, bf16[8,256,256]{2,1,0:T(8,128)(2,1)} %bitcast.11.refs_1_, ...), custom_call_target="tpu_custom_call" | custom-call | flops 2147483648 | bytes 10485760 | tf_op jit(solution)/shard_map/pallas_call | solution.py:79
  78.7 2.7 %shard_map.85 = (bf16[2,8,32,256]{3,2,1,0:T(8,128)(2,1)S(1)}, bf16[2,8,32,256]{3,2,1,0:T(8,128)(2,1)S(1)}, bf16[2,8,32,256]{3,2,1,0:T(8,128)(2,1)S(1)}, bf16[2,8...) custom-call(s32[14]{0:T(128)S(1)} %pad_add_fusion.scalars, ...), custom_call_target="tpu_custom_call" | custom-call | flops 1073741824 | bytes 8388608 | tf_op jit(solution)/shard_map/pallas_call | solution.py:132
  81.4 2.4 %collective-permute-start.16 = (bf16[2,8,32,256]{3,2,1,0:T(8,128)(2,1)S(1)}, bf16[2,8,32,256]{3,2,1,0:T(8,128)(2,1)S(1)}, u32[]{:S(2)}, u32[]{:S(2)}) collective-permute-start(bf16[2,8,32,256]{3,2,1,0:T(8,128)(2,1)S(1)} %get-tuple-element.52), channel_id=1, source_target_pairs={{0,7},{1,6},{2,5},{3,4},{4,3},{5,2},{6,1},{7,0},{8,15},{9,14},{10,... | collective-permute-start | bytes 786440 | tf_op jit(solution)/shard_map/ppermute | solution.py:15
  83.8 2.3 %collective-permute-start.18 = (bf16[2,8,32,256]{3,2,1,0:T(8,128)(2,1)S(1)}, bf16[2,8,32,256]{3,2,1,0:T(8,128)(2,1)S(1)}, u32[]{:S(2)}, u32[]{:S(2)}) collective-permute-start(bf16[2,8,32,256]{3,2,1,0:T(8,128)(2,1)S(1)} %get-tuple-element.54), channel_id=1, source_target_pairs={{0,6},{1,7},{2,4},{3,5},{4,2},{5,3},{6,0},{7,1},{8,14},{9,15},{10,... | collective-permute-start | bytes 786440 | tf_op jit(solution)/shard_map/ppermute | solution.py:15
  87.3 1.7 %collective-permute-start.20 = (bf16[2,8,32,256]{3,2,1,0:T(8,128)(2,1)S(1)}, bf16[2,8,32,256]{3,2,1,0:T(8,128)(2,1)S(1)}, u32[]{:S(2)}, u32[]{:S(2)}) collective-permute-start(bf16[2,8,32,256]{3,2,1,0:T(8,128)(2,1)S(1)} %get-tuple-element.56), channel_id=1, source_target_pairs={{0,5},{1,4},{2,7},{3,6},{4,1},{5,0},{6,3},{7,2},{8,13},{9,12},{10,... | collective-permute-start | bytes 786440 | tf_op jit(solution)/shard_map/ppermute | solution.py:15
  89.3 4.0 %collective-permute-done.16 = bf16[2,8,32,256]{3,2,1,0:T(8,128)(2,1)S(1)} collective-permute-done((bf16[2,8,32,256]{3,2,1,0:T(8,128)(2,1)S(1)}, bf16[2,8,32,256]{3,2,1,0:T(8,128)(2,1)S(1)}, u32[]{:S(2)}, u32[]{:S(2)}) %collective-permute-start.16) | collective-permute-done | bytes 262176 | tf_op jit(solution)/shard_map/ppermute | solution.py:15
  94.8 3.9 %collective-permute-done.17 = bf16[2,8,32,256]{3,2,1,0:T(8,128)(2,1)S(1)} collective-permute-done((bf16[2,8,32,256]{3,2,1,0:T(8,128)(2,1)S(1)}, bf16[2,8,32,256]{3,2,1,0:T(8,128)(2,1)S(1)}, u32[]{:S(2)}, u32[]{:S(2)}) %collective-permute-start.17) | collective-permute-done | bytes 262176 | tf_op jit(solution)/shard_map/ppermute | solution.py:15
  98.7 2.6 %collective-permute-start.22 = (bf16[2,8,32,256]{3,2,1,0:T(8,128)(2,1)S(1)}, bf16[2,8,32,256]{3,2,1,0:T(8,128)(2,1)S(1)}, u32[]{:S(2)}, u32[]{:S(2)}) collective-permute-start(bf16[2,8,32,256]{3,2,1,0:T(8,128)(2,1)S(1)} %get-tuple-element.58), channel_id=1, source_target_pairs={{0,4},{1,5},{2,6},{3,7},{4,0},{5,1},{6,2},{7,3},{8,12},{9,13},{10,... | collective-permute-start | bytes 786440 | tf_op jit(solution)/shard_map/ppermute | solution.py:15
  101.3 5.6 %collective-permute-done.18 = bf16[2,8,32,256]{3,2,1,0:T(8,128)(2,1)S(1)} collective-permute-done((bf16[2,8,32,256]{3,2,1,0:T(8,128)(2,1)S(1)}, bf16[2,8,32,256]{3,2,1,0:T(8,128)(2,1)S(1)}, u32[]{:S(2)}, u32[]{:S(2)}) %collective-permute-start.18) | collective-permute-done | bytes 262176 | tf_op jit(solution)/shard_map/ppermute | solution.py:15
  106.9 8.8 %collective-permute-done.19 = bf16[2,8,32,256]{3,2,1,0:T(8,128)(2,1)S(1)} collective-permute-done((bf16[2,8,32,256]{3,2,1,0:T(8,128)(2,1)S(1)}, bf16[2,8,32,256]{3,2,1,0:T(8,128)(2,1)S(1)}, u32[]{:S(2)}, u32[]{:S(2)}) %collective-permute-start.19) | collective-permute-done | bytes 262176 | tf_op jit(solution)/shard_map/ppermute | solution.py:15
  115.7 9.2 %collective-permute-done.20 = bf16[2,8,32,256]{3,2,1,0:T(8,128)(2,1)S(1)} collective-permute-done((bf16[2,8,32,256]{3,2,1,0:T(8,128)(2,1)S(1)}, bf16[2,8,32,256]{3,2,1,0:T(8,128)(2,1)S(1)}, u32[]{:S(2)}, u32[]{:S(2)}) %collective-permute-start.20) | collective-permute-done | bytes 262176 | tf_op jit(solution)/shard_map/ppermute | solution.py:15
  125.0 3.7 %collective-permute-done.22 = bf16[2,8,32,256]{3,2,1,0:T(8,128)(2,1)S(1)} collective-permute-done((bf16[2,8,32,256]{3,2,1,0:T(8,128)(2,1)S(1)}, bf16[2,8,32,256]{3,2,1,0:T(8,128)(2,1)S(1)}, u32[]{:S(2)}, u32[]{:S(2)}) %collective-permute-start.22) | collective-permute-done | bytes 262176 | tf_op jit(solution)/shard_map/ppermute | solution.py:15
  (76 shorter events, 17.2 us)
Async XLA Ops:
  0.0 67.2 %all-to-all-start = ((bf16[8,2,8,32,256]{4,3,2,1,0:T(8,128)(2,1)}), bf16[8,2,8,32,256]{4,3,2,1,0:T(8,128)(2,1)S(1)}, u32[]{:S(2)}, u32[]{:S(2)}) async-start(bf16[8,2,8,32,256]{4,3,2,1,0:T(8,128)(2,1)} %bitcast.34), calls=%async_computation | async-start | bytes 4194304 | tf_op jit(solution)/shard_map/all_to_all | solution.py:185
  8.6 4.0 %collective-permute-start = (bf16[4,2,128,256]{3,2,1,0:T(8,128)(2,1)}, bf16[4,2,128,256]{3,2,1,0:T(8,128)(2,1)S(1)}, u32[]{:S(2)}, u32[]{:S(2)}) collective-permute-start(bf16[4,2,128,256]{3,2,1,0:T(8,128)(2,1)} %get-tuple-element.61), channel_id=1, source_target_pairs={{0,8},{8,0},{16,24},{24,16},{1,9},{9,1},{17,25},{25,17},{2,10},{10... | collective-permute-start | bytes 1572872 | tf_op jit(solution)/shard_map/ppermute | solution.py:15
  10.9 23.8 %collective-permute-start.4 = (bf16[1,4,256,256]{3,2,1,0:T(8,128)(2,1)}, bf16[1,4,256,256]{3,2,1,0:T(8,128)(2,1)}, u32[]{:S(2)}, u32[]{:S(2)}) collective-permute-start(bf16[1,4,256,256]{3,2,1,0:T(8,128)(2,1)} %get-tuple-element.60), channel_id=1, source_target_pairs={{0,16},{8,24},{16,0},{24,8},{1,17},{9,25},{17,1},{25,9},{2,18},{10... | collective-permute-start | bytes 1572872 | tf_op jit(solution)/shard_map/ppermute | solution.py:15
  12.4 53.5 %collective-permute-start.10 = (bf16[1,8,256,256]{3,2,1,0:T(8,128)(2,1)}, bf16[1,8,256,256]{3,2,1,0:T(8,128)(2,1)}, u32[]{:S(2)}, u32[]{:S(2)}) collective-permute-start(bf16[1,8,256,256]{3,2,1,0:T(8,128)(2,1)} %param.9), channel_id=1, source_target_pairs={{0,8},{8,0},{16,24},{24,16},{1,9},{9,1},{17,25},{25,17},{2,10},{10... | collective-permute-start | bytes 3145736 | tf_op jit(solution)/shard_map/ppermute | solution.py:15
  13.6 17.8 %collective-permute-start.1 = (bf16[256,256]{1,0:T(8,128)(2,1)}, bf16[256,256]{1,0:T(8,128)(2,1)S(1)}, u32[]{:S(2)}, u32[]{:S(2)}) collective-permute-start(bf16[256,256]{1,0:T(8,128)(2,1)} %get-tuple-element.33), channel_id=1, source_target_pairs={{0,1},{1,0},{2,3},{3,2},{4,5},{5,4},{6,7},{7,6},{8,9},{9,8},{10,11... | collective-permute-start | bytes 393224 | tf_op jit(solution)/shard_map/ppermute | solution.py:174
  15.6 15.8 %collective-permute-start.2 = (bf16[256,256]{1,0:T(8,128)(2,1)S(1)}, bf16[256,256]{1,0:T(8,128)(2,1)S(1)}, u32[]{:S(2)}, u32[]{:S(2)}) collective-permute-start(bf16[256,256]{1,0:T(8,128)(2,1)S(1)} %get-tuple-element.34), channel_id=1, source_target_pairs={{0,16},{1,17},{2,18},{3,19},{4,20},{5,21},{6,22},{7,23},{8,24},{9,... | collective-permute-start | bytes 393224 | tf_op jit(solution)/shard_map/ppermute | solution.py:174
  16.1 18.5 %collective-permute-start.3 = (bf16[256,256]{1,0:T(8,128)(2,1)S(1)}, bf16[256,256]{1,0:T(8,128)(2,1)S(1)}, u32[]{:S(2)}, u32[]{:S(2)}) collective-permute-start(bf16[256,256]{1,0:T(8,128)(2,1)S(1)} %get-tuple-element.35), channel_id=1, source_target_pairs={{0,17},{1,16},{2,19},{3,18},{4,21},{5,20},{6,23},{7,22},{8,25},{9,... | collective-permute-start | bytes 393224 | tf_op jit(solution)/shard_map/ppermute | solution.py:174
  34.7 14.2 %collective-permute-start.11 = (bf16[1,4,256,256]{3,2,1,0:T(8,128)(2,1)}, bf16[1,4,256,256]{3,2,1,0:T(8,128)(2,1)S(1)}, u32[]{:S(2)}, u32[]{:S(2)}) collective-permute-start(bf16[1,4,256,256]{3,2,1,0:T(8,128)(2,1)} %get-tuple-element.37), channel_id=1, source_target_pairs={{0,16},{8,24},{16,0},{24,8},{1,17},{9,25},{17,1},{25,9},{2,18},{10... | collective-permute-start | bytes 1572872 | tf_op jit(solution)/shard_map/ppermute | solution.py:15
  37.0 8.3 %collective-permute-start.5 = (bf16[256,256]{1,0:T(8,128)(2,1)}, bf16[256,256]{1,0:T(8,128)(2,1)S(1)}, u32[]{:S(2)}, u32[]{:S(2)}) collective-permute-start(bf16[256,256]{1,0:T(8,128)(2,1)} %convert_element_type.31), channel_id=1, source_target_pairs={{0,2},{1,3},{2,0},{3,1},{4,6},{5,7},{6,4},{7,5},{8,10},{9,11},{10,... | collective-permute-start | bytes 393224 | tf_op jit(solution)/shard_map/ppermute | solution.py:15
  38.4 26.1 %collective-permute-start.12 = (bf16[1,4,256,256]{3,2,1,0:T(8,128)(2,1)}, bf16[1,4,256,256]{3,2,1,0:T(8,128)(2,1)S(1)}, u32[]{:S(2)}, u32[]{:S(2)}) collective-permute-start(bf16[1,4,256,256]{3,2,1,0:T(8,128)(2,1)} %collective-permute-done.4), channel_id=1, source_target_pairs={{0,8},{8,0},{16,24},{24,16},{1,9},{9,1},{17,25},{25,17},{2,10},{10... | collective-permute-start | bytes 1572872 | tf_op jit(solution)/shard_map/ppermute | solution.py:15
  45.4 15.9 %collective-permute-start.6 = (bf16[256,256]{1,0:T(8,128)(2,1)S(1)}, bf16[256,256]{1,0:T(8,128)(2,1)S(1)}, u32[]{:S(2)}, u32[]{:S(2)}) collective-permute-start(bf16[256,256]{1,0:T(8,128)(2,1)S(1)} %fusion.4), channel_id=1, source_target_pairs={{0,4},{1,5},{2,6},{3,7},{4,0},{5,1},{6,2},{7,3},{8,12},{9,13},{10,... | collective-permute-start | bytes 393224 | tf_op jit(solution)/shard_map/ppermute | solution.py:15
  49.0 17.5 %collective-permute-start.13 = (bf16[1,2,256,256]{3,2,1,0:T(8,128)(2,1)S(1)}, bf16[1,2,256,256]{3,2,1,0:T(8,128)(2,1)S(1)}, u32[]{:S(2)}, u32[]{:S(2)}) collective-permute-start(bf16[1,2,256,256]{3,2,1,0:T(8,128)(2,1)S(1)} %get-tuple-element.64), channel_id=1, source_target_pairs={{0,8},{8,0},{16,24},{24,16},{1,9},{9,1},{17,25},{25,17},{2,10},{10... | collective-permute-start | bytes 786440 | tf_op jit(solution)/shard_map/ppermute | solution.py:15
  49.0 17.4 %collective-permute-start.14 = (bf16[1,2,256,256]{3,2,1,0:T(8,128)(2,1)S(1)}, bf16[1,2,256,256]{3,2,1,0:T(8,128)(2,1)S(1)}, u32[]{:S(2)}, u32[]{:S(2)}) collective-permute-start(bf16[1,2,256,256]{3,2,1,0:T(8,128)(2,1)S(1)} %get-tuple-element.63), channel_id=1, source_target_pairs={{0,8},{8,0},{16,24},{24,16},{1,9},{9,1},{17,25},{25,17},{2,10},{10... | collective-permute-start | bytes 786440 | tf_op jit(solution)/shard_map/ppermute | solution.py:15
  63.0 9.8 %collective-permute-start.7 = (bf16[256,256]{1,0:T(8,128)(2,1)}, bf16[256,256]{1,0:T(8,128)(2,1)S(1)}, u32[]{:S(2)}, u32[]{:S(2)}) collective-permute-start(bf16[256,256]{1,0:T(8,128)(2,1)} %multiply_convert_fusion), channel_id=1, source_target_pairs={{0,1},{1,0},{2,3},{3,2},{4,5},{5,4},{6,7},{7,6},{8,9},{9,8},{10,11... | collective-permute-start | bytes 393224 | tf_op jit(solution)/shard_map/ppermute | solution.py:174
  64.4 8.4 %collective-permute-start.8 = (bf16[256,256]{1,0:T(8,128)(2,1)}, bf16[256,256]{1,0:T(8,128)(2,1)}, u32[]{:S(2)}, u32[]{:S(2)}) collective-permute-start(bf16[256,256]{1,0:T(8,128)(2,1)} %multiply_convert_fusion), channel_id=1, source_target_pairs={{0,16},{1,17},{2,18},{3,19},{4,20},{5,21},{6,22},{7,23},{8,24},{9,... | collective-permute-start | bytes 393224 | tf_op jit(solution)/shard_map/ppermute | solution.py:174
  65.9 6.9 %collective-permute-start.9 = (bf16[256,256]{1,0:T(8,128)(2,1)}, bf16[256,256]{1,0:T(8,128)(2,1)}, u32[]{:S(2)}, u32[]{:S(2)}) collective-permute-start(bf16[256,256]{1,0:T(8,128)(2,1)} %multiply_convert_fusion), channel_id=1, source_target_pairs={{0,17},{1,16},{2,19},{3,18},{4,21},{5,20},{6,23},{7,22},{8,25},{9,... | collective-permute-start | bytes 393224 | tf_op jit(solution)/shard_map/ppermute | solution.py:174
  73.9 4.7 %collective-permute-start.15 = (bf16[4,256,256]{2,1,0:T(8,128)(2,1)S(1)}, bf16[4,256,256]{2,1,0:T(8,128)(2,1)S(1)}, u32[]{:S(2)}, u32[]{:S(2)}) collective-permute-start(bf16[4,256,256]{2,1,0:T(8,128)(2,1)S(1)} %pad_maximum_fusion.same_ref), channel_id=1, source_target_pairs={{0,8},{8,0},{16,24},{24,16},{1,9},{9,1},{17,25},{25,17},{2,10},{10... | collective-permute-start | bytes 1572872 | tf_op jit(solution)/shard_map/ppermute | solution.py:15
  81.4 12.0 %collective-permute-start.16 = (bf16[2,8,32,256]{3,2,1,0:T(8,128)(2,1)S(1)}, bf16[2,8,32,256]{3,2,1,0:T(8,128)(2,1)S(1)}, u32[]{:S(2)}, u32[]{:S(2)}) collective-permute-start(bf16[2,8,32,256]{3,2,1,0:T(8,128)(2,1)S(1)} %get-tuple-element.52), channel_id=1, source_target_pairs={{0,7},{1,6},{2,5},{3,4},{4,3},{5,2},{6,1},{7,0},{8,15},{9,14},{10,... | collective-permute-start | bytes 786440 | tf_op jit(solution)/shard_map/ppermute | solution.py:15
  83.8 14.9 %collective-permute-start.17 = (bf16[2,8,32,256]{3,2,1,0:T(8,128)(2,1)S(1)}, bf16[2,8,32,256]{3,2,1,0:T(8,128)(2,1)S(1)}, u32[]{:S(2)}, u32[]{:S(2)}) collective-permute-start(bf16[2,8,32,256]{3,2,1,0:T(8,128)(2,1)S(1)} %get-tuple-element.53), channel_id=1, source_target_pairs={{0,3},{1,2},{2,1},{3,0},{4,7},{5,6},{6,5},{7,4},{8,11},{9,10},{10,... | collective-permute-start | bytes 786440 | tf_op jit(solution)/shard_map/ppermute | solution.py:15
  83.8 23.1 %collective-permute-start.18 = (bf16[2,8,32,256]{3,2,1,0:T(8,128)(2,1)S(1)}, bf16[2,8,32,256]{3,2,1,0:T(8,128)(2,1)S(1)}, u32[]{:S(2)}, u32[]{:S(2)}) collective-permute-start(bf16[2,8,32,256]{3,2,1,0:T(8,128)(2,1)S(1)} %get-tuple-element.54), channel_id=1, source_target_pairs={{0,6},{1,7},{2,4},{3,5},{4,2},{5,3},{6,0},{7,1},{8,14},{9,15},{10,... | collective-permute-start | bytes 786440 | tf_op jit(solution)/shard_map/ppermute | solution.py:15
  86.2 29.6 %collective-permute-start.19 = (bf16[2,8,32,256]{3,2,1,0:T(8,128)(2,1)S(1)}, bf16[2,8,32,256]{3,2,1,0:T(8,128)(2,1)S(1)}, u32[]{:S(2)}, u32[]{:S(2)}) collective-permute-start(bf16[2,8,32,256]{3,2,1,0:T(8,128)(2,1)S(1)} %get-tuple-element.55), channel_id=1, source_target_pairs={{0,2},{1,3},{2,0},{3,1},{4,6},{5,7},{6,4},{7,5},{8,10},{9,11},{10,... | collective-permute-start | bytes 786440 | tf_op jit(solution)/shard_map/ppermute | solution.py:15
  87.3 37.6 %collective-permute-start.20 = (bf16[2,8,32,256]{3,2,1,0:T(8,128)(2,1)S(1)}, bf16[2,8,32,256]{3,2,1,0:T(8,128)(2,1)S(1)}, u32[]{:S(2)}, u32[]{:S(2)}) collective-permute-start(bf16[2,8,32,256]{3,2,1,0:T(8,128)(2,1)S(1)} %get-tuple-element.56), channel_id=1, source_target_pairs={{0,5},{1,4},{2,7},{3,6},{4,1},{5,0},{6,3},{7,2},{8,13},{9,12},{10,... | collective-permute-start | bytes 786440 | tf_op jit(solution)/shard_map/ppermute | solution.py:15
  93.3 31.6 %collective-permute-start.21 = (bf16[2,8,32,256]{3,2,1,0:T(8,128)(2,1)S(1)}, bf16[2,8,32,256]{3,2,1,0:T(8,128)(2,1)S(1)}, u32[]{:S(2)}, u32[]{:S(2)}) collective-permute-start(bf16[2,8,32,256]{3,2,1,0:T(8,128)(2,1)S(1)} %get-tuple-element.57), channel_id=1, source_target_pairs={{0,1},{1,0},{2,3},{3,2},{4,5},{5,4},{6,7},{7,6},{8,9},{9,8},{10,11... | collective-permute-start | bytes 786440 | tf_op jit(solution)/shard_map/ppermute | solution.py:15
  98.7 30.1 %collective-permute-start.22 = (bf16[2,8,32,256]{3,2,1,0:T(8,128)(2,1)S(1)}, bf16[2,8,32,256]{3,2,1,0:T(8,128)(2,1)S(1)}, u32[]{:S(2)}, u32[]{:S(2)}) collective-permute-start(bf16[2,8,32,256]{3,2,1,0:T(8,128)(2,1)S(1)} %get-tuple-element.58), channel_id=1, source_target_pairs={{0,4},{1,5},{2,6},{3,7},{4,0},{5,1},{6,2},{7,3},{8,12},{9,13},{10,... | collective-permute-start | bytes 786440 | tf_op jit(solution)/shard_map/ppermute | solution.py:15
  (11 other events, 132.1 us)

commit v4 on v3

--- a/solution.py
+++ b/solution.py
@@ -15,8 +15,7 @@
     return lax.ppermute(value, axis, [(i, i ^ bits) for i in range(count)])
 
 
-def ladder_kernel(which, slab_at, part_counts, scalars, piece_ref, *refs):
-    part_refs, (ladder_ref, masked_ref, assembled, joined) = refs[:-4], refs[-4:]
+def join_parts(part_counts, part_refs, joined):
     slab_refs, at, room = [], 0, 0
     for parts in part_counts:
         if parts == 1:
@@ -29,75 +28,95 @@
             slab_refs.append(joined.at[room])
             room += 1
         at += parts
-    blk_count, _, _, rows, slots = piece_ref.shape
-    sym = scalars[IRREPS + which]
+    return slab_refs
+
+
+def add_slabs(scalars, slab_at, slab_refs, masked_ref, ladder_ref, before_ref):
+    per_dev = masked_ref.shape[0]
+
+    def one_block(h, carry):
+        for j in range(per_dev):
+            col = h ^ scalars[IRREPS + j]
+            acc = None if before_ref is None else before_ref[j, h]
+            for q, slab in enumerate(slab_refs):
+                shift = scalars[slab_at + q]
+                half = jnp.dot(
+                    slab[h], masked_ref[j, h ^ shift], preferred_element_type=jnp.float32
+                ).astype(jnp.bfloat16)
+                term = lax.dot_general(
+                    half, slab[col], (((1,), (1,)), ((), ())), preferred_element_type=jnp.float32
+                )
+                acc = term if acc is None else acc + term
+            ladder_ref[j, h] = acc
+        return carry
+
+    lax.fori_loop(0, IRREPS, one_block, 0, unroll=max(1, 32 // (per_dev * len(slab_refs))))
+
+
+def first_kernel(slab_at, part_counts, scalars, piece_ref, *refs):
+    part_refs, (ladder_ref, masked_ref, assembled, joined) = refs[:-4], refs[-4:]
+    blk_count, per_dev, _, rows, slots = piece_ref.shape
     whole_tiles = rows % 16 == 0
     row_ids = lax.broadcasted_iota(jnp.int32, (rows, slots), 0)
     col_ids = lax.broadcasted_iota(jnp.int32, (rows, slots), 1)
 
     def mask(h, carry):
-        ones = jnp.where(col_ids < scalars[h ^ sym], 1.0, 0.0)
-        for owner in range(blk_count):
-            in_rows = row_ids < scalars[h] - owner * rows
-            keep = jnp.where(in_rows, ones, 0.0).astype(jnp.bfloat16)
-            block = piece_ref[owner, which, h] * keep
-            at = slice(owner * rows, (owner + 1) * rows)
-            if whole_tiles:
-                masked_ref[h, at, :] = block
-            else:
-                assembled[at, :] = block.astype(jnp.float32)
-        if not whole_tiles:
-            masked_ref[h] = assembled[...].astype(jnp.bfloat16)
+        for j in range(per_dev):
+            ones = jnp.where(col_ids < scalars[h ^ scalars[IRREPS + j]], 1.0, 0.0)
+            cols = ones.astype(jnp.bfloat16)
+            for owner in range(blk_count):
+                keep = cols
+                if (owner + 1) * rows > slots // 2:
+                    in_rows = row_ids < scalars[h] - owner * rows
+                    keep = jnp.where(in_rows, ones, 0.0).astype(jnp.bfloat16)
+                block = piece_ref[owner, j, h] * keep
+                at = slice(owner * rows, (owner + 1) * rows)
+                if whole_tiles:
+                    masked_ref[j, h, at, :] = block
+                else:
+                    assembled[at, :] = block.astype(jnp.float32)
+            if not whole_tiles:
+                masked_ref[j, h] = assembled[...].astype(jnp.bfloat16)
         return carry
 
     lax.fori_loop(0, IRREPS, mask, 0, unroll=2)
-
-    def one_block(h, carry):
-        acc = None
-        for q, slab in enumerate(slab_refs):
-            shift = scalars[slab_at + q]
-            half = jnp.dot(
-                slab[h], masked_ref[h ^ shift], preferred_element_type=jnp.float32
-            ).astype(jnp.bfloat16)
-            term = lax.dot_general(
-                half, slab[h ^ sym], (((1,), (1,)), ((), ())), preferred_element_type=jnp.float32
-            )
-            acc = term if acc is None else acc + term
-        ladder_ref[h] = acc
-        return carry
-
-    lax.fori_loop(0, IRREPS, one_block, 0, unroll=max(1, 32 // len(slab_refs)))
-
-
-def ladder_call(scalars, which, slab_at, pieces, slabs):
-    slots = pieces.shape[-1]
+    slab_refs = join_parts(part_counts, part_refs, joined)
+    add_slabs(scalars, slab_at, slab_refs, masked_ref, ladder_ref, None)
+
+
+def second_kernel(slab_at, part_counts, scalars, masked_ref, before_ref, *refs):
+    part_refs, (ladder_ref, joined) = refs[:-2], refs[-2:]
+    slab_refs = join_parts(part_counts, part_refs, joined)
+    add_slabs(scalars, slab_at, slab_refs, masked_ref, ladder_ref, before_ref)
+
+
+def ladder_call(kernel, slab_at, scalars, inputs, slabs, per_dev, slots):
     vmem = pl.BlockSpec(memory_space=pltpu.VMEM)
-    flops = IRREPS * 2 * len(slabs) * 2 * slots**3
     parts = [part for slab in slabs for part in slab]
     part_counts = [len(slab) for slab in slabs]
     rooms = max(1, sum(count > 1 for count in part_counts))
+    blocks = (per_dev, IRREPS, slots, slots)
+    ladder_shape = jax.ShapeDtypeStruct(blocks, jnp.float32)
+    joined = pltpu.VMEM((rooms, IRREPS, slots, slots), jnp.bfloat16)
+    first = kernel is first_kernel
     return pl.pallas_call(
-        functools.partial(ladder_kernel, which, slab_at, part_counts),
-        out_shape=[
-            jax.ShapeDtypeStruct((IRREPS, slots, slots), jnp.float32),
-            jax.ShapeDtypeStruct((IRREPS, slots, slots), jnp.bfloat16),
-        ],
-        in_specs=[pl.BlockSpec(memory_space=pltpu.SMEM)] + [vmem] * (1 + len(parts)),
-        out_specs=[vmem] * 2,
-        scratch_shapes=[
-            pltpu.VMEM((slots, slots), jnp.float32),
-            pltpu.VMEM((rooms, IRREPS, slots, slots), jnp.bfloat16),
-        ],
+        functools.partial(kernel, slab_at, part_counts),
+        out_shape=[ladder_shape, jax.ShapeDtypeStruct(blocks, jnp.bfloat16)] if first else ladder_shape,
+        in_specs=[pl.BlockSpec(memory_space=pltpu.SMEM)] + [vmem] * (len(inputs) + len(parts)),
+        out_specs=[vmem] * 2 if first else vmem,
+        scratch_shapes=[pltpu.VMEM((slots, slots), jnp.float32), joined] if first else [joined],
         compiler_params=pltpu.CompilerParams(vmem_limit_bytes=16 * 1024 * 1024),
         cost_estimate=pl.CostEstimate(
-            flops=flops, bytes_accessed=10 * 1024 * 1024, transcendentals=0
+            flops=per_dev * IRREPS * 2 * len(slabs) * 2 * slots**3,
+            bytes_accessed=10 * 1024 * 1024,
+            transcendentals=0,
         ),
-    )(scalars, pieces, *parts)
+    )(scalars, *inputs, *parts)
 
 
 def dress_kernel(per_dev, planes, scalars, same_ref, other_ref, *refs):
-    ladder_refs, masked_refs = refs[: 2 * per_dev : 2], refs[1 : 2 * per_dev : 2]
-    out_refs, (coupling, total) = refs[2 * per_dev : -2], refs[-2:]
+    ladder_ref, masked_ref = refs[:2]
+    out_refs, (coupling, total) = refs[2:-2], refs[-2:]
     blk_count = len(out_refs)
     _, _, rows, slots = out_refs[0].shape
     blk = lax.axis_index("blk")
@@ -112,8 +131,8 @@
     def one_block(h, carry):
         for j in range(per_dev):
             col = h ^ scalars[IRREPS + j]
-            block = masked_refs[j][h]
-            acc = ladder_refs[j][h]
+            block = masked_ref[j, h]
+            acc = ladder_ref[j, h]
             acc += jnp.dot(block, coupling[col], preferred_element_type=jnp.float32)
             acc += jnp.dot(coupling[h], block, preferred_element_type=jnp.float32)
             keep = (row_ids < scalars[h]) & (col_ids < scalars[col])
@@ -123,11 +142,11 @@
                 out_ref[j, h] = total[j, at, :].astype(jnp.bfloat16)
         return carry
 
-    lax.fori_loop(0, IRREPS, one_block, 0, unroll=2)
-
-
-def dress_call(scalars, planes, blk_count, ladders, same_core, other_core):
-    per_dev, slots = len(ladders), same_core.shape[-1]
+    lax.fori_loop(0, IRREPS, one_block, 0, unroll=4)
+
+
+def dress_call(scalars, planes, blk_count, ladder, masked, same_core, other_core):
+    per_dev, slots = ladder.shape[0], same_core.shape[-1]
     vmem = pl.BlockSpec(memory_space=pltpu.VMEM)
     return pl.pallas_call(
         functools.partial(dress_kernel, per_dev, planes),
@@ -135,7 +154,7 @@
             jax.ShapeDtypeStruct((per_dev, IRREPS, slots // blk_count, slots), jnp.bfloat16)
         ]
         * blk_count,
-        in_specs=[pl.BlockSpec(memory_space=pltpu.SMEM)] + [vmem] * (2 + 2 * per_dev),
+        in_specs=[pl.BlockSpec(memory_space=pltpu.SMEM)] + [vmem] * 4,
         out_specs=[vmem] * blk_count,
         scratch_shapes=[
             pltpu.VMEM((IRREPS, slots, slots), jnp.bfloat16),
@@ -145,7 +164,7 @@
         cost_estimate=pl.CostEstimate(
             flops=per_dev * IRREPS * 4 * slots**3, bytes_accessed=8 * 1024 * 1024, transcendentals=0
         ),
-    )(scalars, same_core, other_core, *[one for pair in ladders for one in pair])
+    )(scalars, same_core, other_core, ladder, masked)
 
 
 def after(value, *others):
@@ -227,13 +246,6 @@
         mid = two.shape[1] // 2
         other.append(tuple(other_core_of([one, two[:, :mid], two[:, mid:]])))
 
-    bit = low_count
-    while bit < blk_count:
-        came = xor_permute(total.astype(jnp.bfloat16), "blk", blk_count, bit)
-        total = total + came.astype(jnp.float32)
-        bit *= 2
-    scale = 1.0 / math.sqrt(ov_rows * grp_count * blk_count)
-    block = (total * scale).astype(jnp.bfloat16)
     slabs, owners = [], []
     for s in range(grp_count // 2):
         for c, group in enumerate((same, other)):
@@ -251,18 +263,32 @@
 
     scalars = jnp.concatenate([vir_count, pair_irrep, slab_irreps])
     slab_at = IRREPS + per_dev
-    ladders = [ladder_call(scalars, j, slab_at, all_rows, slabs) for j in range(per_dev)]
-
+    split = 2 * per_slab
+    ladder, masked = ladder_call(
+        first_kernel, slab_at, scalars, [all_rows], slabs[:split], per_dev, slots
+    )
+
+    bit = low_count
+    while bit < blk_count:
+        came = xor_permute(total.astype(jnp.bfloat16), "blk", blk_count, bit)
+        if 2 * bit >= blk_count:
+            came, ladder, masked = lax.optimization_barrier((came, ladder, masked))
+        total = total + came.astype(jnp.float32)
+        bit *= 2
+    scale = 1.0 / math.sqrt(ov_rows * grp_count * blk_count)
+    block = (total * scale).astype(jnp.bfloat16)
     got = [
         plane_permute(block, grp_count, blk_count, dx, dy) if dx or dy else block
         for dx, dy in planes
     ]
-    got, ladders[0] = lax.optimization_barrier((tuple(got), ladders[0]))
+    if slabs[split:]:
+        ladder = ladder_call(
+            second_kernel, slab_at + split, scalars, [masked, ladder], slabs[split:], per_dev, slots
+        )
+    got, ladder = lax.optimization_barrier((tuple(got), ladder))
     same_core = jnp.stack(got)
     other_core = xor_permute(same_core, "grp", grp_count, 1)
-    if per_dev > 1:
-        other_core, ladders[1:] = lax.optimization_barrier((other_core, ladders[1:]))
-    sent = dress_call(scalars, planes, blk_count, ladders, same_core, other_core)
+    sent = dress_call(scalars, planes, blk_count, ladder, masked, same_core, other_core)
     result = jnp.zeros(amplitudes.shape, jnp.bfloat16)
     result = lax.dynamic_update_slice(result, sent[0], (blk * per_dev, 0, 0, 0))
     top = blk_count // 2

time: 130 us -> 125 us (0.962)
  waiting for transfers between devices: 70.9 us -> 67.7 us
    ppermute x17, waiting for transfers between devices: 53.8 us -> 42.6 us  [xor_permute(): return lax.ppermute(value, axis, [(i, i ^ bits) for i in range(count)])]
    all_to_all x1, waiting for transfers between devices: 0.01 us -> 9.03 us  [per_device(): lax.all_to_all(by_dest, 'blk', split_axis=0, concat_axis=0, tiled=True)]
    unnamed x22 -> x16, local copies, waits for them, and re-layouts: 1.69 us -> 0.04 us
  transfers between devices with their start and end apart: 24 -> 24, of which waited for: 10 -> 13; matrix products, arithmetic and copies ran while one was open for 6% -> 8% of each run, Pallas kernels for 8% -> 8%
where the time goes in v4:
time: 125 us
  waiting for transfers between devices  67.7 us (54%)
  starting transfers between devices  34.4 us (28%)
  Pallas kernels  12.5 us (10%)
  local copies, waits for them, and re-layouts  5.74 us (5%)
  other arithmetic  4.54 us (4%)
    ppermute x17, waiting for transfers between devices, xor_permute(): return lax.ppermute(value, axis, [(i, i ^ bits) for i in range(count)])  42.6 us
    ppermute x17, starting transfers between devices, xor_permute(): return lax.ppermute(value, axis, [(i, i ^ bits) for i in range(count)])  20 us
    ppermute x6, waiting for transfers between devices, plane_permute(): return lax.ppermute(value, ('grp', 'blk'), perm)  16 us
    all_to_all x1, waiting for transfers between devices, per_device(): lax.all_to_all(by_dest, 'blk', split_axis=0, concat_axis=0, tiled=True)  9.03 us
    pallas_call x2, Pallas kernels, ladder_call(): pl.pallas_call(functools.partial(kernel, slab_at, part_counts), out_shape...  8.08 us
    all_to_all x1, starting transfers between devices, per_device(): lax.all_to_all(by_dest, 'blk', split_axis=0, concat_axis=0, tiled=True)  7.43 us
    ppermute x6, starting transfers between devices, plane_permute(): return lax.ppermute(value, ('grp', 'blk'), perm)  7.04 us
  transfers between devices with their start and end apart: 24, of which 13 were waited for; matrix products, arithmetic and copies ran while one was open for 8% of the time, Pallas kernels for 8%

profile of v4, /device:TPU:0, one launch (start us, length us, event | category | flops | bytes accessed | tf_op | source)
XLA Modules:
  0.0 125.1 jit_solution(6419468936385271601)
XLA Ops:
  0.0 7.4 %all-to-all-start = ((bf16[8,2,8,32,256]{4,3,2,1,0:T(8,128)(2,1)}), bf16[8,2,8,32,256]{4,3,2,1,0:T(8,128)(2,1)S(1)}, u32[]{:S(2)}, u32[]{:S(2)}) async-start(bf16[8,2,8,32,256]{4,3,2,1,0:T(8,128)(2,1)} %bitcast.29), calls=%async_computation | async-start | bytes 4194304 | tf_op jit(solution)/shard_map/all_to_all | solution.py:204
  9.1 2.2 %fusion.7 = (bf16[1,4,256,256]{3,2,1,0:T(8,128)(2,1)}, bf16[1,4,256,256]{3,2,1,0:T(8,128)(2,1)}) fusion(bf16[1,8,256,256]{3,2,1,0:T(8,128)(2,1)} %param.9), kind=kLoop, calls=%fused_computation.32 | loop fusion | bytes 2097152 | tf_op jit(solution)/shard_map/slice | solution.py:241
  13.0 2.0 %shard_map.82 = (bf16[256,256]{1,0:T(8,128)(2,1)S(1)}, bf16[256,256]{1,0:T(8,128)(2,1)}, bf16[256,256]{1,0:T(8,128)(2,1)S(1)}, bf16[256,256]{1,0:T(8,128)(2,1)S(1)}) custom-call(bf16[4,2,128,256]{3,2,1,0:T(8,128)(2,1)S(1)} %get-tuple-element.56.kept, bf16[4,2,128,256]{3,2,1,0:T(8,128)(2,1)} %collective-permute-done.came), custom_call_target="tpu_custom_call" | custom-call | tf_op jit(solution)/shard_map/pallas_call | solution.py:216
  15.0 2.0 %collective-permute-start.1 = (bf16[256,256]{1,0:T(8,128)(2,1)}, bf16[256,256]{1,0:T(8,128)(2,1)S(1)}, u32[]{:S(2)}, u32[]{:S(2)}) collective-permute-start(bf16[256,256]{1,0:T(8,128)(2,1)} %get-tuple-element.30), channel_id=1, source_target_pairs={{0,1},{1,0},{2,3},{3,2},{4,5},{5,4},{6,7},{7,6},{8,9},{9,8},{10,11... | collective-permute-start | bytes 393224 | tf_op jit(solution)/shard_map/ppermute | solution.py:193
  18.9 12.5 %collective-permute-done.1 = bf16[256,256]{1,0:T(8,128)(2,1)S(1)} collective-permute-done((bf16[256,256]{1,0:T(8,128)(2,1)}, bf16[256,256]{1,0:T(8,128)(2,1)S(1)}, u32[]{:S(2)}, u32[]{:S(2)}) %collective-permute-start.1) | collective-permute-done | bytes 131104 | tf_op jit(solution)/shard_map/ppermute | solution.py:193
  31.4 2.7 %collective-permute-done.3 = bf16[256,256]{1,0:T(8,128)(2,1)S(1)} collective-permute-done((bf16[256,256]{1,0:T(8,128)(2,1)S(1)}, bf16[256,256]{1,0:T(8,128)(2,1)S(1)}, u32[]{:S(2)}, u32[]{:S(2)}) %collective-permute-start.3) | collective-permute-done | bytes 131104 | tf_op jit(solution)/shard_map/ppermute | solution.py:193
  34.2 1.6 %collective-permute-start.11 = (bf16[1,4,256,256]{3,2,1,0:T(8,128)(2,1)}, bf16[1,4,256,256]{3,2,1,0:T(8,128)(2,1)S(1)}, u32[]{:S(2)}, u32[]{:S(2)}) collective-permute-start(bf16[1,4,256,256]{3,2,1,0:T(8,128)(2,1)} %get-tuple-element.39), channel_id=1, source_target_pairs={{0,16},{8,24},{16,0},{24,8},{1,17},{9,25},{17,1},{25,9},{2,18},{10... | collective-permute-start | bytes 1572872 | tf_op jit(solution)/shard_map/ppermute | solution.py:15
  39.3 6.0 %collective-permute-done.5 = bf16[256,256]{1,0:T(8,128)(2,1)S(1)} collective-permute-done((bf16[256,256]{1,0:T(8,128)(2,1)}, bf16[256,256]{1,0:T(8,128)(2,1)S(1)}, u32[]{:S(2)}, u32[]{:S(2)}) %collective-permute-start.5) | collective-permute-done | bytes 131104 | tf_op jit(solution)/shard_map/ppermute | solution.py:15
  46.0 3.5 %collective-permute-start.6 = (bf16[256,256]{1,0:T(8,128)(2,1)}, bf16[256,256]{1,0:T(8,128)(2,1)}, u32[]{:S(2)}, u32[]{:S(2)}) collective-permute-start(bf16[256,256]{1,0:T(8,128)(2,1)} %fusion.4), channel_id=1, source_target_pairs={{0,4},{1,5},{2,6},{3,7},{4,0},{5,1},{6,2},{7,3},{8,12},{9,13},{10,... | collective-permute-start | bytes 393224 | tf_op jit(solution)/shard_map/ppermute | solution.py:15
  50.9 9.0 %all-to-all-done.piece_ref = bf16[8,2,8,32,256]{4,3,2,1,0:T(8,128)(2,1)S(1)} async-done(((bf16[8,2,8,32,256]{4,3,2,1,0:T(8,128)(2,1)}), bf16[8,2,8,32,256]{4,3,2,1,0:T(8,128)(2,1)S(1)}, u32[]{:S(2)}, u32[]{:S(2)}) %all-to-all-start) | async-done | bytes 2097184 | tf_op jit(solution)/shard_map/all_to_all | solution.py:204
  59.9 4.4 %shard_map.83 = (f32[2,8,256,256]{3,2,1,0:T(8,128)S(1)}, bf16[2,8,256,256]{3,2,1,0:T(8,128)(2,1)S(1)}) custom-call(s32[14]{0:T(128)S(1)} %pad_add_fusion.scalars, bf16[8,2,8,32,256]{4,3,2,1,0:T(8,128)(2,1)S(1)} %all-to-all-done.piece_ref, bf16[8,256,256]{2,1,0:T(8,128)(2,1)} %bitcast.10.refs_0_, bf16[8,256,256]{2,1,0:T(8,128)(2,1)} %bitcast.11.refs_1_), custom_call_target="tpu_custom_call" | custom-call | flops 2147483648 | bytes 10485760 | tf_op jit(solution)/shard_map/pallas_call | solution.py:102
  65.3 2.1 %collective-permute-start.10 = (bf16[256,256]{1,0:T(8,128)(2,1)S(1)}, bf16[256,256]{1,0:T(8,128)(2,1)S(1)}, u32[]{:S(2)}, u32[]{:S(2)}) collective-permute-start(bf16[256,256]{1,0:T(8,128)(2,1)S(1)} %multiply_convert_fusion), channel_id=1, source_target_pairs={{0,17},{1,16},{2,19},{3,18},{4,21},{5,20},{6,23},{7,22},{8,25},{9,... | collective-permute-start | bytes 393224 | tf_op jit(solution)/shard_map/ppermute | solution.py:193
  68.9 3.6 %shard_map.84.refs_0_ = f32[2,8,256,256]{3,2,1,0:T(8,128)S(1)} custom-call(s32[14]{0:T(128)S(1)} %pad_add_fusion.scalars, bf16[2,8,256,256]{3,2,1,0:T(8,128)(2,1)S(1)} %get-tuple-element.37.masked_ref.refs_1_, f32[2,8,256,256]{3,2,1,0:T(8,128)S(1)} %get-tuple-element.38.before_ref, bf16[4,256,256]{2,1,0:T(8,128)(2,1)S(1)} %bitcast.27, ...), custom_call_target="tpu_custom_call" | custom-call | flops 2147483648 | bytes 10485760 | tf_op jit(solution)/shard_map/pallas_call | solution.py:102
  73.5 1.9 %collective-permute-done.15.other_ref = bf16[4,256,256]{2,1,0:T(8,128)(2,1)S(1)} collective-permute-done((bf16[4,256,256]{2,1,0:T(8,128)(2,1)S(1)}, bf16[4,256,256]{2,1,0:T(8,128)(2,1)S(1)}, u32[]{:S(2)}, u32[]{:S(2)}) %collective-permute-start.15) | collective-permute-done | bytes 524320 | tf_op jit(solution)/shard_map/ppermute | solution.py:15
  75.4 2.4 %shard_map.85 = (bf16[2,8,32,256]{3,2,1,0:T(8,128)(2,1)S(1)}, bf16[2,8,32,256]{3,2,1,0:T(8,128)(2,1)S(1)}, bf16[2,8,32,256]{3,2,1,0:T(8,128)(2,1)S(1)}, bf16[2,8...) custom-call(s32[14]{0:T(128)S(1)} %pad_add_fusion.scalars, ...), custom_call_target="tpu_custom_call" | custom-call | flops 1073741824 | bytes 8388608 | tf_op jit(solution)/shard_map/pallas_call | solution.py:151
  77.8 2.2 %collective-permute-start.16 = (bf16[2,8,32,256]{3,2,1,0:T(8,128)(2,1)S(1)}, bf16[2,8,32,256]{3,2,1,0:T(8,128)(2,1)S(1)}, u32[]{:S(2)}, u32[]{:S(2)}) collective-permute-start(bf16[2,8,32,256]{3,2,1,0:T(8,128)(2,1)S(1)} %get-tuple-element.46), channel_id=1, source_target_pairs={{0,7},{1,6},{2,5},{3,4},{4,3},{5,2},{6,1},{7,0},{8,15},{9,14},{10,... | collective-permute-start | bytes 786440 | tf_op jit(solution)/shard_map/ppermute | solution.py:15
  80.0 2.2 %collective-permute-start.18 = (bf16[2,8,32,256]{3,2,1,0:T(8,128)(2,1)S(1)}, bf16[2,8,32,256]{3,2,1,0:T(8,128)(2,1)S(1)}, u32[]{:S(2)}, u32[]{:S(2)}) collective-permute-start(bf16[2,8,32,256]{3,2,1,0:T(8,128)(2,1)S(1)} %get-tuple-element.48), channel_id=1, source_target_pairs={{0,6},{1,7},{2,4},{3,5},{4,2},{5,3},{6,0},{7,1},{8,14},{9,15},{10,... | collective-permute-start | bytes 786440 | tf_op jit(solution)/shard_map/ppermute | solution.py:15
  85.5 4.3 %collective-permute-done.16 = bf16[2,8,32,256]{3,2,1,0:T(8,128)(2,1)S(1)} collective-permute-done((bf16[2,8,32,256]{3,2,1,0:T(8,128)(2,1)S(1)}, bf16[2,8,32,256]{3,2,1,0:T(8,128)(2,1)S(1)}, u32[]{:S(2)}, u32[]{:S(2)}) %collective-permute-start.16) | collective-permute-done | bytes 262176 | tf_op jit(solution)/shard_map/ppermute | solution.py:15
  90.9 3.8 %collective-permute-done.17 = bf16[2,8,32,256]{3,2,1,0:T(8,128)(2,1)S(1)} collective-permute-done((bf16[2,8,32,256]{3,2,1,0:T(8,128)(2,1)S(1)}, bf16[2,8,32,256]{3,2,1,0:T(8,128)(2,1)S(1)}, u32[]{:S(2)}, u32[]{:S(2)}) %collective-permute-start.17) | collective-permute-done | bytes 262176 | tf_op jit(solution)/shard_map/ppermute | solution.py:15
  94.8 2.9 %collective-permute-start.22 = (bf16[2,8,32,256]{3,2,1,0:T(8,128)(2,1)S(1)}, bf16[2,8,32,256]{3,2,1,0:T(8,128)(2,1)S(1)}, u32[]{:S(2)}, u32[]{:S(2)}) collective-permute-start(bf16[2,8,32,256]{3,2,1,0:T(8,128)(2,1)S(1)} %get-tuple-element.52), channel_id=1, source_target_pairs={{0,4},{1,5},{2,6},{3,7},{4,0},{5,1},{6,2},{7,3},{8,12},{9,13},{10,... | collective-permute-start | bytes 786440 | tf_op jit(solution)/shard_map/ppermute | solution.py:15
  97.7 4.9 %collective-permute-done.18 = bf16[2,8,32,256]{3,2,1,0:T(8,128)(2,1)S(1)} collective-permute-done((bf16[2,8,32,256]{3,2,1,0:T(8,128)(2,1)S(1)}, bf16[2,8,32,256]{3,2,1,0:T(8,128)(2,1)S(1)}, u32[]{:S(2)}, u32[]{:S(2)}) %collective-permute-start.18) | collective-permute-done | bytes 262176 | tf_op jit(solution)/shard_map/ppermute | solution.py:15
  102.6 8.5 %collective-permute-done.19 = bf16[2,8,32,256]{3,2,1,0:T(8,128)(2,1)S(1)} collective-permute-done((bf16[2,8,32,256]{3,2,1,0:T(8,128)(2,1)S(1)}, bf16[2,8,32,256]{3,2,1,0:T(8,128)(2,1)S(1)}, u32[]{:S(2)}, u32[]{:S(2)}) %collective-permute-start.19) | collective-permute-done | bytes 262176 | tf_op jit(solution)/shard_map/ppermute | solution.py:15
  111.2 9.3 %collective-permute-done.20 = bf16[2,8,32,256]{3,2,1,0:T(8,128)(2,1)S(1)} collective-permute-done((bf16[2,8,32,256]{3,2,1,0:T(8,128)(2,1)S(1)}, bf16[2,8,32,256]{3,2,1,0:T(8,128)(2,1)S(1)}, u32[]{:S(2)}, u32[]{:S(2)}) %collective-permute-start.20) | collective-permute-done | bytes 262176 | tf_op jit(solution)/shard_map/ppermute | solution.py:15
  120.5 3.9 %collective-permute-done.22 = bf16[2,8,32,256]{3,2,1,0:T(8,128)(2,1)S(1)} collective-permute-done((bf16[2,8,32,256]{3,2,1,0:T(8,128)(2,1)S(1)}, bf16[2,8,32,256]{3,2,1,0:T(8,128)(2,1)S(1)}, u32[]{:S(2)}, u32[]{:S(2)}) %collective-permute-start.22) | collective-permute-done | bytes 262176 | tf_op jit(solution)/shard_map/ppermute | solution.py:15
  (70 shorter events, 19.3 us)
Async XLA Ops:
  0.0 59.9 %all-to-all-start = ((bf16[8,2,8,32,256]{4,3,2,1,0:T(8,128)(2,1)}), bf16[8,2,8,32,256]{4,3,2,1,0:T(8,128)(2,1)S(1)}, u32[]{:S(2)}, u32[]{:S(2)}) async-start(bf16[8,2,8,32,256]{4,3,2,1,0:T(8,128)(2,1)} %bitcast.29), calls=%async_computation | async-start | bytes 4194304 | tf_op jit(solution)/shard_map/all_to_all | solution.py:204
  8.6 4.4 %collective-permute-start = (bf16[4,2,128,256]{3,2,1,0:T(8,128)(2,1)}, bf16[4,2,128,256]{3,2,1,0:T(8,128)(2,1)}, u32[]{:S(2)}, u32[]{:S(2)}) collective-permute-start(bf16[4,2,128,256]{3,2,1,0:T(8,128)(2,1)} %get-tuple-element.55), channel_id=1, source_target_pairs={{0,8},{8,0},{16,24},{24,16},{1,9},{9,1},{17,25},{25,17},{2,10},{10... | collective-permute-start | bytes 1572872 | tf_op jit(solution)/shard_map/ppermute | solution.py:15
  8.6 42.3 %collective-permute-start.7 = (bf16[1,8,256,256]{3,2,1,0:T(8,128)(2,1)}, bf16[1,8,256,256]{3,2,1,0:T(8,128)(2,1)}, u32[]{:S(2)}, u32[]{:S(2)}) collective-permute-start(bf16[1,8,256,256]{3,2,1,0:T(8,128)(2,1)} %param.9), channel_id=1, source_target_pairs={{0,8},{8,0},{16,24},{24,16},{1,9},{9,1},{17,25},{25,17},{2,10},{10... | collective-permute-start | bytes 3145736 | tf_op jit(solution)/shard_map/ppermute | solution.py:15
  11.3 22.9 %collective-permute-start.4 = (bf16[1,4,256,256]{3,2,1,0:T(8,128)(2,1)}, bf16[1,4,256,256]{3,2,1,0:T(8,128)(2,1)S(1)}, u32[]{:S(2)}, u32[]{:S(2)}) collective-permute-start(bf16[1,4,256,256]{3,2,1,0:T(8,128)(2,1)} %get-tuple-element.54), channel_id=1, source_target_pairs={{0,16},{8,24},{16,0},{24,8},{1,17},{9,25},{17,1},{25,9},{2,18},{10... | collective-permute-start | bytes 1572872 | tf_op jit(solution)/shard_map/ppermute | solution.py:15
  15.0 16.4 %collective-permute-start.1 = (bf16[256,256]{1,0:T(8,128)(2,1)}, bf16[256,256]{1,0:T(8,128)(2,1)S(1)}, u32[]{:S(2)}, u32[]{:S(2)}) collective-permute-start(bf16[256,256]{1,0:T(8,128)(2,1)} %get-tuple-element.30), channel_id=1, source_target_pairs={{0,1},{1,0},{2,3},{3,2},{4,5},{5,4},{6,7},{7,6},{8,9},{9,8},{10,11... | collective-permute-start | bytes 393224 | tf_op jit(solution)/shard_map/ppermute | solution.py:193
  17.0 14.4 %collective-permute-start.2 = (bf16[256,256]{1,0:T(8,128)(2,1)S(1)}, bf16[256,256]{1,0:T(8,128)(2,1)S(1)}, u32[]{:S(2)}, u32[]{:S(2)}) collective-permute-start(bf16[256,256]{1,0:T(8,128)(2,1)S(1)} %get-tuple-element.31), channel_id=1, source_target_pairs={{0,16},{1,17},{2,18},{3,19},{4,20},{5,21},{6,22},{7,23},{8,24},{9,... | collective-permute-start | bytes 393224 | tf_op jit(solution)/shard_map/ppermute | solution.py:193
  17.6 16.6 %collective-permute-start.3 = (bf16[256,256]{1,0:T(8,128)(2,1)S(1)}, bf16[256,256]{1,0:T(8,128)(2,1)S(1)}, u32[]{:S(2)}, u32[]{:S(2)}) collective-permute-start(bf16[256,256]{1,0:T(8,128)(2,1)S(1)} %get-tuple-element.32), channel_id=1, source_target_pairs={{0,17},{1,16},{2,19},{3,18},{4,21},{5,20},{6,23},{7,22},{8,25},{9,... | collective-permute-start | bytes 393224 | tf_op jit(solution)/shard_map/ppermute | solution.py:193
  34.2 15.3 %collective-permute-start.11 = (bf16[1,4,256,256]{3,2,1,0:T(8,128)(2,1)}, bf16[1,4,256,256]{3,2,1,0:T(8,128)(2,1)S(1)}, u32[]{:S(2)}, u32[]{:S(2)}) collective-permute-start(bf16[1,4,256,256]{3,2,1,0:T(8,128)(2,1)} %get-tuple-element.39), channel_id=1, source_target_pairs={{0,16},{8,24},{16,0},{24,8},{1,17},{9,25},{17,1},{25,9},{2,18},{10... | collective-permute-start | bytes 1572872 | tf_op jit(solution)/shard_map/ppermute | solution.py:15
  36.5 8.8 %collective-permute-start.5 = (bf16[256,256]{1,0:T(8,128)(2,1)}, bf16[256,256]{1,0:T(8,128)(2,1)S(1)}, u32[]{:S(2)}, u32[]{:S(2)}) collective-permute-start(bf16[256,256]{1,0:T(8,128)(2,1)} %convert_element_type.31), channel_id=1, source_target_pairs={{0,2},{1,3},{2,0},{3,1},{4,6},{5,7},{6,4},{7,5},{8,10},{9,11},{10,... | collective-permute-start | bytes 393224 | tf_op jit(solution)/shard_map/ppermute | solution.py:15
  39.3 29.1 %collective-permute-start.12 = (bf16[1,4,256,256]{3,2,1,0:T(8,128)(2,1)S(1)}, bf16[1,4,256,256]{3,2,1,0:T(8,128)(2,1)}, u32[]{:S(2)}, u32[]{:S(2)}) collective-permute-start(bf16[1,4,256,256]{3,2,1,0:T(8,128)(2,1)S(1)} %collective-permute-done.4), channel_id=1, source_target_pairs={{0,8},{8,0},{16,24},{24,16},{1,9},{9,1},{17,25},{25,17},{2,10},{10... | collective-permute-start | bytes 1572872 | tf_op jit(solution)/shard_map/ppermute | solution.py:15
  46.0 18.3 %collective-permute-start.6 = (bf16[256,256]{1,0:T(8,128)(2,1)}, bf16[256,256]{1,0:T(8,128)(2,1)}, u32[]{:S(2)}, u32[]{:S(2)}) collective-permute-start(bf16[256,256]{1,0:T(8,128)(2,1)} %fusion.4), channel_id=1, source_target_pairs={{0,4},{1,5},{2,6},{3,7},{4,0},{5,1},{6,2},{7,3},{8,12},{9,13},{10,... | collective-permute-start | bytes 393224 | tf_op jit(solution)/shard_map/ppermute | solution.py:15
  50.3 18.5 %collective-permute-start.13 = (bf16[1,2,256,256]{3,2,1,0:T(8,128)(2,1)}, bf16[1,2,256,256]{3,2,1,0:T(8,128)(2,1)S(1)}, u32[]{:S(2)}, u32[]{:S(2)}) collective-permute-start(bf16[1,2,256,256]{3,2,1,0:T(8,128)(2,1)} %get-tuple-element.58), channel_id=1, source_target_pairs={{0,8},{8,0},{16,24},{24,16},{1,9},{9,1},{17,25},{25,17},{2,10},{10... | collective-permute-start | bytes 786440 | tf_op jit(solution)/shard_map/ppermute | solution.py:15
  50.3 18.5 %collective-permute-start.14 = (bf16[1,2,256,256]{3,2,1,0:T(8,128)(2,1)}, bf16[1,2,256,256]{3,2,1,0:T(8,128)(2,1)}, u32[]{:S(2)}, u32[]{:S(2)}) collective-permute-start(bf16[1,2,256,256]{3,2,1,0:T(8,128)(2,1)} %get-tuple-element.57), channel_id=1, source_target_pairs={{0,8},{8,0},{16,24},{24,16},{1,9},{9,1},{17,25},{25,17},{2,10},{10... | collective-permute-start | bytes 786440 | tf_op jit(solution)/shard_map/ppermute | solution.py:15
  65.3 7.2 %collective-permute-start.10 = (bf16[256,256]{1,0:T(8,128)(2,1)S(1)}, bf16[256,256]{1,0:T(8,128)(2,1)S(1)}, u32[]{:S(2)}, u32[]{:S(2)}) collective-permute-start(bf16[256,256]{1,0:T(8,128)(2,1)S(1)} %multiply_convert_fusion), channel_id=1, source_target_pairs={{0,17},{1,16},{2,19},{3,18},{4,21},{5,20},{6,23},{7,22},{8,25},{9,... | collective-permute-start | bytes 393224 | tf_op jit(solution)/shard_map/ppermute | solution.py:193
  67.4 5.7 %collective-permute-start.8 = (bf16[256,256]{1,0:T(8,128)(2,1)S(1)}, bf16[256,256]{1,0:T(8,128)(2,1)S(1)}, u32[]{:S(2)}, u32[]{:S(2)}) collective-permute-start(bf16[256,256]{1,0:T(8,128)(2,1)S(1)} %multiply_convert_fusion), channel_id=1, source_target_pairs={{0,1},{1,0},{2,3},{3,2},{4,5},{5,4},{6,7},{7,6},{8,9},{9,8},{10,11... | collective-permute-start | bytes 393224 | tf_op jit(solution)/shard_map/ppermute | solution.py:193
  68.3 5.0 %collective-permute-start.9 = (bf16[256,256]{1,0:T(8,128)(2,1)S(1)}, bf16[256,256]{1,0:T(8,128)(2,1)S(1)}, u32[]{:S(2)}, u32[]{:S(2)}) collective-permute-start(bf16[256,256]{1,0:T(8,128)(2,1)S(1)} %multiply_convert_fusion), channel_id=1, source_target_pairs={{0,16},{1,17},{2,18},{3,19},{4,20},{5,21},{6,22},{7,23},{8,24},{9,... | collective-permute-start | bytes 393224 | tf_op jit(solution)/shard_map/ppermute | solution.py:193
  73.4 2.0 %collective-permute-start.15 = (bf16[4,256,256]{2,1,0:T(8,128)(2,1)S(1)}, bf16[4,256,256]{2,1,0:T(8,128)(2,1)S(1)}, u32[]{:S(2)}, u32[]{:S(2)}) collective-permute-start(bf16[4,256,256]{2,1,0:T(8,128)(2,1)S(1)} %pad_maximum_fusion.same_ref), channel_id=1, source_target_pairs={{0,8},{8,0},{16,24},{24,16},{1,9},{9,1},{17,25},{25,17},{2,10},{10... | collective-permute-start | bytes 1572872 | tf_op jit(solution)/shard_map/ppermute | solution.py:15
  77.8 12.0 %collective-permute-start.16 = (bf16[2,8,32,256]{3,2,1,0:T(8,128)(2,1)S(1)}, bf16[2,8,32,256]{3,2,1,0:T(8,128)(2,1)S(1)}, u32[]{:S(2)}, u32[]{:S(2)}) collective-permute-start(bf16[2,8,32,256]{3,2,1,0:T(8,128)(2,1)S(1)} %get-tuple-element.46), channel_id=1, source_target_pairs={{0,7},{1,6},{2,5},{3,4},{4,3},{5,2},{6,1},{7,0},{8,15},{9,14},{10,... | collective-permute-start | bytes 786440 | tf_op jit(solution)/shard_map/ppermute | solution.py:15
  80.0 14.7 %collective-permute-start.17 = (bf16[2,8,32,256]{3,2,1,0:T(8,128)(2,1)S(1)}, bf16[2,8,32,256]{3,2,1,0:T(8,128)(2,1)S(1)}, u32[]{:S(2)}, u32[]{:S(2)}) collective-permute-start(bf16[2,8,32,256]{3,2,1,0:T(8,128)(2,1)S(1)} %get-tuple-element.47), channel_id=1, source_target_pairs={{0,3},{1,2},{2,1},{3,0},{4,7},{5,6},{6,5},{7,4},{8,11},{9,10},{10,... | collective-permute-start | bytes 786440 | tf_op jit(solution)/shard_map/ppermute | solution.py:15
  80.0 22.6 %collective-permute-start.18 = (bf16[2,8,32,256]{3,2,1,0:T(8,128)(2,1)S(1)}, bf16[2,8,32,256]{3,2,1,0:T(8,128)(2,1)S(1)}, u32[]{:S(2)}, u32[]{:S(2)}) collective-permute-start(bf16[2,8,32,256]{3,2,1,0:T(8,128)(2,1)S(1)} %get-tuple-element.48), channel_id=1, source_target_pairs={{0,6},{1,7},{2,4},{3,5},{4,2},{5,3},{6,0},{7,1},{8,14},{9,15},{10,... | collective-permute-start | bytes 786440 | tf_op jit(solution)/shard_map/ppermute | solution.py:15
  82.2 28.9 %collective-permute-start.19 = (bf16[2,8,32,256]{3,2,1,0:T(8,128)(2,1)S(1)}, bf16[2,8,32,256]{3,2,1,0:T(8,128)(2,1)S(1)}, u32[]{:S(2)}, u32[]{:S(2)}) collective-permute-start(bf16[2,8,32,256]{3,2,1,0:T(8,128)(2,1)S(1)} %get-tuple-element.49), channel_id=1, source_target_pairs={{0,2},{1,3},{2,0},{3,1},{4,6},{5,7},{6,4},{7,5},{8,10},{9,11},{10,... | collective-permute-start | bytes 786440 | tf_op jit(solution)/shard_map/ppermute | solution.py:15
  83.7 36.8 %collective-permute-start.20 = (bf16[2,8,32,256]{3,2,1,0:T(8,128)(2,1)S(1)}, bf16[2,8,32,256]{3,2,1,0:T(8,128)(2,1)S(1)}, u32[]{:S(2)}, u32[]{:S(2)}) collective-permute-start(bf16[2,8,32,256]{3,2,1,0:T(8,128)(2,1)S(1)} %get-tuple-element.50), channel_id=1, source_target_pairs={{0,5},{1,4},{2,7},{3,6},{4,1},{5,0},{6,3},{7,2},{8,13},{9,12},{10,... | collective-permute-start | bytes 786440 | tf_op jit(solution)/shard_map/ppermute | solution.py:15
  89.8 30.7 %collective-permute-start.21 = (bf16[2,8,32,256]{3,2,1,0:T(8,128)(2,1)S(1)}, bf16[2,8,32,256]{3,2,1,0:T(8,128)(2,1)S(1)}, u32[]{:S(2)}, u32[]{:S(2)}) collective-permute-start(bf16[2,8,32,256]{3,2,1,0:T(8,128)(2,1)S(1)} %get-tuple-element.51), channel_id=1, source_target_pairs={{0,1},{1,0},{2,3},{3,2},{4,5},{5,4},{6,7},{7,6},{8,9},{9,8},{10,11... | collective-permute-start | bytes 786440 | tf_op jit(solution)/shard_map/ppermute | solution.py:15
  94.8 29.6 %collective-permute-start.22 = (bf16[2,8,32,256]{3,2,1,0:T(8,128)(2,1)S(1)}, bf16[2,8,32,256]{3,2,1,0:T(8,128)(2,1)S(1)}, u32[]{:S(2)}, u32[]{:S(2)}) collective-permute-start(bf16[2,8,32,256]{3,2,1,0:T(8,128)(2,1)S(1)} %get-tuple-element.52), channel_id=1, source_target_pairs={{0,4},{1,5},{2,6},{3,7},{4,0},{5,1},{6,2},{7,3},{8,12},{9,13},{10,... | collective-permute-start | bytes 786440 | tf_op jit(solution)/shard_map/ppermute | solution.py:15
  (8 other events, 90.9 us)

commit v5 on v4

--- a/solution.py
+++ b/solution.py
@@ -37,16 +37,21 @@
     def one_block(h, carry):
         for j in range(per_dev):
             col = h ^ scalars[IRREPS + j]
-            acc = None if before_ref is None else before_ref[j, h]
+            halves = []
             for q, slab in enumerate(slab_refs):
                 shift = scalars[slab_at + q]
                 half = jnp.dot(
                     slab[h], masked_ref[j, h ^ shift], preferred_element_type=jnp.float32
-                ).astype(jnp.bfloat16)
-                term = lax.dot_general(
-                    half, slab[col], (((1,), (1,)), ((), ())), preferred_element_type=jnp.float32
                 )
-                acc = term if acc is None else acc + term
+                halves.append(half.astype(jnp.bfloat16))
+            acc = lax.dot_general(
+                jnp.concatenate(halves, axis=1),
+                jnp.concatenate([slab[col] for slab in slab_refs], axis=1),
+                (((1,), (1,)), ((), ())),
+                preferred_element_type=jnp.float32,
+            )
+            if before_ref is not None:
+                acc += before_ref[j, h]
             ladder_ref[j, h] = acc
         return carry
 
@@ -133,8 +138,11 @@
             col = h ^ scalars[IRREPS + j]
             block = masked_ref[j, h]
             acc = ladder_ref[j, h]
-            acc += jnp.dot(block, coupling[col], preferred_element_type=jnp.float32)
-            acc += jnp.dot(coupling[h], block, preferred_element_type=jnp.float32)
+            acc += jnp.dot(
+                jnp.concatenate([block, coupling[h]], axis=1),
+                jnp.concatenate([coupling[col], block], axis=0),
+                preferred_element_type=jnp.float32,
+            )
             keep = (row_ids < scalars[h]) & (col_ids < scalars[col])
             total[j] = jnp.where(keep, acc, 0.0)
             for s, out_ref in enumerate(out_refs):
@@ -264,14 +272,17 @@
     scalars = jnp.concatenate([vir_count, pair_irrep, slab_irreps])
     slab_at = IRREPS + per_dev
     split = 2 * per_slab
-    ladder, masked = ladder_call(
-        first_kernel, slab_at, scalars, [all_rows], slabs[:split], per_dev, slots
-    )
 
     bit = low_count
     while bit < blk_count:
-        came = xor_permute(total.astype(jnp.bfloat16), "blk", blk_count, bit)
+        sent = total.astype(jnp.bfloat16)
         if 2 * bit >= blk_count:
+            sent, all_rows = lax.optimization_barrier((sent, all_rows))
+        came = xor_permute(sent, "blk", blk_count, bit)
+        if 2 * bit >= blk_count:
+            ladder, masked = ladder_call(
+                first_kernel, slab_at, scalars, [all_rows], slabs[:split], per_dev, slots
+            )
             came, ladder, masked = lax.optimization_barrier((came, ladder, masked))
         total = total + came.astype(jnp.float32)
         bit *= 2
@@ -292,7 +303,7 @@
     result = jnp.zeros(amplitudes.shape, jnp.bfloat16)
     result = lax.dynamic_update_slice(result, sent[0], (blk * per_dev, 0, 0, 0))
     top = blk_count // 2
-    far, near = list(range(blk_count - 1, top - 1, -1)), list(range(top - 1, 0, -1))
+    far, near = list(range(top, blk_count)), list(range(1, top))
     for s in [s for two in zip(far, near + [0]) for s in two if s]:
         came = xor_permute(sent[s], "blk", blk_count, s)
         result = lax.dynamic_update_slice(result, came, ((blk ^ s) * per_dev, 0, 0, 0))

time: 125 us -> 125 us (level); the launches traced: 125 us -> 122 us
  starting transfers between devices: 34.4 us -> 28.7 us
  waiting for transfers between devices: 67.7 us -> 70 us
  local copies, waits for them, and re-layouts: 5.74 us -> 7.04 us
    ppermute x17, starting transfers between devices: 20 us -> 14.2 us  [xor_permute(): return lax.ppermute(value, axis, [(i, i ^ bits) for i in range(count)])]
    ppermute x17, waiting for transfers between devices: 42.6 us -> 44.6 us  [xor_permute(): return lax.ppermute(value, axis, [(i, i ^ bits) for i in range(count)])]
    unnamed x16, local copies, waits for them, and re-layouts: 0.04 us -> 1.33 us
    ppermute x6, waiting for transfers between devices: 16 us -> 17.3 us  [plane_permute(): return lax.ppermute(value, ('grp', 'blk'), perm)]
  transfers between devices with their start and end apart: 24 -> 24, of which waited for: 13 -> 12; matrix products, arithmetic and copies ran while one was open for 8% -> 7% of each run, Pallas kernels for 8% -> 8%
where the time goes in v5:
time: 125 us; the launch traced here: 122 us
  waiting for transfers between devices  70 us (56%)
  starting transfers between devices  28.7 us (23%)
  Pallas kernels  12.6 us (10%)
  local copies, waits for them, and re-layouts  7.04 us (6%)
  other arithmetic  3.64 us (3%)
    ppermute x17, waiting for transfers between devices, xor_permute(): return lax.ppermute(value, axis, [(i, i ^ bits) for i in range(count)])  44.6 us
    ppermute x6, waiting for transfers between devices, plane_permute(): return lax.ppermute(value, ('grp', 'blk'), perm)  17.3 us
    ppermute x17, starting transfers between devices, xor_permute(): return lax.ppermute(value, axis, [(i, i ^ bits) for i in range(count)])  14.2 us
    pallas_call x2, Pallas kernels, ladder_call(): pl.pallas_call(functools.partial(kernel, slab_at, part_counts), out_shape...  8.12 us
    all_to_all x1, waiting for transfers between devices, per_device(): lax.all_to_all(by_dest, 'blk', split_axis=0, concat_axis=0, tiled=True)  8.08 us
    all_to_all x1, starting transfers between devices, per_device(): lax.all_to_all(by_dest, 'blk', split_axis=0, concat_axis=0, tiled=True)  7.43 us
    ppermute x6, starting transfers between devices, plane_permute(): return lax.ppermute(value, ('grp', 'blk'), perm)  7.04 us
  transfers between devices with their start and end apart: 24, of which 12 were waited for; matrix products, arithmetic and copies ran while one was open for 7% of the time, Pallas kernels for 8%

profile of v5, /device:TPU:0, one launch (start us, length us, event | category | flops | bytes accessed | tf_op | source)
XLA Modules:
  0.0 122.2 jit_solution(7031153443138330310)
XLA Ops:
  0.0 7.4 %all-to-all-start = ((bf16[8,2,8,32,256]{4,3,2,1,0:T(8,128)(2,1)}), bf16[8,2,8,32,256]{4,3,2,1,0:T(8,128)(2,1)S(1)}, u32[]{:S(2)}, u32[]{:S(2)}) async-start(bf16[8,2,8,32,256]{4,3,2,1,0:T(8,128)(2,1)} %bitcast.29), calls=%async_computation | async-start | bytes 4194304 | tf_op jit(solution)/shard_map/all_to_all | solution.py:212
  9.1 2.2 %fusion.7 = (bf16[1,4,256,256]{3,2,1,0:T(8,128)(2,1)}, bf16[1,4,256,256]{3,2,1,0:T(8,128)(2,1)}) fusion(bf16[1,8,256,256]{3,2,1,0:T(8,128)(2,1)} %param.9), kind=kLoop, calls=%fused_computation.32 | loop fusion | bytes 2097152 | tf_op jit(solution)/shard_map/slice | solution.py:249
  11.3 1.5 %collective-permute-start.4 = (bf16[1,4,256,256]{3,2,1,0:T(8,128)(2,1)}, bf16[1,4,256,256]{3,2,1,0:T(8,128)(2,1)S(1)}, u32[]{:S(2)}, u32[]{:S(2)}) collective-permute-start(bf16[1,4,256,256]{3,2,1,0:T(8,128)(2,1)} %get-tuple-element.58), channel_id=1, source_target_pairs={{0,16},{8,24},{16,0},{24,8},{1,17},{9,25},{17,1},{25,9},{2,18},{10... | collective-permute-start | bytes 1572872 | tf_op jit(solution)/shard_map/ppermute | solution.py:15
  13.0 2.0 %shard_map.82 = (bf16[256,256]{1,0:T(8,128)(2,1)S(1)}, bf16[256,256]{1,0:T(8,128)(2,1)}, bf16[256,256]{1,0:T(8,128)(2,1)S(1)}, bf16[256,256]{1,0:T(8,128)(2,1)S(1)}) custom-call(bf16[4,2,128,256]{3,2,1,0:T(8,128)(2,1)S(1)} %get-tuple-element.60.kept, bf16[4,2,128,256]{3,2,1,0:T(8,128)(2,1)} %collective-permute-done.came), custom_call_target="tpu_custom_call" | custom-call | tf_op jit(solution)/shard_map/pallas_call | solution.py:224
  15.0 2.0 %collective-permute-start.1 = (bf16[256,256]{1,0:T(8,128)(2,1)}, bf16[256,256]{1,0:T(8,128)(2,1)S(1)}, u32[]{:S(2)}, u32[]{:S(2)}) collective-permute-start(bf16[256,256]{1,0:T(8,128)(2,1)} %get-tuple-element.32), channel_id=1, source_target_pairs={{0,1},{1,0},{2,3},{3,2},{4,5},{5,4},{6,7},{7,6},{8,9},{9,8},{10,11... | collective-permute-start | bytes 393224 | tf_op jit(solution)/shard_map/ppermute | solution.py:201
  18.9 12.5 %collective-permute-done.1 = bf16[256,256]{1,0:T(8,128)(2,1)S(1)} collective-permute-done((bf16[256,256]{1,0:T(8,128)(2,1)}, bf16[256,256]{1,0:T(8,128)(2,1)S(1)}, u32[]{:S(2)}, u32[]{:S(2)}) %collective-permute-start.1) | collective-permute-done | bytes 131104 | tf_op jit(solution)/shard_map/ppermute | solution.py:201
  31.4 2.7 %collective-permute-done.3 = bf16[256,256]{1,0:T(8,128)(2,1)S(1)} collective-permute-done((bf16[256,256]{1,0:T(8,128)(2,1)S(1)}, bf16[256,256]{1,0:T(8,128)(2,1)S(1)}, u32[]{:S(2)}, u32[]{:S(2)}) %collective-permute-start.3) | collective-permute-done | bytes 131104 | tf_op jit(solution)/shard_map/ppermute | solution.py:201
  34.2 1.6 %collective-permute-start.11 = (bf16[1,4,256,256]{3,2,1,0:T(8,128)(2,1)}, bf16[1,4,256,256]{3,2,1,0:T(8,128)(2,1)S(1)}, u32[]{:S(2)}, u32[]{:S(2)}) collective-permute-start(bf16[1,4,256,256]{3,2,1,0:T(8,128)(2,1)} %get-tuple-element.43), channel_id=1, source_target_pairs={{0,16},{8,24},{16,0},{24,8},{1,17},{9,25},{17,1},{25,9},{2,18},{10... | collective-permute-start | bytes 1572872 | tf_op jit(solution)/shard_map/ppermute | solution.py:15
  39.3 6.0 %collective-permute-done.5 = bf16[256,256]{1,0:T(8,128)(2,1)S(1)} collective-permute-done((bf16[256,256]{1,0:T(8,128)(2,1)}, bf16[256,256]{1,0:T(8,128)(2,1)S(1)}, u32[]{:S(2)}, u32[]{:S(2)}) %collective-permute-start.5) | collective-permute-done | bytes 131104 | tf_op jit(solution)/shard_map/ppermute | solution.py:15
  47.6 8.1 %all-to-all-done.piece_ref = bf16[8,2,8,32,256]{4,3,2,1,0:T(8,128)(2,1)S(1)} async-done(((bf16[8,2,8,32,256]{4,3,2,1,0:T(8,128)(2,1)}), bf16[8,2,8,32,256]{4,3,2,1,0:T(8,128)(2,1)S(1)}, u32[]{:S(2)}, u32[]{:S(2)}) %all-to-all-start) | async-done | bytes 2097184 | tf_op jit(solution)/shard_map/all_to_all | solution.py:212
  55.7 4.4 %shard_map.83 = (f32[2,8,256,256]{3,2,1,0:T(8,128)S(1)}, bf16[2,8,256,256]{3,2,1,0:T(8,128)(2,1)S(1)}) custom-call(s32[14]{0:T(128)S(1)} %pad_add_fusion.scalars, bf16[8,2,8,32,256]{4,3,2,1,0:T(8,128)(2,1)S(1)} %all-to-all-done.piece_ref, bf16[8,256,256]{2,1,0:T(8,128)(2,1)} %bitcast.10.refs_0_, bf16[8,256,256]{2,1,0:T(8,128)(2,1)} %bitcast.11.refs_1_), custom_call_target="tpu_custom_call" | custom-call | flops 2147483648 | bytes 10485760 | tf_op jit(solution)/shard_map/pallas_call | solution.py:107
  60.1 3.6 %collective-permute-done.6 = bf16[256,256]{1,0:T(8,128)(2,1)S(1)} collective-permute-done((bf16[256,256]{1,0:T(8,128)(2,1)}, bf16[256,256]{1,0:T(8,128)(2,1)S(1)}, u32[]{:S(2)}, u32[]{:S(2)}) %collective-permute-start.6) | collective-permute-done | bytes 131104 | tf_op jit(solution)/shard_map/ppermute | solution.py:15
  63.7 2.6 %collective-permute-start.10 = (bf16[256,256]{1,0:T(8,128)(2,1)S(1)}, bf16[256,256]{1,0:T(8,128)(2,1)S(1)}, u32[]{:S(2)}, u32[]{:S(2)}) collective-permute-start(bf16[256,256]{1,0:T(8,128)(2,1)S(1)} %multiply_convert_fusion), channel_id=1, source_target_pairs={{0,17},{1,16},{2,19},{3,18},{4,21},{5,20},{6,23},{7,22},{8,25},{9,... | collective-permute-start | bytes 393224 | tf_op jit(solution)/shard_map/ppermute | solution.py:201
  67.3 3.7 %shard_map.84.refs_0_ = f32[2,8,256,256]{3,2,1,0:T(8,128)S(1)} custom-call(s32[14]{0:T(128)S(1)} %pad_add_fusion.scalars, bf16[2,8,256,256]{3,2,1,0:T(8,128)(2,1)S(1)} %get-tuple-element.41.masked_ref.refs_1_, f32[2,8,256,256]{3,2,1,0:T(8,128)S(1)} %get-tuple-element.42.before_ref, bf16[4,256,256]{2,1,0:T(8,128)(2,1)S(1)} %bitcast.27, ...), custom_call_target="tpu_custom_call" | custom-call | flops 2147483648 | bytes 10485760 | tf_op jit(solution)/shard_map/pallas_call | solution.py:107
  71.1 1.8 %collective-permute-done.8 = bf16[256,256]{1,0:T(8,128)(2,1)S(1)} collective-permute-done((bf16[256,256]{1,0:T(8,128)(2,1)S(1)}, bf16[256,256]{1,0:T(8,128)(2,1)S(1)}, u32[]{:S(2)}, u32[]{:S(2)}) %collective-permute-start.8) | collective-permute-done | bytes 131104 | tf_op jit(solution)/shard_map/ppermute | solution.py:201
  73.3 1.9 %collective-permute-done.15.other_ref = bf16[4,256,256]{2,1,0:T(8,128)(2,1)S(1)} collective-permute-done((bf16[4,256,256]{2,1,0:T(8,128)(2,1)S(1)}, bf16[4,256,256]{2,1,0:T(8,128)(2,1)S(1)}, u32[]{:S(2)}, u32[]{:S(2)}) %collective-permute-start.15) | collective-permute-done | bytes 524320 | tf_op jit(solution)/shard_map/ppermute | solution.py:15
  75.2 2.4 %shard_map.85 = (bf16[2,8,32,256]{3,2,1,0:T(8,128)(2,1)S(1)}, bf16[2,8,32,256]{3,2,1,0:T(8,128)(2,1)S(1)}, bf16[2,8,32,256]{3,2,1,0:T(8,128)(2,1)S(1)}, bf16[2,8...) custom-call(s32[14]{0:T(128)S(1)} %pad_add_fusion.scalars, ...), custom_call_target="tpu_custom_call" | custom-call | flops 1073741824 | bytes 8388608 | tf_op jit(solution)/shard_map/pallas_call | solution.py:159
  77.7 1.5 %collective-permute-start.17 = (bf16[2,8,32,256]{3,2,1,0:T(8,128)(2,1)S(1)}, bf16[2,8,32,256]{3,2,1,0:T(8,128)(2,1)S(1)}, u32[]{:S(2)}, u32[]{:S(2)}) collective-permute-start(bf16[2,8,32,256]{3,2,1,0:T(8,128)(2,1)S(1)} %get-tuple-element.51), channel_id=1, source_target_pairs={{0,1},{1,0},{2,3},{3,2},{4,5},{5,4},{6,7},{7,6},{8,9},{9,8},{10,11... | collective-permute-start | bytes 786440 | tf_op jit(solution)/shard_map/ppermute | solution.py:15
  79.2 2.9 %collective-permute-start.18 = (bf16[2,8,32,256]{3,2,1,0:T(8,128)(2,1)S(1)}, bf16[2,8,32,256]{3,2,1,0:T(8,128)(2,1)S(1)}, u32[]{:S(2)}, u32[]{:S(2)}) collective-permute-start(bf16[2,8,32,256]{3,2,1,0:T(8,128)(2,1)S(1)} %get-tuple-element.52), channel_id=1, source_target_pairs={{0,5},{1,4},{2,7},{3,6},{4,1},{5,0},{6,3},{7,2},{8,13},{9,12},{10,... | collective-permute-start | bytes 786440 | tf_op jit(solution)/shard_map/ppermute | solution.py:15
  82.0 1.6 %collective-permute-start.20 = (bf16[2,8,32,256]{3,2,1,0:T(8,128)(2,1)S(1)}, bf16[2,8,32,256]{3,2,1,0:T(8,128)(2,1)S(1)}, u32[]{:S(2)}, u32[]{:S(2)}) collective-permute-start(bf16[2,8,32,256]{3,2,1,0:T(8,128)(2,1)S(1)} %get-tuple-element.54), channel_id=1, source_target_pairs={{0,6},{1,7},{2,4},{3,5},{4,2},{5,3},{6,0},{7,1},{8,14},{9,15},{10,... | collective-permute-start | bytes 786440 | tf_op jit(solution)/shard_map/ppermute | solution.py:15
  83.9 13.7 %collective-permute-done.16 = bf16[2,8,32,256]{3,2,1,0:T(8,128)(2,1)S(1)} collective-permute-done((bf16[2,8,32,256]{3,2,1,0:T(8,128)(2,1)S(1)}, bf16[2,8,32,256]{3,2,1,0:T(8,128)(2,1)S(1)}, u32[]{:S(2)}, u32[]{:S(2)}) %collective-permute-start.16) | collective-permute-done | bytes 262176 | tf_op jit(solution)/shard_map/ppermute | solution.py:15
  97.7 3.1 %collective-permute-start.22 = (bf16[2,8,32,256]{3,2,1,0:T(8,128)(2,1)S(1)}, bf16[2,8,32,256]{3,2,1,0:T(8,128)(2,1)S(1)}, u32[]{:S(2)}, u32[]{:S(2)}) collective-permute-start(bf16[2,8,32,256]{3,2,1,0:T(8,128)(2,1)S(1)} %get-tuple-element.56), channel_id=1, source_target_pairs={{0,7},{1,6},{2,5},{3,4},{4,3},{5,2},{6,1},{7,0},{8,15},{9,14},{10,... | collective-permute-start | bytes 786440 | tf_op jit(solution)/shard_map/ppermute | solution.py:15
  100.9 8.6 %collective-permute-done.18 = bf16[2,8,32,256]{3,2,1,0:T(8,128)(2,1)S(1)} collective-permute-done((bf16[2,8,32,256]{3,2,1,0:T(8,128)(2,1)S(1)}, bf16[2,8,32,256]{3,2,1,0:T(8,128)(2,1)S(1)}, u32[]{:S(2)}, u32[]{:S(2)}) %collective-permute-start.18) | collective-permute-done | bytes 262176 | tf_op jit(solution)/shard_map/ppermute | solution.py:15
  109.6 10.5 %collective-permute-done.21 = bf16[2,8,32,256]{3,2,1,0:T(8,128)(2,1)S(1)} collective-permute-done((bf16[2,8,32,256]{3,2,1,0:T(8,128)(2,1)S(1)}, bf16[2,8,32,256]{3,2,1,0:T(8,128)(2,1)S(1)}, u32[]{:S(2)}, u32[]{:S(2)}) %collective-permute-start.21) | collective-permute-done | bytes 262176 | tf_op jit(solution)/shard_map/ppermute | solution.py:15
  (70 shorter events, 13.5 us)
Async XLA Ops:
  0.0 55.7 %all-to-all-start = ((bf16[8,2,8,32,256]{4,3,2,1,0:T(8,128)(2,1)}), bf16[8,2,8,32,256]{4,3,2,1,0:T(8,128)(2,1)S(1)}, u32[]{:S(2)}, u32[]{:S(2)}) async-start(bf16[8,2,8,32,256]{4,3,2,1,0:T(8,128)(2,1)} %bitcast.29), calls=%async_computation | async-start | bytes 4194304 | tf_op jit(solution)/shard_map/all_to_all | solution.py:212
  8.6 4.4 %collective-permute-start = (bf16[4,2,128,256]{3,2,1,0:T(8,128)(2,1)}, bf16[4,2,128,256]{3,2,1,0:T(8,128)(2,1)}, u32[]{:S(2)}, u32[]{:S(2)}) collective-permute-start(bf16[4,2,128,256]{3,2,1,0:T(8,128)(2,1)} %get-tuple-element.59), channel_id=1, source_target_pairs={{0,8},{8,0},{16,24},{24,16},{1,9},{9,1},{17,25},{25,17},{2,10},{10... | collective-permute-start | bytes 1572872 | tf_op jit(solution)/shard_map/ppermute | solution.py:15
  8.6 47.1 %collective-permute-start.7 = (bf16[1,8,256,256]{3,2,1,0:T(8,128)(2,1)}, bf16[1,8,256,256]{3,2,1,0:T(8,128)(2,1)}, u32[]{:S(2)}, u32[]{:S(2)}) collective-permute-start(bf16[1,8,256,256]{3,2,1,0:T(8,128)(2,1)} %param.9), channel_id=1, source_target_pairs={{0,8},{8,0},{16,24},{24,16},{1,9},{9,1},{17,25},{25,17},{2,10},{10... | collective-permute-start | bytes 3145736 | tf_op jit(solution)/shard_map/ppermute | solution.py:15
  11.3 22.9 %collective-permute-start.4 = (bf16[1,4,256,256]{3,2,1,0:T(8,128)(2,1)}, bf16[1,4,256,256]{3,2,1,0:T(8,128)(2,1)S(1)}, u32[]{:S(2)}, u32[]{:S(2)}) collective-permute-start(bf16[1,4,256,256]{3,2,1,0:T(8,128)(2,1)} %get-tuple-element.58), channel_id=1, source_target_pairs={{0,16},{8,24},{16,0},{24,8},{1,17},{9,25},{17,1},{25,9},{2,18},{10... | collective-permute-start | bytes 1572872 | tf_op jit(solution)/shard_map/ppermute | solution.py:15
  15.0 16.4 %collective-permute-start.1 = (bf16[256,256]{1,0:T(8,128)(2,1)}, bf16[256,256]{1,0:T(8,128)(2,1)S(1)}, u32[]{:S(2)}, u32[]{:S(2)}) collective-permute-start(bf16[256,256]{1,0:T(8,128)(2,1)} %get-tuple-element.32), channel_id=1, source_target_pairs={{0,1},{1,0},{2,3},{3,2},{4,5},{5,4},{6,7},{7,6},{8,9},{9,8},{10,11... | collective-permute-start | bytes 393224 | tf_op jit(solution)/shard_map/ppermute | solution.py:201
  17.0 14.4 %collective-permute-start.2 = (bf16[256,256]{1,0:T(8,128)(2,1)S(1)}, bf16[256,256]{1,0:T(8,128)(2,1)S(1)}, u32[]{:S(2)}, u32[]{:S(2)}) collective-permute-start(bf16[256,256]{1,0:T(8,128)(2,1)S(1)} %get-tuple-element.33), channel_id=1, source_target_pairs={{0,16},{1,17},{2,18},{3,19},{4,20},{5,21},{6,22},{7,23},{8,24},{9,... | collective-permute-start | bytes 393224 | tf_op jit(solution)/shard_map/ppermute | solution.py:201
  17.6 16.6 %collective-permute-start.3 = (bf16[256,256]{1,0:T(8,128)(2,1)S(1)}, bf16[256,256]{1,0:T(8,128)(2,1)S(1)}, u32[]{:S(2)}, u32[]{:S(2)}) collective-permute-start(bf16[256,256]{1,0:T(8,128)(2,1)S(1)} %get-tuple-element.34), channel_id=1, source_target_pairs={{0,17},{1,16},{2,19},{3,18},{4,21},{5,20},{6,23},{7,22},{8,25},{9,... | collective-permute-start | bytes 393224 | tf_op jit(solution)/shard_map/ppermute | solution.py:201
  34.2 12.0 %collective-permute-start.11 = (bf16[1,4,256,256]{3,2,1,0:T(8,128)(2,1)}, bf16[1,4,256,256]{3,2,1,0:T(8,128)(2,1)S(1)}, u32[]{:S(2)}, u32[]{:S(2)}) collective-permute-start(bf16[1,4,256,256]{3,2,1,0:T(8,128)(2,1)} %get-tuple-element.43), channel_id=1, source_target_pairs={{0,16},{8,24},{16,0},{24,8},{1,17},{9,25},{17,1},{25,9},{2,18},{10... | collective-permute-start | bytes 1572872 | tf_op jit(solution)/shard_map/ppermute | solution.py:15
  36.5 8.8 %collective-permute-start.5 = (bf16[256,256]{1,0:T(8,128)(2,1)}, bf16[256,256]{1,0:T(8,128)(2,1)S(1)}, u32[]{:S(2)}, u32[]{:S(2)}) collective-permute-start(bf16[256,256]{1,0:T(8,128)(2,1)} %convert_element_type.31), channel_id=1, source_target_pairs={{0,2},{1,3},{2,0},{3,1},{4,6},{5,7},{6,4},{7,5},{8,10},{9,11},{10,... | collective-permute-start | bytes 393224 | tf_op jit(solution)/shard_map/ppermute | solution.py:15
  39.3 27.5 %collective-permute-start.12 = (bf16[1,4,256,256]{3,2,1,0:T(8,128)(2,1)S(1)}, bf16[1,4,256,256]{3,2,1,0:T(8,128)(2,1)}, u32[]{:S(2)}, u32[]{:S(2)}) collective-permute-start(bf16[1,4,256,256]{3,2,1,0:T(8,128)(2,1)S(1)} %collective-permute-done.4), channel_id=1, source_target_pairs={{0,8},{8,0},{16,24},{24,16},{1,9},{9,1},{17,25},{25,17},{2,10},{10... | collective-permute-start | bytes 1572872 | tf_op jit(solution)/shard_map/ppermute | solution.py:15
  47.1 20.2 %collective-permute-start.13 = (bf16[1,2,256,256]{3,2,1,0:T(8,128)(2,1)}, bf16[1,2,256,256]{3,2,1,0:T(8,128)(2,1)S(1)}, u32[]{:S(2)}, u32[]{:S(2)}) collective-permute-start(bf16[1,2,256,256]{3,2,1,0:T(8,128)(2,1)} %get-tuple-element.62), channel_id=1, source_target_pairs={{0,8},{8,0},{16,24},{24,16},{1,9},{9,1},{17,25},{25,17},{2,10},{10... | collective-permute-start | bytes 786440 | tf_op jit(solution)/shard_map/ppermute | solution.py:15
  47.1 20.2 %collective-permute-start.14 = (bf16[1,2,256,256]{3,2,1,0:T(8,128)(2,1)}, bf16[1,2,256,256]{3,2,1,0:T(8,128)(2,1)}, u32[]{:S(2)}, u32[]{:S(2)}) collective-permute-start(bf16[1,2,256,256]{3,2,1,0:T(8,128)(2,1)} %get-tuple-element.61), channel_id=1, source_target_pairs={{0,8},{8,0},{16,24},{24,16},{1,9},{9,1},{17,25},{25,17},{2,10},{10... | collective-permute-start | bytes 786440 | tf_op jit(solution)/shard_map/ppermute | solution.py:15
  55.7 8.0 %collective-permute-start.6 = (bf16[256,256]{1,0:T(8,128)(2,1)}, bf16[256,256]{1,0:T(8,128)(2,1)S(1)}, u32[]{:S(2)}, u32[]{:S(2)}) collective-permute-start(bf16[256,256]{1,0:T(8,128)(2,1)} %fusion.4), channel_id=1, source_target_pairs={{0,4},{1,5},{2,6},{3,7},{4,0},{5,1},{6,2},{7,3},{8,12},{9,13},{10,... | collective-permute-start | bytes 393224 | tf_op jit(solution)/shard_map/ppermute | solution.py:15
  63.7 7.3 %collective-permute-start.10 = (bf16[256,256]{1,0:T(8,128)(2,1)S(1)}, bf16[256,256]{1,0:T(8,128)(2,1)S(1)}, u32[]{:S(2)}, u32[]{:S(2)}) collective-permute-start(bf16[256,256]{1,0:T(8,128)(2,1)S(1)} %multiply_convert_fusion), channel_id=1, source_target_pairs={{0,17},{1,16},{2,19},{3,18},{4,21},{5,20},{6,23},{7,22},{8,25},{9,... | collective-permute-start | bytes 393224 | tf_op jit(solution)/shard_map/ppermute | solution.py:201
  66.3 6.5 %collective-permute-start.8 = (bf16[256,256]{1,0:T(8,128)(2,1)S(1)}, bf16[256,256]{1,0:T(8,128)(2,1)S(1)}, u32[]{:S(2)}, u32[]{:S(2)}) collective-permute-start(bf16[256,256]{1,0:T(8,128)(2,1)S(1)} %multiply_convert_fusion), channel_id=1, source_target_pairs={{0,1},{1,0},{2,3},{3,2},{4,5},{5,4},{6,7},{7,6},{8,9},{9,8},{10,11... | collective-permute-start | bytes 393224 | tf_op jit(solution)/shard_map/ppermute | solution.py:201
  66.8 6.4 %collective-permute-start.9 = (bf16[256,256]{1,0:T(8,128)(2,1)S(1)}, bf16[256,256]{1,0:T(8,128)(2,1)S(1)}, u32[]{:S(2)}, u32[]{:S(2)}) collective-permute-start(bf16[256,256]{1,0:T(8,128)(2,1)S(1)} %multiply_convert_fusion), channel_id=1, source_target_pairs={{0,16},{1,17},{2,18},{3,19},{4,20},{5,21},{6,22},{7,23},{8,24},{9,... | collective-permute-start | bytes 393224 | tf_op jit(solution)/shard_map/ppermute | solution.py:201
  73.2 2.0 %collective-permute-start.15 = (bf16[4,256,256]{2,1,0:T(8,128)(2,1)S(1)}, bf16[4,256,256]{2,1,0:T(8,128)(2,1)S(1)}, u32[]{:S(2)}, u32[]{:S(2)}) collective-permute-start(bf16[4,256,256]{2,1,0:T(8,128)(2,1)S(1)} %pad_maximum_fusion.same_ref), channel_id=1, source_target_pairs={{0,8},{8,0},{16,24},{24,16},{1,9},{9,1},{17,25},{25,17},{2,10},{10... | collective-permute-start | bytes 1572872 | tf_op jit(solution)/shard_map/ppermute | solution.py:15
  77.6 20.1 %collective-permute-start.16 = (bf16[2,8,32,256]{3,2,1,0:T(8,128)(2,1)S(1)}, bf16[2,8,32,256]{3,2,1,0:T(8,128)(2,1)S(1)}, u32[]{:S(2)}, u32[]{:S(2)}) collective-permute-start(bf16[2,8,32,256]{3,2,1,0:T(8,128)(2,1)S(1)} %get-tuple-element.50), channel_id=1, source_target_pairs={{0,4},{1,5},{2,6},{3,7},{4,0},{5,1},{6,2},{7,3},{8,12},{9,13},{10,... | collective-permute-start | bytes 786440 | tf_op jit(solution)/shard_map/ppermute | solution.py:15
  77.7 20.0 %collective-permute-start.17 = (bf16[2,8,32,256]{3,2,1,0:T(8,128)(2,1)S(1)}, bf16[2,8,32,256]{3,2,1,0:T(8,128)(2,1)S(1)}, u32[]{:S(2)}, u32[]{:S(2)}) collective-permute-start(bf16[2,8,32,256]{3,2,1,0:T(8,128)(2,1)S(1)} %get-tuple-element.51), channel_id=1, source_target_pairs={{0,1},{1,0},{2,3},{3,2},{4,5},{5,4},{6,7},{7,6},{8,9},{9,8},{10,11... | collective-permute-start | bytes 786440 | tf_op jit(solution)/shard_map/ppermute | solution.py:15
  79.2 30.3 %collective-permute-start.18 = (bf16[2,8,32,256]{3,2,1,0:T(8,128)(2,1)S(1)}, bf16[2,8,32,256]{3,2,1,0:T(8,128)(2,1)S(1)}, u32[]{:S(2)}, u32[]{:S(2)}) collective-permute-start(bf16[2,8,32,256]{3,2,1,0:T(8,128)(2,1)S(1)} %get-tuple-element.52), channel_id=1, source_target_pairs={{0,5},{1,4},{2,7},{3,6},{4,1},{5,0},{6,3},{7,2},{8,13},{9,12},{10,... | collective-permute-start | bytes 786440 | tf_op jit(solution)/shard_map/ppermute | solution.py:15
  82.0 27.5 %collective-permute-start.19 = (bf16[2,8,32,256]{3,2,1,0:T(8,128)(2,1)S(1)}, bf16[2,8,32,256]{3,2,1,0:T(8,128)(2,1)S(1)}, u32[]{:S(2)}, u32[]{:S(2)}) collective-permute-start(bf16[2,8,32,256]{3,2,1,0:T(8,128)(2,1)S(1)} %get-tuple-element.53), channel_id=1, source_target_pairs={{0,2},{1,3},{2,0},{3,1},{4,6},{5,7},{6,4},{7,5},{8,10},{9,11},{10,... | collective-permute-start | bytes 786440 | tf_op jit(solution)/shard_map/ppermute | solution.py:15
  82.0 27.5 %collective-permute-start.20 = (bf16[2,8,32,256]{3,2,1,0:T(8,128)(2,1)S(1)}, bf16[2,8,32,256]{3,2,1,0:T(8,128)(2,1)S(1)}, u32[]{:S(2)}, u32[]{:S(2)}) collective-permute-start(bf16[2,8,32,256]{3,2,1,0:T(8,128)(2,1)S(1)} %get-tuple-element.54), channel_id=1, source_target_pairs={{0,6},{1,7},{2,4},{3,5},{4,2},{5,3},{6,0},{7,1},{8,14},{9,15},{10,... | collective-permute-start | bytes 786440 | tf_op jit(solution)/shard_map/ppermute | solution.py:15
  97.7 22.5 %collective-permute-start.21 = (bf16[2,8,32,256]{3,2,1,0:T(8,128)(2,1)S(1)}, bf16[2,8,32,256]{3,2,1,0:T(8,128)(2,1)S(1)}, u32[]{:S(2)}, u32[]{:S(2)}) collective-permute-start(bf16[2,8,32,256]{3,2,1,0:T(8,128)(2,1)S(1)} %get-tuple-element.55), channel_id=1, source_target_pairs={{0,3},{1,2},{2,1},{3,0},{4,7},{5,6},{6,5},{7,4},{8,11},{9,10},{10,... | collective-permute-start | bytes 786440 | tf_op jit(solution)/shard_map/ppermute | solution.py:15
  97.7 22.5 %collective-permute-start.22 = (bf16[2,8,32,256]{3,2,1,0:T(8,128)(2,1)S(1)}, bf16[2,8,32,256]{3,2,1,0:T(8,128)(2,1)S(1)}, u32[]{:S(2)}, u32[]{:S(2)}) collective-permute-start(bf16[2,8,32,256]{3,2,1,0:T(8,128)(2,1)S(1)} %get-tuple-element.56), channel_id=1, source_target_pairs={{0,7},{1,6},{2,5},{3,4},{4,3},{5,2},{6,1},{7,0},{8,15},{9,14},{10,... | collective-permute-start | bytes 786440 | tf_op jit(solution)/shard_map/ppermute | solution.py:15
  (8 other events, 88.7 us)

commit v6 on v5

--- a/solution.py
+++ b/solution.py
@@ -144,13 +144,13 @@
                 preferred_element_type=jnp.float32,
             )
             keep = (row_ids < scalars[h]) & (col_ids < scalars[col])
-            total[j] = jnp.where(keep, acc, 0.0)
+            total[j] = jnp.where(keep, acc, 0.0).astype(total.dtype)
             for s, out_ref in enumerate(out_refs):
                 at = pl.ds(pl.multiple_of((blk ^ s) * rows, rows), rows)
                 out_ref[j, h] = total[j, at, :].astype(jnp.bfloat16)
         return carry
 
-    lax.fori_loop(0, IRREPS, one_block, 0, unroll=4)
+    lax.fori_loop(0, IRREPS, one_block, 0, unroll=8)
 
 
 def dress_call(scalars, planes, blk_count, ladder, masked, same_core, other_core):
@@ -166,7 +166,9 @@
         out_specs=[vmem] * blk_count,
         scratch_shapes=[
             pltpu.VMEM((IRREPS, slots, slots), jnp.bfloat16),
-            pltpu.VMEM((per_dev, slots, slots), jnp.float32),
+            pltpu.VMEM(
+                (per_dev, slots, slots), jnp.float32 if slots // blk_count % 16 else jnp.bfloat16
+            ),
         ],
         compiler_params=pltpu.CompilerParams(vmem_limit_bytes=16 * 1024 * 1024),
         cost_estimate=pl.CostEstimate(

time: 125 us -> 124 us (level)
  no operation moved by 1% of the time
where the time goes in v6:
time: 124 us; the launch traced here: 122 us
  waiting for transfers between devices  70.1 us (57%)
  starting transfers between devices  28.7 us (23%)
  Pallas kernels  12.2 us (10%)
  local copies, waits for them, and re-layouts  7.04 us (6%)
  other arithmetic  3.64 us (3%)
    ppermute x17, waiting for transfers between devices, xor_permute(): return lax.ppermute(value, axis, [(i, i ^ bits) for i in range(count)])  44.7 us
    ppermute x6, waiting for transfers between devices, plane_permute(): return lax.ppermute(value, ('grp', 'blk'), perm)  17.3 us
    ppermute x17, starting transfers between devices, xor_permute(): return lax.ppermute(value, axis, [(i, i ^ bits) for i in range(count)])  14.2 us
    pallas_call x2, Pallas kernels, ladder_call(): pl.pallas_call(functools.partial(kernel, slab_at, part_counts), out_shape...  8.12 us
    all_to_all x1, waiting for transfers between devices, per_device(): lax.all_to_all(by_dest, 'blk', split_axis=0, concat_axis=0, tiled=True)  8.08 us
    all_to_all x1, starting transfers between devices, per_device(): lax.all_to_all(by_dest, 'blk', split_axis=0, concat_axis=0, tiled=True)  7.43 us
    ppermute x6, starting transfers between devices, plane_permute(): return lax.ppermute(value, ('grp', 'blk'), perm)  7.04 us
  transfers between devices with their start and end apart: 24, of which 12 were waited for; matrix products, arithmetic and copies ran while one was open for 7% of the time, Pallas kernels for 8%

profile of v6, /device:TPU:0, one launch (start us, length us, event | category | flops | bytes accessed | tf_op | source)
XLA Modules:
  0.0 121.8 jit_solution(11662858159296300953)
XLA Ops:
  0.0 7.4 %all-to-all-start = ((bf16[8,2,8,32,256]{4,3,2,1,0:T(8,128)(2,1)}), bf16[8,2,8,32,256]{4,3,2,1,0:T(8,128)(2,1)S(1)}, u32[]{:S(2)}, u32[]{:S(2)}) async-start(bf16[8,2,8,32,256]{4,3,2,1,0:T(8,128)(2,1)} %bitcast.29), calls=%async_computation | async-start | bytes 4194304 | tf_op jit(solution)/shard_map/all_to_all | solution.py:214
  9.1 2.2 %fusion.7 = (bf16[1,4,256,256]{3,2,1,0:T(8,128)(2,1)}, bf16[1,4,256,256]{3,2,1,0:T(8,128)(2,1)}) fusion(bf16[1,8,256,256]{3,2,1,0:T(8,128)(2,1)} %param.9), kind=kLoop, calls=%fused_computation.32 | loop fusion | bytes 2097152 | tf_op jit(solution)/shard_map/slice | solution.py:251
  11.3 1.5 %collective-permute-start.4 = (bf16[1,4,256,256]{3,2,1,0:T(8,128)(2,1)}, bf16[1,4,256,256]{3,2,1,0:T(8,128)(2,1)S(1)}, u32[]{:S(2)}, u32[]{:S(2)}) collective-permute-start(bf16[1,4,256,256]{3,2,1,0:T(8,128)(2,1)} %get-tuple-element.58), channel_id=1, source_target_pairs={{0,16},{8,24},{16,0},{24,8},{1,17},{9,25},{17,1},{25,9},{2,18},{10... | collective-permute-start | bytes 1572872 | tf_op jit(solution)/shard_map/ppermute | solution.py:15
  13.0 2.0 %shard_map.82 = (bf16[256,256]{1,0:T(8,128)(2,1)S(1)}, bf16[256,256]{1,0:T(8,128)(2,1)}, bf16[256,256]{1,0:T(8,128)(2,1)S(1)}, bf16[256,256]{1,0:T(8,128)(2,1)S(1)}) custom-call(bf16[4,2,128,256]{3,2,1,0:T(8,128)(2,1)S(1)} %get-tuple-element.60.kept, bf16[4,2,128,256]{3,2,1,0:T(8,128)(2,1)} %collective-permute-done.came), custom_call_target="tpu_custom_call" | custom-call | tf_op jit(solution)/shard_map/pallas_call | solution.py:226
  15.0 2.0 %collective-permute-start.1 = (bf16[256,256]{1,0:T(8,128)(2,1)}, bf16[256,256]{1,0:T(8,128)(2,1)S(1)}, u32[]{:S(2)}, u32[]{:S(2)}) collective-permute-start(bf16[256,256]{1,0:T(8,128)(2,1)} %get-tuple-element.32), channel_id=1, source_target_pairs={{0,1},{1,0},{2,3},{3,2},{4,5},{5,4},{6,7},{7,6},{8,9},{9,8},{10,11... | collective-permute-start | bytes 393224 | tf_op jit(solution)/shard_map/ppermute | solution.py:203
  18.9 12.5 %collective-permute-done.1 = bf16[256,256]{1,0:T(8,128)(2,1)S(1)} collective-permute-done((bf16[256,256]{1,0:T(8,128)(2,1)}, bf16[256,256]{1,0:T(8,128)(2,1)S(1)}, u32[]{:S(2)}, u32[]{:S(2)}) %collective-permute-start.1) | collective-permute-done | bytes 131104 | tf_op jit(solution)/shard_map/ppermute | solution.py:203
  31.4 2.7 %collective-permute-done.3 = bf16[256,256]{1,0:T(8,128)(2,1)S(1)} collective-permute-done((bf16[256,256]{1,0:T(8,128)(2,1)S(1)}, bf16[256,256]{1,0:T(8,128)(2,1)S(1)}, u32[]{:S(2)}, u32[]{:S(2)}) %collective-permute-start.3) | collective-permute-done | bytes 131104 | tf_op jit(solution)/shard_map/ppermute | solution.py:203
  34.2 1.6 %collective-permute-start.11 = (bf16[1,4,256,256]{3,2,1,0:T(8,128)(2,1)}, bf16[1,4,256,256]{3,2,1,0:T(8,128)(2,1)S(1)}, u32[]{:S(2)}, u32[]{:S(2)}) collective-permute-start(bf16[1,4,256,256]{3,2,1,0:T(8,128)(2,1)} %get-tuple-element.43), channel_id=1, source_target_pairs={{0,16},{8,24},{16,0},{24,8},{1,17},{9,25},{17,1},{25,9},{2,18},{10... | collective-permute-start | bytes 1572872 | tf_op jit(solution)/shard_map/ppermute | solution.py:15
  39.3 6.0 %collective-permute-done.5 = bf16[256,256]{1,0:T(8,128)(2,1)S(1)} collective-permute-done((bf16[256,256]{1,0:T(8,128)(2,1)}, bf16[256,256]{1,0:T(8,128)(2,1)S(1)}, u32[]{:S(2)}, u32[]{:S(2)}) %collective-permute-start.5) | collective-permute-done | bytes 131104 | tf_op jit(solution)/shard_map/ppermute | solution.py:15
  47.6 8.1 %all-to-all-done.piece_ref = bf16[8,2,8,32,256]{4,3,2,1,0:T(8,128)(2,1)S(1)} async-done(((bf16[8,2,8,32,256]{4,3,2,1,0:T(8,128)(2,1)}), bf16[8,2,8,32,256]{4,3,2,1,0:T(8,128)(2,1)S(1)}, u32[]{:S(2)}, u32[]{:S(2)}) %all-to-all-start) | async-done | bytes 2097184 | tf_op jit(solution)/shard_map/all_to_all | solution.py:214
  55.7 4.4 %shard_map.83 = (f32[2,8,256,256]{3,2,1,0:T(8,128)S(1)}, bf16[2,8,256,256]{3,2,1,0:T(8,128)(2,1)S(1)}) custom-call(s32[14]{0:T(128)S(1)} %pad_add_fusion.scalars, bf16[8,2,8,32,256]{4,3,2,1,0:T(8,128)(2,1)S(1)} %all-to-all-done.piece_ref, bf16[8,256,256]{2,1,0:T(8,128)(2,1)} %bitcast.10.refs_0_, bf16[8,256,256]{2,1,0:T(8,128)(2,1)} %bitcast.11.refs_1_), custom_call_target="tpu_custom_call" | custom-call | flops 2147483648 | bytes 10485760 | tf_op jit(solution)/shard_map/pallas_call | solution.py:107
  60.1 3.6 %collective-permute-done.6 = bf16[256,256]{1,0:T(8,128)(2,1)S(1)} collective-permute-done((bf16[256,256]{1,0:T(8,128)(2,1)}, bf16[256,256]{1,0:T(8,128)(2,1)S(1)}, u32[]{:S(2)}, u32[]{:S(2)}) %collective-permute-start.6) | collective-permute-done | bytes 131104 | tf_op jit(solution)/shard_map/ppermute | solution.py:15
  63.7 2.6 %collective-permute-start.10 = (bf16[256,256]{1,0:T(8,128)(2,1)S(1)}, bf16[256,256]{1,0:T(8,128)(2,1)S(1)}, u32[]{:S(2)}, u32[]{:S(2)}) collective-permute-start(bf16[256,256]{1,0:T(8,128)(2,1)S(1)} %multiply_convert_fusion), channel_id=1, source_target_pairs={{0,17},{1,16},{2,19},{3,18},{4,21},{5,20},{6,23},{7,22},{8,25},{9,... | collective-permute-start | bytes 393224 | tf_op jit(solution)/shard_map/ppermute | solution.py:203
  67.3 3.7 %shard_map.84.refs_0_ = f32[2,8,256,256]{3,2,1,0:T(8,128)S(1)} custom-call(s32[14]{0:T(128)S(1)} %pad_add_fusion.scalars, bf16[2,8,256,256]{3,2,1,0:T(8,128)(2,1)S(1)} %get-tuple-element.41.masked_ref.refs_1_, f32[2,8,256,256]{3,2,1,0:T(8,128)S(1)} %get-tuple-element.42.before_ref, bf16[4,256,256]{2,1,0:T(8,128)(2,1)S(1)} %bitcast.27, ...), custom_call_target="tpu_custom_call" | custom-call | flops 2147483648 | bytes 10485760 | tf_op jit(solution)/shard_map/pallas_call | solution.py:107
  71.1 1.8 %collective-permute-done.8 = bf16[256,256]{1,0:T(8,128)(2,1)S(1)} collective-permute-done((bf16[256,256]{1,0:T(8,128)(2,1)S(1)}, bf16[256,256]{1,0:T(8,128)(2,1)S(1)}, u32[]{:S(2)}, u32[]{:S(2)}) %collective-permute-start.8) | collective-permute-done | bytes 131104 | tf_op jit(solution)/shard_map/ppermute | solution.py:203
  73.3 1.9 %collective-permute-done.15.other_ref = bf16[4,256,256]{2,1,0:T(8,128)(2,1)S(1)} collective-permute-done((bf16[4,256,256]{2,1,0:T(8,128)(2,1)S(1)}, bf16[4,256,256]{2,1,0:T(8,128)(2,1)S(1)}, u32[]{:S(2)}, u32[]{:S(2)}) %collective-permute-start.15) | collective-permute-done | bytes 524320 | tf_op jit(solution)/shard_map/ppermute | solution.py:15
  75.2 2.0 %shard_map.85 = (bf16[2,8,32,256]{3,2,1,0:T(8,128)(2,1)S(1)}, bf16[2,8,32,256]{3,2,1,0:T(8,128)(2,1)S(1)}, bf16[2,8,32,256]{3,2,1,0:T(8,128)(2,1)S(1)}, bf16[2,8...) custom-call(s32[14]{0:T(128)S(1)} %pad_add_fusion.scalars, ...), custom_call_target="tpu_custom_call" | custom-call | flops 1073741824 | bytes 8388608 | tf_op jit(solution)/shard_map/pallas_call | solution.py:159
  77.3 1.5 %collective-permute-start.17 = (bf16[2,8,32,256]{3,2,1,0:T(8,128)(2,1)S(1)}, bf16[2,8,32,256]{3,2,1,0:T(8,128)(2,1)S(1)}, u32[]{:S(2)}, u32[]{:S(2)}) collective-permute-start(bf16[2,8,32,256]{3,2,1,0:T(8,128)(2,1)S(1)} %get-tuple-element.51), channel_id=1, source_target_pairs={{0,1},{1,0},{2,3},{3,2},{4,5},{5,4},{6,7},{7,6},{8,9},{9,8},{10,11... | collective-permute-start | bytes 786440 | tf_op jit(solution)/shard_map/ppermute | solution.py:15
  78.8 2.9 %collective-permute-start.18 = (bf16[2,8,32,256]{3,2,1,0:T(8,128)(2,1)S(1)}, bf16[2,8,32,256]{3,2,1,0:T(8,128)(2,1)S(1)}, u32[]{:S(2)}, u32[]{:S(2)}) collective-permute-start(bf16[2,8,32,256]{3,2,1,0:T(8,128)(2,1)S(1)} %get-tuple-element.52), channel_id=1, source_target_pairs={{0,5},{1,4},{2,7},{3,6},{4,1},{5,0},{6,3},{7,2},{8,13},{9,12},{10,... | collective-permute-start | bytes 786440 | tf_op jit(solution)/shard_map/ppermute | solution.py:15
  81.7 1.6 %collective-permute-start.20 = (bf16[2,8,32,256]{3,2,1,0:T(8,128)(2,1)S(1)}, bf16[2,8,32,256]{3,2,1,0:T(8,128)(2,1)S(1)}, u32[]{:S(2)}, u32[]{:S(2)}) collective-permute-start(bf16[2,8,32,256]{3,2,1,0:T(8,128)(2,1)S(1)} %get-tuple-element.54), channel_id=1, source_target_pairs={{0,6},{1,7},{2,4},{3,5},{4,2},{5,3},{6,0},{7,1},{8,14},{9,15},{10,... | collective-permute-start | bytes 786440 | tf_op jit(solution)/shard_map/ppermute | solution.py:15
  83.6 13.7 %collective-permute-done.16 = bf16[2,8,32,256]{3,2,1,0:T(8,128)(2,1)S(1)} collective-permute-done((bf16[2,8,32,256]{3,2,1,0:T(8,128)(2,1)S(1)}, bf16[2,8,32,256]{3,2,1,0:T(8,128)(2,1)S(1)}, u32[]{:S(2)}, u32[]{:S(2)}) %collective-permute-start.16) | collective-permute-done | bytes 262176 | tf_op jit(solution)/shard_map/ppermute | solution.py:15
  97.3 3.1 %collective-permute-start.22 = (bf16[2,8,32,256]{3,2,1,0:T(8,128)(2,1)S(1)}, bf16[2,8,32,256]{3,2,1,0:T(8,128)(2,1)S(1)}, u32[]{:S(2)}, u32[]{:S(2)}) collective-permute-start(bf16[2,8,32,256]{3,2,1,0:T(8,128)(2,1)S(1)} %get-tuple-element.56), channel_id=1, source_target_pairs={{0,7},{1,6},{2,5},{3,4},{4,3},{5,2},{6,1},{7,0},{8,15},{9,14},{10,... | collective-permute-start | bytes 786440 | tf_op jit(solution)/shard_map/ppermute | solution.py:15
  100.5 8.6 %collective-permute-done.18 = bf16[2,8,32,256]{3,2,1,0:T(8,128)(2,1)S(1)} collective-permute-done((bf16[2,8,32,256]{3,2,1,0:T(8,128)(2,1)S(1)}, bf16[2,8,32,256]{3,2,1,0:T(8,128)(2,1)S(1)}, u32[]{:S(2)}, u32[]{:S(2)}) %collective-permute-start.18) | collective-permute-done | bytes 262176 | tf_op jit(solution)/shard_map/ppermute | solution.py:15
  109.2 10.5 %collective-permute-done.21 = bf16[2,8,32,256]{3,2,1,0:T(8,128)(2,1)S(1)} collective-permute-done((bf16[2,8,32,256]{3,2,1,0:T(8,128)(2,1)S(1)}, bf16[2,8,32,256]{3,2,1,0:T(8,128)(2,1)S(1)}, u32[]{:S(2)}, u32[]{:S(2)}) %collective-permute-start.21) | collective-permute-done | bytes 262176 | tf_op jit(solution)/shard_map/ppermute | solution.py:15
  (70 shorter events, 13.5 us)
Async XLA Ops:
  0.0 55.7 %all-to-all-start = ((bf16[8,2,8,32,256]{4,3,2,1,0:T(8,128)(2,1)}), bf16[8,2,8,32,256]{4,3,2,1,0:T(8,128)(2,1)S(1)}, u32[]{:S(2)}, u32[]{:S(2)}) async-start(bf16[8,2,8,32,256]{4,3,2,1,0:T(8,128)(2,1)} %bitcast.29), calls=%async_computation | async-start | bytes 4194304 | tf_op jit(solution)/shard_map/all_to_all | solution.py:214
  8.6 4.4 %collective-permute-start = (bf16[4,2,128,256]{3,2,1,0:T(8,128)(2,1)}, bf16[4,2,128,256]{3,2,1,0:T(8,128)(2,1)}, u32[]{:S(2)}, u32[]{:S(2)}) collective-permute-start(bf16[4,2,128,256]{3,2,1,0:T(8,128)(2,1)} %get-tuple-element.59), channel_id=1, source_target_pairs={{0,8},{8,0},{16,24},{24,16},{1,9},{9,1},{17,25},{25,17},{2,10},{10... | collective-permute-start | bytes 1572872 | tf_op jit(solution)/shard_map/ppermute | solution.py:15
  8.6 47.1 %collective-permute-start.7 = (bf16[1,8,256,256]{3,2,1,0:T(8,128)(2,1)}, bf16[1,8,256,256]{3,2,1,0:T(8,128)(2,1)}, u32[]{:S(2)}, u32[]{:S(2)}) collective-permute-start(bf16[1,8,256,256]{3,2,1,0:T(8,128)(2,1)} %param.9), channel_id=1, source_target_pairs={{0,8},{8,0},{16,24},{24,16},{1,9},{9,1},{17,25},{25,17},{2,10},{10... | collective-permute-start | bytes 3145736 | tf_op jit(solution)/shard_map/ppermute | solution.py:15
  11.3 22.9 %collective-permute-start.4 = (bf16[1,4,256,256]{3,2,1,0:T(8,128)(2,1)}, bf16[1,4,256,256]{3,2,1,0:T(8,128)(2,1)S(1)}, u32[]{:S(2)}, u32[]{:S(2)}) collective-permute-start(bf16[1,4,256,256]{3,2,1,0:T(8,128)(2,1)} %get-tuple-element.58), channel_id=1, source_target_pairs={{0,16},{8,24},{16,0},{24,8},{1,17},{9,25},{17,1},{25,9},{2,18},{10... | collective-permute-start | bytes 1572872 | tf_op jit(solution)/shard_map/ppermute | solution.py:15
  15.0 16.4 %collective-permute-start.1 = (bf16[256,256]{1,0:T(8,128)(2,1)}, bf16[256,256]{1,0:T(8,128)(2,1)S(1)}, u32[]{:S(2)}, u32[]{:S(2)}) collective-permute-start(bf16[256,256]{1,0:T(8,128)(2,1)} %get-tuple-element.32), channel_id=1, source_target_pairs={{0,1},{1,0},{2,3},{3,2},{4,5},{5,4},{6,7},{7,6},{8,9},{9,8},{10,11... | collective-permute-start | bytes 393224 | tf_op jit(solution)/shard_map/ppermute | solution.py:203
  17.0 14.4 %collective-permute-start.2 = (bf16[256,256]{1,0:T(8,128)(2,1)S(1)}, bf16[256,256]{1,0:T(8,128)(2,1)S(1)}, u32[]{:S(2)}, u32[]{:S(2)}) collective-permute-start(bf16[256,256]{1,0:T(8,128)(2,1)S(1)} %get-tuple-element.33), channel_id=1, source_target_pairs={{0,16},{1,17},{2,18},{3,19},{4,20},{5,21},{6,22},{7,23},{8,24},{9,... | collective-permute-start | bytes 393224 | tf_op jit(solution)/shard_map/ppermute | solution.py:203
  17.6 16.6 %collective-permute-start.3 = (bf16[256,256]{1,0:T(8,128)(2,1)S(1)}, bf16[256,256]{1,0:T(8,128)(2,1)S(1)}, u32[]{:S(2)}, u32[]{:S(2)}) collective-permute-start(bf16[256,256]{1,0:T(8,128)(2,1)S(1)} %get-tuple-element.34), channel_id=1, source_target_pairs={{0,17},{1,16},{2,19},{3,18},{4,21},{5,20},{6,23},{7,22},{8,25},{9,... | collective-permute-start | bytes 393224 | tf_op jit(solution)/shard_map/ppermute | solution.py:203
  34.2 12.0 %collective-permute-start.11 = (bf16[1,4,256,256]{3,2,1,0:T(8,128)(2,1)}, bf16[1,4,256,256]{3,2,1,0:T(8,128)(2,1)S(1)}, u32[]{:S(2)}, u32[]{:S(2)}) collective-permute-start(bf16[1,4,256,256]{3,2,1,0:T(8,128)(2,1)} %get-tuple-element.43), channel_id=1, source_target_pairs={{0,16},{8,24},{16,0},{24,8},{1,17},{9,25},{17,1},{25,9},{2,18},{10... | collective-permute-start | bytes 1572872 | tf_op jit(solution)/shard_map/ppermute | solution.py:15
  36.5 8.8 %collective-permute-start.5 = (bf16[256,256]{1,0:T(8,128)(2,1)}, bf16[256,256]{1,0:T(8,128)(2,1)S(1)}, u32[]{:S(2)}, u32[]{:S(2)}) collective-permute-start(bf16[256,256]{1,0:T(8,128)(2,1)} %convert_element_type.31), channel_id=1, source_target_pairs={{0,2},{1,3},{2,0},{3,1},{4,6},{5,7},{6,4},{7,5},{8,10},{9,11},{10,... | collective-permute-start | bytes 393224 | tf_op jit(solution)/shard_map/ppermute | solution.py:15
  39.3 27.5 %collective-permute-start.12 = (bf16[1,4,256,256]{3,2,1,0:T(8,128)(2,1)S(1)}, bf16[1,4,256,256]{3,2,1,0:T(8,128)(2,1)}, u32[]{:S(2)}, u32[]{:S(2)}) collective-permute-start(bf16[1,4,256,256]{3,2,1,0:T(8,128)(2,1)S(1)} %collective-permute-done.4), channel_id=1, source_target_pairs={{0,8},{8,0},{16,24},{24,16},{1,9},{9,1},{17,25},{25,17},{2,10},{10... | collective-permute-start | bytes 1572872 | tf_op jit(solution)/shard_map/ppermute | solution.py:15
  47.1 20.2 %collective-permute-start.13 = (bf16[1,2,256,256]{3,2,1,0:T(8,128)(2,1)}, bf16[1,2,256,256]{3,2,1,0:T(8,128)(2,1)S(1)}, u32[]{:S(2)}, u32[]{:S(2)}) collective-permute-start(bf16[1,2,256,256]{3,2,1,0:T(8,128)(2,1)} %get-tuple-element.62), channel_id=1, source_target_pairs={{0,8},{8,0},{16,24},{24,16},{1,9},{9,1},{17,25},{25,17},{2,10},{10... | collective-permute-start | bytes 786440 | tf_op jit(solution)/shard_map/ppermute | solution.py:15
  47.1 20.2 %collective-permute-start.14 = (bf16[1,2,256,256]{3,2,1,0:T(8,128)(2,1)}, bf16[1,2,256,256]{3,2,1,0:T(8,128)(2,1)}, u32[]{:S(2)}, u32[]{:S(2)}) collective-permute-start(bf16[1,2,256,256]{3,2,1,0:T(8,128)(2,1)} %get-tuple-element.61), channel_id=1, source_target_pairs={{0,8},{8,0},{16,24},{24,16},{1,9},{9,1},{17,25},{25,17},{2,10},{10... | collective-permute-start | bytes 786440 | tf_op jit(solution)/shard_map/ppermute | solution.py:15
  55.7 8.0 %collective-permute-start.6 = (bf16[256,256]{1,0:T(8,128)(2,1)}, bf16[256,256]{1,0:T(8,128)(2,1)S(1)}, u32[]{:S(2)}, u32[]{:S(2)}) collective-permute-start(bf16[256,256]{1,0:T(8,128)(2,1)} %fusion.4), channel_id=1, source_target_pairs={{0,4},{1,5},{2,6},{3,7},{4,0},{5,1},{6,2},{7,3},{8,12},{9,13},{10,... | collective-permute-start | bytes 393224 | tf_op jit(solution)/shard_map/ppermute | solution.py:15
  63.7 7.3 %collective-permute-start.10 = (bf16[256,256]{1,0:T(8,128)(2,1)S(1)}, bf16[256,256]{1,0:T(8,128)(2,1)S(1)}, u32[]{:S(2)}, u32[]{:S(2)}) collective-permute-start(bf16[256,256]{1,0:T(8,128)(2,1)S(1)} %multiply_convert_fusion), channel_id=1, source_target_pairs={{0,17},{1,16},{2,19},{3,18},{4,21},{5,20},{6,23},{7,22},{8,25},{9,... | collective-permute-start | bytes 393224 | tf_op jit(solution)/shard_map/ppermute | solution.py:203
  66.3 6.5 %collective-permute-start.8 = (bf16[256,256]{1,0:T(8,128)(2,1)S(1)}, bf16[256,256]{1,0:T(8,128)(2,1)S(1)}, u32[]{:S(2)}, u32[]{:S(2)}) collective-permute-start(bf16[256,256]{1,0:T(8,128)(2,1)S(1)} %multiply_convert_fusion), channel_id=1, source_target_pairs={{0,1},{1,0},{2,3},{3,2},{4,5},{5,4},{6,7},{7,6},{8,9},{9,8},{10,11... | collective-permute-start | bytes 393224 | tf_op jit(solution)/shard_map/ppermute | solution.py:203
  66.8 6.4 %collective-permute-start.9 = (bf16[256,256]{1,0:T(8,128)(2,1)S(1)}, bf16[256,256]{1,0:T(8,128)(2,1)S(1)}, u32[]{:S(2)}, u32[]{:S(2)}) collective-permute-start(bf16[256,256]{1,0:T(8,128)(2,1)S(1)} %multiply_convert_fusion), channel_id=1, source_target_pairs={{0,16},{1,17},{2,18},{3,19},{4,20},{5,21},{6,22},{7,23},{8,24},{9,... | collective-permute-start | bytes 393224 | tf_op jit(solution)/shard_map/ppermute | solution.py:203
  73.2 2.0 %collective-permute-start.15 = (bf16[4,256,256]{2,1,0:T(8,128)(2,1)S(1)}, bf16[4,256,256]{2,1,0:T(8,128)(2,1)S(1)}, u32[]{:S(2)}, u32[]{:S(2)}) collective-permute-start(bf16[4,256,256]{2,1,0:T(8,128)(2,1)S(1)} %pad_maximum_fusion.same_ref), channel_id=1, source_target_pairs={{0,8},{8,0},{16,24},{24,16},{1,9},{9,1},{17,25},{25,17},{2,10},{10... | collective-permute-start | bytes 1572872 | tf_op jit(solution)/shard_map/ppermute | solution.py:15
  77.2 20.1 %collective-permute-start.16 = (bf16[2,8,32,256]{3,2,1,0:T(8,128)(2,1)S(1)}, bf16[2,8,32,256]{3,2,1,0:T(8,128)(2,1)S(1)}, u32[]{:S(2)}, u32[]{:S(2)}) collective-permute-start(bf16[2,8,32,256]{3,2,1,0:T(8,128)(2,1)S(1)} %get-tuple-element.50), channel_id=1, source_target_pairs={{0,4},{1,5},{2,6},{3,7},{4,0},{5,1},{6,2},{7,3},{8,12},{9,13},{10,... | collective-permute-start | bytes 786440 | tf_op jit(solution)/shard_map/ppermute | solution.py:15
  77.3 20.0 %collective-permute-start.17 = (bf16[2,8,32,256]{3,2,1,0:T(8,128)(2,1)S(1)}, bf16[2,8,32,256]{3,2,1,0:T(8,128)(2,1)S(1)}, u32[]{:S(2)}, u32[]{:S(2)}) collective-permute-start(bf16[2,8,32,256]{3,2,1,0:T(8,128)(2,1)S(1)} %get-tuple-element.51), channel_id=1, source_target_pairs={{0,1},{1,0},{2,3},{3,2},{4,5},{5,4},{6,7},{7,6},{8,9},{9,8},{10,11... | collective-permute-start | bytes 786440 | tf_op jit(solution)/shard_map/ppermute | solution.py:15
  78.8 30.3 %collective-permute-start.18 = (bf16[2,8,32,256]{3,2,1,0:T(8,128)(2,1)S(1)}, bf16[2,8,32,256]{3,2,1,0:T(8,128)(2,1)S(1)}, u32[]{:S(2)}, u32[]{:S(2)}) collective-permute-start(bf16[2,8,32,256]{3,2,1,0:T(8,128)(2,1)S(1)} %get-tuple-element.52), channel_id=1, source_target_pairs={{0,5},{1,4},{2,7},{3,6},{4,1},{5,0},{6,3},{7,2},{8,13},{9,12},{10,... | collective-permute-start | bytes 786440 | tf_op jit(solution)/shard_map/ppermute | solution.py:15
  81.7 27.5 %collective-permute-start.19 = (bf16[2,8,32,256]{3,2,1,0:T(8,128)(2,1)S(1)}, bf16[2,8,32,256]{3,2,1,0:T(8,128)(2,1)S(1)}, u32[]{:S(2)}, u32[]{:S(2)}) collective-permute-start(bf16[2,8,32,256]{3,2,1,0:T(8,128)(2,1)S(1)} %get-tuple-element.53), channel_id=1, source_target_pairs={{0,2},{1,3},{2,0},{3,1},{4,6},{5,7},{6,4},{7,5},{8,10},{9,11},{10,... | collective-permute-start | bytes 786440 | tf_op jit(solution)/shard_map/ppermute | solution.py:15
  81.7 27.5 %collective-permute-start.20 = (bf16[2,8,32,256]{3,2,1,0:T(8,128)(2,1)S(1)}, bf16[2,8,32,256]{3,2,1,0:T(8,128)(2,1)S(1)}, u32[]{:S(2)}, u32[]{:S(2)}) collective-permute-start(bf16[2,8,32,256]{3,2,1,0:T(8,128)(2,1)S(1)} %get-tuple-element.54), channel_id=1, source_target_pairs={{0,6},{1,7},{2,4},{3,5},{4,2},{5,3},{6,0},{7,1},{8,14},{9,15},{10,... | collective-permute-start | bytes 786440 | tf_op jit(solution)/shard_map/ppermute | solution.py:15
  97.3 22.5 %collective-permute-start.21 = (bf16[2,8,32,256]{3,2,1,0:T(8,128)(2,1)S(1)}, bf16[2,8,32,256]{3,2,1,0:T(8,128)(2,1)S(1)}, u32[]{:S(2)}, u32[]{:S(2)}) collective-permute-start(bf16[2,8,32,256]{3,2,1,0:T(8,128)(2,1)S(1)} %get-tuple-element.55), channel_id=1, source_target_pairs={{0,3},{1,2},{2,1},{3,0},{4,7},{5,6},{6,5},{7,4},{8,11},{9,10},{10,... | collective-permute-start | bytes 786440 | tf_op jit(solution)/shard_map/ppermute | solution.py:15
  97.3 22.5 %collective-permute-start.22 = (bf16[2,8,32,256]{3,2,1,0:T(8,128)(2,1)S(1)}, bf16[2,8,32,256]{3,2,1,0:T(8,128)(2,1)S(1)}, u32[]{:S(2)}, u32[]{:S(2)}) collective-permute-start(bf16[2,8,32,256]{3,2,1,0:T(8,128)(2,1)S(1)} %get-tuple-element.56), channel_id=1, source_target_pairs={{0,7},{1,6},{2,5},{3,4},{4,3},{5,2},{6,1},{7,0},{8,15},{9,14},{10,... | collective-permute-start | bytes 786440 | tf_op jit(solution)/shard_map/ppermute | solution.py:15
  (8 other events, 88.7 us)

commit v7 on v6

--- a/solution.py
+++ b/solution.py
@@ -305,7 +305,8 @@
     result = jnp.zeros(amplitudes.shape, jnp.bfloat16)
     result = lax.dynamic_update_slice(result, sent[0], (blk * per_dev, 0, 0, 0))
     top = blk_count // 2
-    far, near = list(range(top, blk_count)), list(range(1, top))
+    far, near = list(range(top, blk_count)), list(range(top - 1, 0, -1))
+    far = far[1::2] + far[0::2]
     for s in [s for two in zip(far, near + [0]) for s in two if s]:
         came = xor_permute(sent[s], "blk", blk_count, s)
         result = lax.dynamic_update_slice(result, came, ((blk ^ s) * per_dev, 0, 0, 0))

time: 124 us -> 124 us (level)
  waiting for transfers between devices: 70.1 us -> 68.2 us
  starting transfers between devices: 28.7 us -> 30.2 us
    ppermute x17, waiting for transfers between devices: 44.7 us -> 42.8 us  [xor_permute(): return lax.ppermute(value, axis, [(i, i ^ bits) for i in range(count)])]
    ppermute x17, starting transfers between devices: 14.2 us -> 15.8 us  [xor_permute(): return lax.ppermute(value, axis, [(i, i ^ bits) for i in range(count)])]
  transfers between devices with their start and end apart: 24 -> 24, of which waited for: 12 -> 13; matrix products, arithmetic and copies ran while one was open for 7% -> 7% of each run, Pallas kernels for 8% -> 8%
where the time goes in v7:
time: 124 us; the launch traced here: 121 us
  waiting for transfers between devices  68.2 us (55%)
  starting transfers between devices  30.2 us (24%)
  Pallas kernels  12.2 us (10%)
  local copies, waits for them, and re-layouts  7.04 us (6%)
  other arithmetic  3.64 us (3%)
    ppermute x17, waiting for transfers between devices, xor_permute(): return lax.ppermute(value, axis, [(i, i ^ bits) for i in range(count)])  42.8 us
    ppermute x6, waiting for transfers between devices, plane_permute(): return lax.ppermute(value, ('grp', 'blk'), perm)  17.3 us
    ppermute x17, starting transfers between devices, xor_permute(): return lax.ppermute(value, axis, [(i, i ^ bits) for i in range(count)])  15.8 us
    pallas_call x2, Pallas kernels, ladder_call(): pl.pallas_call(functools.partial(kernel, slab_at, part_counts), out_shape...  8.12 us
    all_to_all x1, waiting for transfers between devices, per_device(): lax.all_to_all(by_dest, 'blk', split_axis=0, concat_axis=0, tiled=True)  8.08 us
    all_to_all x1, starting transfers between devices, per_device(): lax.all_to_all(by_dest, 'blk', split_axis=0, concat_axis=0, tiled=True)  7.43 us
    ppermute x6, starting transfers between devices, plane_permute(): return lax.ppermute(value, ('grp', 'blk'), perm)  7.04 us
  transfers between devices with their start and end apart: 24, of which 13 were waited for; matrix products, arithmetic and copies ran while one was open for 7% of the time, Pallas kernels for 8%

profile of v7, /device:TPU:0, one launch (start us, length us, event | category | flops | bytes accessed | tf_op | source)
XLA Modules:
  0.0 121.5 jit_solution(10004212432570588951)
XLA Ops:
  0.0 7.4 %all-to-all-start = ((bf16[8,2,8,32,256]{4,3,2,1,0:T(8,128)(2,1)}), bf16[8,2,8,32,256]{4,3,2,1,0:T(8,128)(2,1)S(1)}, u32[]{:S(2)}, u32[]{:S(2)}) async-start(bf16[8,2,8,32,256]{4,3,2,1,0:T(8,128)(2,1)} %bitcast.29), calls=%async_computation | async-start | bytes 4194304 | tf_op jit(solution)/shard_map/all_to_all | solution.py:214
  9.1 2.2 %fusion.7 = (bf16[1,4,256,256]{3,2,1,0:T(8,128)(2,1)}, bf16[1,4,256,256]{3,2,1,0:T(8,128)(2,1)}) fusion(bf16[1,8,256,256]{3,2,1,0:T(8,128)(2,1)} %param.9), kind=kLoop, calls=%fused_computation.32 | loop fusion | bytes 2097152 | tf_op jit(solution)/shard_map/slice | solution.py:251
  13.0 2.0 %shard_map.82 = (bf16[256,256]{1,0:T(8,128)(2,1)S(1)}, bf16[256,256]{1,0:T(8,128)(2,1)}, bf16[256,256]{1,0:T(8,128)(2,1)S(1)}, bf16[256,256]{1,0:T(8,128)(2,1)S(1)}) custom-call(bf16[4,2,128,256]{3,2,1,0:T(8,128)(2,1)S(1)} %get-tuple-element.60.kept, bf16[4,2,128,256]{3,2,1,0:T(8,128)(2,1)} %collective-permute-done.came), custom_call_target="tpu_custom_call" | custom-call | tf_op jit(solution)/shard_map/pallas_call | solution.py:226
  15.0 2.0 %collective-permute-start.1 = (bf16[256,256]{1,0:T(8,128)(2,1)}, bf16[256,256]{1,0:T(8,128)(2,1)S(1)}, u32[]{:S(2)}, u32[]{:S(2)}) collective-permute-start(bf16[256,256]{1,0:T(8,128)(2,1)} %get-tuple-element.32), channel_id=1, source_target_pairs={{0,1},{1,0},{2,3},{3,2},{4,5},{5,4},{6,7},{7,6},{8,9},{9,8},{10,11... | collective-permute-start | bytes 393224 | tf_op jit(solution)/shard_map/ppermute | solution.py:203
  18.9 12.5 %collective-permute-done.1 = bf16[256,256]{1,0:T(8,128)(2,1)S(1)} collective-permute-done((bf16[256,256]{1,0:T(8,128)(2,1)}, bf16[256,256]{1,0:T(8,128)(2,1)S(1)}, u32[]{:S(2)}, u32[]{:S(2)}) %collective-permute-start.1) | collective-permute-done | bytes 131104 | tf_op jit(solution)/shard_map/ppermute | solution.py:203
  31.4 2.7 %collective-permute-done.3 = bf16[256,256]{1,0:T(8,128)(2,1)S(1)} collective-permute-done((bf16[256,256]{1,0:T(8,128)(2,1)S(1)}, bf16[256,256]{1,0:T(8,128)(2,1)S(1)}, u32[]{:S(2)}, u32[]{:S(2)}) %collective-permute-start.3) | collective-permute-done | bytes 131104 | tf_op jit(solution)/shard_map/ppermute | solution.py:203
  34.2 1.6 %collective-permute-start.11 = (bf16[1,4,256,256]{3,2,1,0:T(8,128)(2,1)}, bf16[1,4,256,256]{3,2,1,0:T(8,128)(2,1)S(1)}, u32[]{:S(2)}, u32[]{:S(2)}) collective-permute-start(bf16[1,4,256,256]{3,2,1,0:T(8,128)(2,1)} %get-tuple-element.43), channel_id=1, source_target_pairs={{0,16},{8,24},{16,0},{24,8},{1,17},{9,25},{17,1},{25,9},{2,18},{10... | collective-permute-start | bytes 1572872 | tf_op jit(solution)/shard_map/ppermute | solution.py:15
  39.3 6.0 %collective-permute-done.5 = bf16[256,256]{1,0:T(8,128)(2,1)S(1)} collective-permute-done((bf16[256,256]{1,0:T(8,128)(2,1)}, bf16[256,256]{1,0:T(8,128)(2,1)S(1)}, u32[]{:S(2)}, u32[]{:S(2)}) %collective-permute-start.5) | collective-permute-done | bytes 131104 | tf_op jit(solution)/shard_map/ppermute | solution.py:15
  47.6 8.1 %all-to-all-done.piece_ref = bf16[8,2,8,32,256]{4,3,2,1,0:T(8,128)(2,1)S(1)} async-done(((bf16[8,2,8,32,256]{4,3,2,1,0:T(8,128)(2,1)}), bf16[8,2,8,32,256]{4,3,2,1,0:T(8,128)(2,1)S(1)}, u32[]{:S(2)}, u32[]{:S(2)}) %all-to-all-start) | async-done | bytes 2097184 | tf_op jit(solution)/shard_map/all_to_all | solution.py:214
  55.7 4.4 %shard_map.83 = (f32[2,8,256,256]{3,2,1,0:T(8,128)S(1)}, bf16[2,8,256,256]{3,2,1,0:T(8,128)(2,1)S(1)}) custom-call(s32[14]{0:T(128)S(1)} %pad_add_fusion.scalars, bf16[8,2,8,32,256]{4,3,2,1,0:T(8,128)(2,1)S(1)} %all-to-all-done.piece_ref, bf16[8,256,256]{2,1,0:T(8,128)(2,1)} %bitcast.10.refs_0_, bf16[8,256,256]{2,1,0:T(8,128)(2,1)} %bitcast.11.refs_1_), custom_call_target="tpu_custom_call" | custom-call | flops 2147483648 | bytes 10485760 | tf_op jit(solution)/shard_map/pallas_call | solution.py:107
  60.1 3.6 %collective-permute-done.6 = bf16[256,256]{1,0:T(8,128)(2,1)S(1)} collective-permute-done((bf16[256,256]{1,0:T(8,128)(2,1)}, bf16[256,256]{1,0:T(8,128)(2,1)S(1)}, u32[]{:S(2)}, u32[]{:S(2)}) %collective-permute-start.6) | collective-permute-done | bytes 131104 | tf_op jit(solution)/shard_map/ppermute | solution.py:15
  63.7 2.6 %collective-permute-start.10 = (bf16[256,256]{1,0:T(8,128)(2,1)S(1)}, bf16[256,256]{1,0:T(8,128)(2,1)S(1)}, u32[]{:S(2)}, u32[]{:S(2)}) collective-permute-start(bf16[256,256]{1,0:T(8,128)(2,1)S(1)} %multiply_convert_fusion), channel_id=1, source_target_pairs={{0,17},{1,16},{2,19},{3,18},{4,21},{5,20},{6,23},{7,22},{8,25},{9,... | collective-permute-start | bytes 393224 | tf_op jit(solution)/shard_map/ppermute | solution.py:203
  67.3 3.7 %shard_map.84.refs_0_ = f32[2,8,256,256]{3,2,1,0:T(8,128)S(1)} custom-call(s32[14]{0:T(128)S(1)} %pad_add_fusion.scalars, bf16[2,8,256,256]{3,2,1,0:T(8,128)(2,1)S(1)} %get-tuple-element.41.masked_ref.refs_1_, f32[2,8,256,256]{3,2,1,0:T(8,128)S(1)} %get-tuple-element.42.before_ref, bf16[4,256,256]{2,1,0:T(8,128)(2,1)S(1)} %bitcast.27, ...), custom_call_target="tpu_custom_call" | custom-call | flops 2147483648 | bytes 10485760 | tf_op jit(solution)/shard_map/pallas_call | solution.py:107
  71.1 1.8 %collective-permute-done.8 = bf16[256,256]{1,0:T(8,128)(2,1)S(1)} collective-permute-done((bf16[256,256]{1,0:T(8,128)(2,1)S(1)}, bf16[256,256]{1,0:T(8,128)(2,1)S(1)}, u32[]{:S(2)}, u32[]{:S(2)}) %collective-permute-start.8) | collective-permute-done | bytes 131104 | tf_op jit(solution)/shard_map/ppermute | solution.py:203
  73.3 1.9 %collective-permute-done.15.other_ref = bf16[4,256,256]{2,1,0:T(8,128)(2,1)S(1)} collective-permute-done((bf16[4,256,256]{2,1,0:T(8,128)(2,1)S(1)}, bf16[4,256,256]{2,1,0:T(8,128)(2,1)S(1)}, u32[]{:S(2)}, u32[]{:S(2)}) %collective-permute-start.15) | collective-permute-done | bytes 524320 | tf_op jit(solution)/shard_map/ppermute | solution.py:15
  75.2 2.0 %shard_map.85 = (bf16[2,8,32,256]{3,2,1,0:T(8,128)(2,1)S(1)}, bf16[2,8,32,256]{3,2,1,0:T(8,128)(2,1)S(1)}, bf16[2,8,32,256]{3,2,1,0:T(8,128)(2,1)S(1)}, bf16[2,8...) custom-call(s32[14]{0:T(128)S(1)} %pad_add_fusion.scalars, ...), custom_call_target="tpu_custom_call" | custom-call | flops 1073741824 | bytes 8388608 | tf_op jit(solution)/shard_map/pallas_call | solution.py:159
  77.8 2.5 %collective-permute-start.17 = (bf16[2,8,32,256]{3,2,1,0:T(8,128)(2,1)S(1)}, bf16[2,8,32,256]{3,2,1,0:T(8,128)(2,1)S(1)}, u32[]{:S(2)}, u32[]{:S(2)}) collective-permute-start(bf16[2,8,32,256]{3,2,1,0:T(8,128)(2,1)S(1)} %get-tuple-element.51), channel_id=1, source_target_pairs={{0,3},{1,2},{2,1},{3,0},{4,7},{5,6},{6,5},{7,4},{8,11},{9,10},{10,... | collective-permute-start | bytes 786440 | tf_op jit(solution)/shard_map/ppermute | solution.py:15
  80.3 3.1 %collective-permute-start.18 = (bf16[2,8,32,256]{3,2,1,0:T(8,128)(2,1)S(1)}, bf16[2,8,32,256]{3,2,1,0:T(8,128)(2,1)S(1)}, u32[]{:S(2)}, u32[]{:S(2)}) collective-permute-start(bf16[2,8,32,256]{3,2,1,0:T(8,128)(2,1)S(1)} %get-tuple-element.52), channel_id=1, source_target_pairs={{0,7},{1,6},{2,5},{3,4},{4,3},{5,2},{6,1},{7,0},{8,15},{9,14},{10,... | collective-permute-start | bytes 786440 | tf_op jit(solution)/shard_map/ppermute | solution.py:15
  83.4 1.9 %collective-permute-start.20 = (bf16[2,8,32,256]{3,2,1,0:T(8,128)(2,1)S(1)}, bf16[2,8,32,256]{3,2,1,0:T(8,128)(2,1)S(1)}, u32[]{:S(2)}, u32[]{:S(2)}) collective-permute-start(bf16[2,8,32,256]{3,2,1,0:T(8,128)(2,1)S(1)} %get-tuple-element.54), channel_id=1, source_target_pairs={{0,4},{1,5},{2,6},{3,7},{4,0},{5,1},{6,2},{7,3},{8,12},{9,13},{10,... | collective-permute-start | bytes 786440 | tf_op jit(solution)/shard_map/ppermute | solution.py:15
  85.6 6.2 %collective-permute-done.16 = bf16[2,8,32,256]{3,2,1,0:T(8,128)(2,1)S(1)} collective-permute-done((bf16[2,8,32,256]{3,2,1,0:T(8,128)(2,1)S(1)}, bf16[2,8,32,256]{3,2,1,0:T(8,128)(2,1)S(1)}, u32[]{:S(2)}, u32[]{:S(2)}) %collective-permute-start.16) | collective-permute-done | bytes 262176 | tf_op jit(solution)/shard_map/ppermute | solution.py:15
  92.7 6.4 %collective-permute-done.17 = bf16[2,8,32,256]{3,2,1,0:T(8,128)(2,1)S(1)} collective-permute-done((bf16[2,8,32,256]{3,2,1,0:T(8,128)(2,1)S(1)}, bf16[2,8,32,256]{3,2,1,0:T(8,128)(2,1)S(1)}, u32[]{:S(2)}, u32[]{:S(2)}) %collective-permute-start.17) | collective-permute-done | bytes 262176 | tf_op jit(solution)/shard_map/ppermute | solution.py:15
  99.1 1.8 %collective-permute-start.22 = (bf16[2,8,32,256]{3,2,1,0:T(8,128)(2,1)S(1)}, bf16[2,8,32,256]{3,2,1,0:T(8,128)(2,1)S(1)}, u32[]{:S(2)}, u32[]{:S(2)}) collective-permute-start(bf16[2,8,32,256]{3,2,1,0:T(8,128)(2,1)S(1)} %get-tuple-element.56), channel_id=1, source_target_pairs={{0,6},{1,7},{2,4},{3,5},{4,2},{5,3},{6,0},{7,1},{8,14},{9,15},{10,... | collective-permute-start | bytes 786440 | tf_op jit(solution)/shard_map/ppermute | solution.py:15
  101.0 3.6 %collective-permute-done.19 = bf16[2,8,32,256]{3,2,1,0:T(8,128)(2,1)S(1)} collective-permute-done((bf16[2,8,32,256]{3,2,1,0:T(8,128)(2,1)S(1)}, bf16[2,8,32,256]{3,2,1,0:T(8,128)(2,1)S(1)}, u32[]{:S(2)}, u32[]{:S(2)}) %collective-permute-start.19) | collective-permute-done | bytes 262176 | tf_op jit(solution)/shard_map/ppermute | solution.py:15
  104.6 14.8 %collective-permute-done.20 = bf16[2,8,32,256]{3,2,1,0:T(8,128)(2,1)S(1)} collective-permute-done((bf16[2,8,32,256]{3,2,1,0:T(8,128)(2,1)S(1)}, bf16[2,8,32,256]{3,2,1,0:T(8,128)(2,1)S(1)}, u32[]{:S(2)}, u32[]{:S(2)}) %collective-permute-start.20) | collective-permute-done | bytes 262176 | tf_op jit(solution)/shard_map/ppermute | solution.py:15
  (70 shorter events, 16.4 us)
Async XLA Ops:
  0.0 55.7 %all-to-all-start = ((bf16[8,2,8,32,256]{4,3,2,1,0:T(8,128)(2,1)}), bf16[8,2,8,32,256]{4,3,2,1,0:T(8,128)(2,1)S(1)}, u32[]{:S(2)}, u32[]{:S(2)}) async-start(bf16[8,2,8,32,256]{4,3,2,1,0:T(8,128)(2,1)} %bitcast.29), calls=%async_computation | async-start | bytes 4194304 | tf_op jit(solution)/shard_map/all_to_all | solution.py:214
  8.6 4.4 %collective-permute-start = (bf16[4,2,128,256]{3,2,1,0:T(8,128)(2,1)}, bf16[4,2,128,256]{3,2,1,0:T(8,128)(2,1)}, u32[]{:S(2)}, u32[]{:S(2)}) collective-permute-start(bf16[4,2,128,256]{3,2,1,0:T(8,128)(2,1)} %get-tuple-element.59), channel_id=1, source_target_pairs={{0,8},{8,0},{16,24},{24,16},{1,9},{9,1},{17,25},{25,17},{2,10},{10... | collective-permute-start | bytes 1572872 | tf_op jit(solution)/shard_map/ppermute | solution.py:15
  8.6 47.1 %collective-permute-start.7 = (bf16[1,8,256,256]{3,2,1,0:T(8,128)(2,1)}, bf16[1,8,256,256]{3,2,1,0:T(8,128)(2,1)}, u32[]{:S(2)}, u32[]{:S(2)}) collective-permute-start(bf16[1,8,256,256]{3,2,1,0:T(8,128)(2,1)} %param.9), channel_id=1, source_target_pairs={{0,8},{8,0},{16,24},{24,16},{1,9},{9,1},{17,25},{25,17},{2,10},{10... | collective-permute-start | bytes 3145736 | tf_op jit(solution)/shard_map/ppermute | solution.py:15
  11.3 22.9 %collective-permute-start.4 = (bf16[1,4,256,256]{3,2,1,0:T(8,128)(2,1)}, bf16[1,4,256,256]{3,2,1,0:T(8,128)(2,1)S(1)}, u32[]{:S(2)}, u32[]{:S(2)}) collective-permute-start(bf16[1,4,256,256]{3,2,1,0:T(8,128)(2,1)} %get-tuple-element.58), channel_id=1, source_target_pairs={{0,16},{8,24},{16,0},{24,8},{1,17},{9,25},{17,1},{25,9},{2,18},{10... | collective-permute-start | bytes 1572872 | tf_op jit(solution)/shard_map/ppermute | solution.py:15
  15.0 16.4 %collective-permute-start.1 = (bf16[256,256]{1,0:T(8,128)(2,1)}, bf16[256,256]{1,0:T(8,128)(2,1)S(1)}, u32[]{:S(2)}, u32[]{:S(2)}) collective-permute-start(bf16[256,256]{1,0:T(8,128)(2,1)} %get-tuple-element.32), channel_id=1, source_target_pairs={{0,1},{1,0},{2,3},{3,2},{4,5},{5,4},{6,7},{7,6},{8,9},{9,8},{10,11... | collective-permute-start | bytes 393224 | tf_op jit(solution)/shard_map/ppermute | solution.py:203
  17.0 14.4 %collective-permute-start.2 = (bf16[256,256]{1,0:T(8,128)(2,1)S(1)}, bf16[256,256]{1,0:T(8,128)(2,1)S(1)}, u32[]{:S(2)}, u32[]{:S(2)}) collective-permute-start(bf16[256,256]{1,0:T(8,128)(2,1)S(1)} %get-tuple-element.33), channel_id=1, source_target_pairs={{0,16},{1,17},{2,18},{3,19},{4,20},{5,21},{6,22},{7,23},{8,24},{9,... | collective-permute-start | bytes 393224 | tf_op jit(solution)/shard_map/ppermute | solution.py:203
  17.6 16.6 %collective-permute-start.3 = (bf16[256,256]{1,0:T(8,128)(2,1)S(1)}, bf16[256,256]{1,0:T(8,128)(2,1)S(1)}, u32[]{:S(2)}, u32[]{:S(2)}) collective-permute-start(bf16[256,256]{1,0:T(8,128)(2,1)S(1)} %get-tuple-element.34), channel_id=1, source_target_pairs={{0,17},{1,16},{2,19},{3,18},{4,21},{5,20},{6,23},{7,22},{8,25},{9,... | collective-permute-start | bytes 393224 | tf_op jit(solution)/shard_map/ppermute | solution.py:203
  34.2 12.0 %collective-permute-start.11 = (bf16[1,4,256,256]{3,2,1,0:T(8,128)(2,1)}, bf16[1,4,256,256]{3,2,1,0:T(8,128)(2,1)S(1)}, u32[]{:S(2)}, u32[]{:S(2)}) collective-permute-start(bf16[1,4,256,256]{3,2,1,0:T(8,128)(2,1)} %get-tuple-element.43), channel_id=1, source_target_pairs={{0,16},{8,24},{16,0},{24,8},{1,17},{9,25},{17,1},{25,9},{2,18},{10... | collective-permute-start | bytes 1572872 | tf_op jit(solution)/shard_map/ppermute | solution.py:15
  36.5 8.8 %collective-permute-start.5 = (bf16[256,256]{1,0:T(8,128)(2,1)}, bf16[256,256]{1,0:T(8,128)(2,1)S(1)}, u32[]{:S(2)}, u32[]{:S(2)}) collective-permute-start(bf16[256,256]{1,0:T(8,128)(2,1)} %convert_element_type.31), channel_id=1, source_target_pairs={{0,2},{1,3},{2,0},{3,1},{4,6},{5,7},{6,4},{7,5},{8,10},{9,11},{10,... | collective-permute-start | bytes 393224 | tf_op jit(solution)/shard_map/ppermute | solution.py:15
  39.3 27.5 %collective-permute-start.12 = (bf16[1,4,256,256]{3,2,1,0:T(8,128)(2,1)S(1)}, bf16[1,4,256,256]{3,2,1,0:T(8,128)(2,1)}, u32[]{:S(2)}, u32[]{:S(2)}) collective-permute-start(bf16[1,4,256,256]{3,2,1,0:T(8,128)(2,1)S(1)} %collective-permute-done.4), channel_id=1, source_target_pairs={{0,8},{8,0},{16,24},{24,16},{1,9},{9,1},{17,25},{25,17},{2,10},{10... | collective-permute-start | bytes 1572872 | tf_op jit(solution)/shard_map/ppermute | solution.py:15
  47.1 20.2 %collective-permute-start.13 = (bf16[1,2,256,256]{3,2,1,0:T(8,128)(2,1)}, bf16[1,2,256,256]{3,2,1,0:T(8,128)(2,1)S(1)}, u32[]{:S(2)}, u32[]{:S(2)}) collective-permute-start(bf16[1,2,256,256]{3,2,1,0:T(8,128)(2,1)} %get-tuple-element.62), channel_id=1, source_target_pairs={{0,8},{8,0},{16,24},{24,16},{1,9},{9,1},{17,25},{25,17},{2,10},{10... | collective-permute-start | bytes 786440 | tf_op jit(solution)/shard_map/ppermute | solution.py:15
  47.1 20.2 %collective-permute-start.14 = (bf16[1,2,256,256]{3,2,1,0:T(8,128)(2,1)}, bf16[1,2,256,256]{3,2,1,0:T(8,128)(2,1)}, u32[]{:S(2)}, u32[]{:S(2)}) collective-permute-start(bf16[1,2,256,256]{3,2,1,0:T(8,128)(2,1)} %get-tuple-element.61), channel_id=1, source_target_pairs={{0,8},{8,0},{16,24},{24,16},{1,9},{9,1},{17,25},{25,17},{2,10},{10... | collective-permute-start | bytes 786440 | tf_op jit(solution)/shard_map/ppermute | solution.py:15
  55.7 8.0 %collective-permute-start.6 = (bf16[256,256]{1,0:T(8,128)(2,1)}, bf16[256,256]{1,0:T(8,128)(2,1)S(1)}, u32[]{:S(2)}, u32[]{:S(2)}) collective-permute-start(bf16[256,256]{1,0:T(8,128)(2,1)} %fusion.4), channel_id=1, source_target_pairs={{0,4},{1,5},{2,6},{3,7},{4,0},{5,1},{6,2},{7,3},{8,12},{9,13},{10,... | collective-permute-start | bytes 393224 | tf_op jit(solution)/shard_map/ppermute | solution.py:15
  63.7 7.3 %collective-permute-start.10 = (bf16[256,256]{1,0:T(8,128)(2,1)S(1)}, bf16[256,256]{1,0:T(8,128)(2,1)S(1)}, u32[]{:S(2)}, u32[]{:S(2)}) collective-permute-start(bf16[256,256]{1,0:T(8,128)(2,1)S(1)} %multiply_convert_fusion), channel_id=1, source_target_pairs={{0,17},{1,16},{2,19},{3,18},{4,21},{5,20},{6,23},{7,22},{8,25},{9,... | collective-permute-start | bytes 393224 | tf_op jit(solution)/shard_map/ppermute | solution.py:203
  66.3 6.5 %collective-permute-start.8 = (bf16[256,256]{1,0:T(8,128)(2,1)S(1)}, bf16[256,256]{1,0:T(8,128)(2,1)S(1)}, u32[]{:S(2)}, u32[]{:S(2)}) collective-permute-start(bf16[256,256]{1,0:T(8,128)(2,1)S(1)} %multiply_convert_fusion), channel_id=1, source_target_pairs={{0,1},{1,0},{2,3},{3,2},{4,5},{5,4},{6,7},{7,6},{8,9},{9,8},{10,11... | collective-permute-start | bytes 393224 | tf_op jit(solution)/shard_map/ppermute | solution.py:203
  66.8 6.4 %collective-permute-start.9 = (bf16[256,256]{1,0:T(8,128)(2,1)S(1)}, bf16[256,256]{1,0:T(8,128)(2,1)S(1)}, u32[]{:S(2)}, u32[]{:S(2)}) collective-permute-start(bf16[256,256]{1,0:T(8,128)(2,1)S(1)} %multiply_convert_fusion), channel_id=1, source_target_pairs={{0,16},{1,17},{2,18},{3,19},{4,20},{5,21},{6,22},{7,23},{8,24},{9,... | collective-permute-start | bytes 393224 | tf_op jit(solution)/shard_map/ppermute | solution.py:203
  73.2 2.0 %collective-permute-start.15 = (bf16[4,256,256]{2,1,0:T(8,128)(2,1)S(1)}, bf16[4,256,256]{2,1,0:T(8,128)(2,1)S(1)}, u32[]{:S(2)}, u32[]{:S(2)}) collective-permute-start(bf16[4,256,256]{2,1,0:T(8,128)(2,1)S(1)} %pad_maximum_fusion.same_ref), channel_id=1, source_target_pairs={{0,8},{8,0},{16,24},{24,16},{1,9},{9,1},{17,25},{25,17},{2,10},{10... | collective-permute-start | bytes 1572872 | tf_op jit(solution)/shard_map/ppermute | solution.py:15
  77.2 14.6 %collective-permute-start.16 = (bf16[2,8,32,256]{3,2,1,0:T(8,128)(2,1)S(1)}, bf16[2,8,32,256]{3,2,1,0:T(8,128)(2,1)S(1)}, u32[]{:S(2)}, u32[]{:S(2)}) collective-permute-start(bf16[2,8,32,256]{3,2,1,0:T(8,128)(2,1)S(1)} %get-tuple-element.50), channel_id=1, source_target_pairs={{0,5},{1,4},{2,7},{3,6},{4,1},{5,0},{6,3},{7,2},{8,13},{9,12},{10,... | collective-permute-start | bytes 786440 | tf_op jit(solution)/shard_map/ppermute | solution.py:15
  77.8 21.3 %collective-permute-start.17 = (bf16[2,8,32,256]{3,2,1,0:T(8,128)(2,1)S(1)}, bf16[2,8,32,256]{3,2,1,0:T(8,128)(2,1)S(1)}, u32[]{:S(2)}, u32[]{:S(2)}) collective-permute-start(bf16[2,8,32,256]{3,2,1,0:T(8,128)(2,1)S(1)} %get-tuple-element.51), channel_id=1, source_target_pairs={{0,3},{1,2},{2,1},{3,0},{4,7},{5,6},{6,5},{7,4},{8,11},{9,10},{10,... | collective-permute-start | bytes 786440 | tf_op jit(solution)/shard_map/ppermute | solution.py:15
  80.3 20.6 %collective-permute-start.18 = (bf16[2,8,32,256]{3,2,1,0:T(8,128)(2,1)S(1)}, bf16[2,8,32,256]{3,2,1,0:T(8,128)(2,1)S(1)}, u32[]{:S(2)}, u32[]{:S(2)}) collective-permute-start(bf16[2,8,32,256]{3,2,1,0:T(8,128)(2,1)S(1)} %get-tuple-element.52), channel_id=1, source_target_pairs={{0,7},{1,6},{2,5},{3,4},{4,3},{5,2},{6,1},{7,0},{8,15},{9,14},{10,... | collective-permute-start | bytes 786440 | tf_op jit(solution)/shard_map/ppermute | solution.py:15
  83.4 21.1 %collective-permute-start.19 = (bf16[2,8,32,256]{3,2,1,0:T(8,128)(2,1)S(1)}, bf16[2,8,32,256]{3,2,1,0:T(8,128)(2,1)S(1)}, u32[]{:S(2)}, u32[]{:S(2)}) collective-permute-start(bf16[2,8,32,256]{3,2,1,0:T(8,128)(2,1)S(1)} %get-tuple-element.53), channel_id=1, source_target_pairs={{0,2},{1,3},{2,0},{3,1},{4,6},{5,7},{6,4},{7,5},{8,10},{9,11},{10,... | collective-permute-start | bytes 786440 | tf_op jit(solution)/shard_map/ppermute | solution.py:15
  83.4 35.9 %collective-permute-start.20 = (bf16[2,8,32,256]{3,2,1,0:T(8,128)(2,1)S(1)}, bf16[2,8,32,256]{3,2,1,0:T(8,128)(2,1)S(1)}, u32[]{:S(2)}, u32[]{:S(2)}) collective-permute-start(bf16[2,8,32,256]{3,2,1,0:T(8,128)(2,1)S(1)} %get-tuple-element.54), channel_id=1, source_target_pairs={{0,4},{1,5},{2,6},{3,7},{4,0},{5,1},{6,2},{7,3},{8,12},{9,13},{10,... | collective-permute-start | bytes 786440 | tf_op jit(solution)/shard_map/ppermute | solution.py:15
  91.8 27.6 %collective-permute-start.21 = (bf16[2,8,32,256]{3,2,1,0:T(8,128)(2,1)S(1)}, bf16[2,8,32,256]{3,2,1,0:T(8,128)(2,1)S(1)}, u32[]{:S(2)}, u32[]{:S(2)}) collective-permute-start(bf16[2,8,32,256]{3,2,1,0:T(8,128)(2,1)S(1)} %get-tuple-element.55), channel_id=1, source_target_pairs={{0,1},{1,0},{2,3},{3,2},{4,5},{5,4},{6,7},{7,6},{8,9},{9,8},{10,11... | collective-permute-start | bytes 786440 | tf_op jit(solution)/shard_map/ppermute | solution.py:15
  99.1 20.3 %collective-permute-start.22 = (bf16[2,8,32,256]{3,2,1,0:T(8,128)(2,1)S(1)}, bf16[2,8,32,256]{3,2,1,0:T(8,128)(2,1)S(1)}, u32[]{:S(2)}, u32[]{:S(2)}) collective-permute-start(bf16[2,8,32,256]{3,2,1,0:T(8,128)(2,1)S(1)} %get-tuple-element.56), channel_id=1, source_target_pairs={{0,6},{1,7},{2,4},{3,5},{4,2},{5,3},{6,0},{7,1},{8,14},{9,15},{10,... | collective-permute-start | bytes 786440 | tf_op jit(solution)/shard_map/ppermute | solution.py:15
  (8 other events, 88.7 us)
